TPU v7x, 32 devices: a whole 2x2x4 slice. The times are simulated.
32 devices in a mesh: dp: 8 (over z, y), expert: 2 (over core), shard: 2 (over x).
Axes of the slice: x: 2, y: 2, z: 4, core: 2. Of those that a mesh axis runs over, the one named last changes fastest.
Arguments:
- tokens: bfloat16 [2, 1024, 2048], P('expert', 'dp'), may hold values from -6 to 6
- cotangent: bfloat16 [2, 1024, 2048], P('expert', 'dp'), may hold values from -6 to 6
- attn_gain: float32 [2048], replicated, may hold values from 0.5 to 1.5
- mlp_gain: float32 [2048], replicated, may hold values from 0.5 to 1.5
- key_weight: bfloat16 [2048, 2048], P(None, 'shard'), may hold values from -0.125 to 0.125
- value_weight: bfloat16 [2048, 2048], P(None, 'shard'), may hold values from -0.125 to 0.125
- query_weight: bfloat16 [2048, 16384], P(None, ('dp', 'expert', 'shard')), may hold values from -0.125 to 0.125
- output_weight: bfloat16 [2048, 16384], P(None, ('dp', 'expert', 'shard')), may hold values from -1.5 to 1.5
- attn_router: bfloat16 [2048, 8], replicated, may hold values from -0.09375 to 0.09375
- gate_weight: bfloat16 [2048, 45056], P(None, ('dp', 'expert', 'shard')), may hold values from -0.125 to 0.125
- up_weight: bfloat16 [2048, 45056], P(None, ('dp', 'expert', 'shard')), may hold values from -0.125 to 0.125
- down_weight: bfloat16 [2048, 45056], P(None, ('dp', 'expert', 'shard')), may hold values from -0.15625 to 0.15625
- mlp_router: bfloat16 [2048, 8], replicated, may hold values from -0.09375 to 0.09375
- segment_ids: int32 [2, 1024], P('expert'), may hold values from 0 to 12, as said below
- parent_ids: int32 [2, 13], P('expert'), may hold values from 0 to 11, as said below
- attn_routes: int32 [2, 1024, 2], P('expert', 'dp'), may hold values from 0 to 7, all different within a row; in each aligned block of 128 rows (0 to 127, 128 to 255, ..., all dimensions but the last counted through in order) at most 40 rows name the same one
- mlp_routes: int32 [2, 1024, 2], P('expert', 'dp'), may hold values from 0 to 7, all different within a row
- slot_order: int32 [2, 8, 256], P('expert', 'dp'), may hold values from 0 to 255, each once within a row
Outputs:
- layer_out: bfloat16 [2, 1024, 2048], P('expert', 'dp')
- tokens_grad: float32 [2, 1024, 2048], P('expert', 'dp')
- attn_gain_grad: float32 [2048], P(('dp', 'expert'))
- mlp_gain_grad: float32 [2048], P(('dp', 'expert'))
- key_grad: float32 [2048, 2048], P(('dp', 'expert'), 'shard')
- value_grad: float32 [2048, 2048], P(('dp', 'expert'), 'shard')
- query_grad: float32 [2048, 16384], P(None, ('dp', 'expert', 'shard'))
- output_grad: float32 [2048, 16384], P(None, ('dp', 'expert', 'shard'))
- attn_router_grad: float32 [2048, 8], P(('dp', 'expert'))
- gate_grad: float32 [2048, 45056], P(None, ('dp', 'expert', 'shard'))
- up_grad: float32 [2048, 45056], P(None, ('dp', 'expert', 'shard'))
- down_grad: float32 [2048, 45056], P(None, ('dp', 'expert', 'shard'))
- mlp_router_grad: float32 [2048, 8], P(('dp', 'expert'))
Inputs may be any that keep to these rules, and one draw needn't show every extreme that they name: `segment_ids`: along a tree the segment number never falls, segment 0 comes first, and every segment holds at least one token. parent_ids[t, 0] = 0; for s >= 1, parent_ids[t, s] is 0 or a segment r with 1 <= r < s and parent_ids[t, r] = 0. `attn_routes`: A token's 2 attention experts differ. In each block of 128 tokens of a tree no attention expert is named by more than 40 pairs, and in every draw some expert is named by exactly 40 pairs in some block. `mlp_routes`: A token's 2 feed-forward experts differ. `slot_order`: each row holds every pair number of the block once.
All inputs are finite; a program needn't handle non-finite values.
Results may differ from a plain program's by a relative error of at most 0.019.
Values may be sent and summed in bfloat16 or wider, within the bound.
No kernel may reach another device: no remote copies, remote signals or barrier semaphores. Data moves between devices by JAX's collectives and lax.ppermute only.
A program may use at most 384 MiB of HBM per device.

v0:
```python
import jax
import jax.numpy as jnp
from jax import lax
from jax.sharding import PartitionSpec as P

HEAD = 128


epsilon = 1e-06
negative = -1e30


def product(former, latter):
    return jnp.dot(former, latter, preferred_element_type=jnp.float32)


def product_last(former, latter):
    return lax.dot_general(
        former, latter, (((1,), (1,)), ((), ())), preferred_element_type=jnp.float32
    )


def product_first(former, latter):
    return lax.dot_general(
        former, latter, (((0,), (0,)), ((), ())), preferred_element_type=jnp.float32
    )


def inverse_rms(values):
    return lax.rsqrt(jnp.mean(values * values, axis=1, keepdims=True) + epsilon)


def norm_backward(values, scales, gains, upstream):
    normed = values * scales
    weighted = upstream * gains
    gain_grad = jnp.sum(upstream * normed, axis=0)
    value_grad = scales * (weighted - normed * jnp.mean(weighted * normed, axis=1, keepdims=True))
    return (value_grad, gain_grad)


def pair_targets(routes, ranking, experts, capacity):
    flat_routes = routes.reshape(-1)
    same_expert = flat_routes[:, None] == flat_routes[None, :]
    earlier = ranking[None, :] < ranking[:, None]
    slots = jnp.sum(jnp.logical_and(same_expert, earlier).astype(jnp.int32), axis=1)
    kept = slots < capacity
    targets = jnp.where(kept, flat_routes * capacity + slots, experts * capacity)
    return (targets, kept)


def pack_rows(rows, targets, experts, capacity):
    holder = jnp.zeros((experts * capacity, rows.shape[1]), rows.dtype)
    return holder.at[targets].set(rows, mode="drop").reshape(experts, capacity, rows.shape[1])


def unpack_rows(arrived, targets):
    flat_rows = arrived.reshape(-1, arrived.shape[2])
    return jnp.take(flat_rows, targets, axis=0, mode="fill", fill_value=0)


def fan_out(buffer, members):
    experts, capacity, columns = buffer.shape
    spread = jnp.broadcast_to(buffer[:, None], (experts, members, capacity, columns))
    return spread.reshape(experts * members, capacity, columns)


def spread_pieces(pieces, targets, experts, capacity, members):
    columns = pieces.shape[2]
    packed = pack_rows(
        pieces.reshape(pieces.shape[0], members * columns), targets, experts, capacity
    )
    ordered = packed.reshape(experts, capacity, members, columns).transpose(0, 2, 1, 3)
    return ordered.reshape(experts * members, capacity, columns)


def collect_pieces(arrived, targets, experts, members):
    capacity, columns = (arrived.shape[1], arrived.shape[2])
    ordered = arrived.reshape(experts, members, capacity, columns).transpose(0, 2, 1, 3)
    return unpack_rows(ordered.reshape(experts, capacity, members * columns), targets).reshape(
        -1, members, columns
    )


def collect_sums(arrived, targets, experts, members):
    capacity, columns = (arrived.shape[1], arrived.shape[2])
    summed = jnp.sum(arrived.reshape(experts, members, capacity, columns), axis=1)
    return unpack_rows(summed, targets)


def heads_to_members(values, members, shards):
    pairs = values.shape[0]
    columns = values.shape[1] // members
    split = values.reshape(pairs, members // shards, shards, columns)
    moved = lax.all_to_all(split, "shard", split_axis=2, concat_axis=1, tiled=True)
    return moved.reshape(pairs, members, columns)


def heads_to_tokens(pieces):
    pairs, members, columns = pieces.shape
    moved = lax.all_to_all(
        pieces.reshape(pairs, members, 1, columns), "shard", split_axis=1, concat_axis=2, tiled=True
    )
    return moved.reshape(pairs, members * columns)


def pair_gates(logits, routes):
    onehot = routes[:, :, None] == jnp.arange(logits.shape[1])[None, None, :]
    chosen = jnp.sum(jnp.where(onehot, logits[:, None, :], 0.0), axis=2)
    return (jax.nn.softmax(chosen, axis=1), onehot)


def logit_grad(gates, upstream, onehot):
    centred = upstream - jnp.sum(gates * upstream, axis=1, keepdims=True)
    spread = jnp.where(onehot, (gates * centred)[:, :, None], 0.0)
    return jnp.sum(spread, axis=1).astype(jnp.bfloat16)


def split_heads(matrix):
    return matrix.reshape(matrix.shape[0], -1, HEAD).transpose(1, 0, 2)


def join_heads(stacked):
    return stacked.transpose(1, 0, 2).reshape(stacked.shape[1], -1)


def head_forward(query, keys, values, visible):
    scores = jnp.where(visible, product_last(query, keys) * HEAD ** (-0.5), negative)
    highest = jnp.max(scores, axis=1, keepdims=True)
    expo = jnp.exp(scores - highest)
    summed = jnp.sum(expo, axis=1, keepdims=True)
    probs = (expo / summed).astype(jnp.bfloat16)
    mixed = product(probs, values).astype(jnp.bfloat16)
    return (mixed, highest + jnp.log(summed))


def head_backward(query, keys, values, log_total, mixed_grad, visible):
    scores = jnp.where(visible, product_last(query, keys) * HEAD ** (-0.5), negative)
    probs = jnp.exp(scores - log_total)
    prob_grad = product_last(mixed_grad, values)
    inner = jnp.sum(probs * prob_grad, axis=1, keepdims=True)
    score_grad = (probs * (prob_grad - inner) * HEAD ** (-0.5)).astype(jnp.bfloat16)
    query_grad = product(score_grad, keys).astype(jnp.bfloat16)
    key_grad = product_first(score_grad, query)
    value_grad = product_first(probs.astype(jnp.bfloat16), mixed_grad)
    return (query_grad, key_grad, value_grad)


def send_rows(buffers):
    return lax.all_to_all(buffers, ("dp", "expert"), split_axis=0, concat_axis=0, tiled=True)


def send_both(grad_buffer, row_buffer):
    return (
        lax.all_to_all(grad_buffer, ("dp", "expert"), split_axis=0, concat_axis=0, tiled=True),
        lax.all_to_all(row_buffer, ("dp", "expert"), split_axis=0, concat_axis=0, tiled=True),
    )


def return_rows(buffers):
    return lax.all_to_all(buffers, ("dp", "expert"), split_axis=0, concat_axis=0, tiled=True)


def return_sums(buffers):
    return lax.all_to_all(buffers, ("dp", "expert"), split_axis=0, concat_axis=0, tiled=True)


def shard_total(values):
    return lax.psum(values, "shard")


def shard_pair(values, gate_terms):
    return (
        lax.psum(values.astype(jnp.bfloat16), "shard").astype(jnp.float32),
        lax.psum(gate_terms.astype(jnp.bfloat16), "shard").astype(jnp.float32),
    )


def per_device(
    tokens,
    cotangent,
    attn_gain,
    mlp_gain,
    key_weight,
    value_weight,
    query_weight,
    output_weight,
    attn_router,
    gate_weight,
    up_weight,
    down_weight,
    mlp_router,
    segment_ids,
    parent_ids,
    attn_routes,
    mlp_routes,
    slot_order,
):
    inputs = tokens[0].astype(jnp.float32)
    tok_rows = inputs.shape[0]
    width = inputs.shape[1]
    piece_cols = query_weight.shape[1]
    top_count = attn_routes.shape[2]
    experts = attn_router.shape[1]
    groups = lax.axis_size("dp") * lax.axis_size("expert")
    members = groups // experts
    shards = lax.axis_size("shard")
    capacity = min(tok_rows, 5 * tok_rows * top_count // (4 * experts))
    ranking = slot_order[0, 0]
    attn_targets = pair_targets(attn_routes[0], ranking, experts, capacity)[0]
    mlp_targets, mlp_kept = pair_targets(mlp_routes[0], ranking, experts, capacity)
    mlp_kept = mlp_kept.reshape(tok_rows, top_count)
    tree_segments = segment_ids[0]
    parents = parent_ids[0]
    tree_len = tree_segments.shape[0]
    begin = lax.axis_index("dp") * tok_rows
    own_segments = lax.dynamic_slice_in_dim(tree_segments, begin, tok_rows)
    segment_range = jnp.arange(parents.shape[0])
    parent_one = jnp.sum(
        jnp.where(own_segments[:, None] == segment_range[None, :], parents[None, :], 0), axis=1
    )
    parent_two = jnp.sum(
        jnp.where(parent_one[:, None] == segment_range[None, :], parents[None, :], 0), axis=1
    )
    positions = begin + jnp.arange(tok_rows)
    key_places = jnp.arange(tree_len)
    ancestor = (
        (tree_segments[None, :] == own_segments[:, None])
        | (tree_segments[None, :] == parent_one[:, None])
        | (tree_segments[None, :] == parent_two[:, None])
    )
    visible = jnp.repeat(
        jnp.logical_and(key_places[None, :] <= positions[:, None], ancestor), top_count, axis=0
    )
    attn_scale = inverse_rms(inputs)
    normed = (inputs * attn_scale * attn_gain).astype(jnp.bfloat16)
    local_keys = product(normed, key_weight).astype(jnp.bfloat16)
    local_values = product(normed, value_weight).astype(jnp.bfloat16)
    tree_keys, tree_values = (
        lax.all_gather(local_keys, "dp", axis=0, tiled=True),
        lax.all_gather(local_values, "dp", axis=0, tiled=True),
    )
    attn_gates, attn_onehot = pair_gates(product(normed, attn_router), attn_routes[0])
    pair_normed = jnp.repeat(normed, top_count, axis=0)
    normed_out = fan_out(pack_rows(pair_normed, attn_targets, experts, capacity), members)
    owner_normed = send_rows(normed_out).reshape(-1, width)
    owner_queries = product(owner_normed, query_weight).astype(jnp.bfloat16)
    query_pieces = collect_pieces(
        return_rows(owner_queries.reshape(groups, capacity, piece_cols)),
        attn_targets,
        experts,
        members,
    )
    queries = heads_to_tokens(query_pieces)
    head_queries = split_heads(queries)
    head_keys = split_heads(tree_keys)
    head_values = split_heads(tree_values)

    def forward_head(parts):
        return head_forward(parts[0], parts[1], parts[2], visible)

    mixed, log_total = lax.map(forward_head, (head_queries, head_keys, head_values))
    attended = join_heads(mixed)
    attended_out = spread_pieces(
        heads_to_members(attended, members, shards), attn_targets, experts, capacity, members
    )
    owner_attended = send_rows(attended_out).reshape(-1, piece_cols)
    owner_attn = product_last(owner_attended, output_weight)
    attn_pairs = collect_sums(
        return_sums(owner_attn.reshape(groups, capacity, width)), attn_targets, experts, members
    ).reshape(tok_rows, top_count, width)
    attn_mix = shard_total(jnp.sum(attn_gates[:, :, None] * attn_pairs, axis=1))
    middle = inputs + attn_mix
    mlp_scale = inverse_rms(middle)
    mlp_normed = (middle * mlp_scale * mlp_gain).astype(jnp.bfloat16)
    mlp_gates, mlp_onehot = pair_gates(product(mlp_normed, mlp_router), mlp_routes[0])
    pair_mlp_rows = jnp.repeat(mlp_normed, top_count, axis=0)
    mlp_out = fan_out(pack_rows(pair_mlp_rows, mlp_targets, experts, capacity), members)
    owner_mlp_rows = send_rows(mlp_out).reshape(-1, width)
    gate_pre = product(owner_mlp_rows, gate_weight)
    up_pre = product(owner_mlp_rows, up_weight)
    hidden = (jax.nn.silu(gate_pre) * up_pre).astype(jnp.bfloat16)
    owner_mlp = product_last(hidden, down_weight)
    mlp_pairs = collect_sums(
        return_sums(owner_mlp.reshape(groups, capacity, width)), mlp_targets, experts, members
    ).reshape(tok_rows, top_count, width)
    mlp_weights = jnp.where(mlp_kept, mlp_gates, 0.0)
    mlp_mix = shard_total(jnp.sum(mlp_weights[:, :, None] * mlp_pairs, axis=1))
    layer_out = (middle + mlp_mix).astype(jnp.bfloat16)[None]
    out_grad = cotangent[0].astype(jnp.float32)
    mlp_pair_grad = (
        (mlp_weights[:, :, None] * out_grad[:, None, :])
        .astype(jnp.bfloat16)
        .reshape(tok_rows * top_count, width)
    )
    mlp_grad_buffer = fan_out(pack_rows(mlp_pair_grad, mlp_targets, experts, capacity), members)
    arrived_grad, arrived_rows = send_both(mlp_grad_buffer, mlp_out)
    owner_rows = arrived_rows.reshape(-1, width)
    owner_grad = arrived_grad.reshape(-1, width)
    gate_again = product(owner_rows, gate_weight)
    up_again = product(owner_rows, up_weight)
    gate_sigmoid = jax.nn.sigmoid(gate_again)
    silu_values = gate_again * gate_sigmoid
    hidden_again = (silu_values * up_again).astype(jnp.bfloat16)
    hidden_grad = product(owner_grad, down_weight)
    down_grad = product_first(owner_grad, hidden_again)
    gate_pre_grad = (
        hidden_grad * up_again * gate_sigmoid * (1.0 + gate_again * (1.0 - gate_sigmoid))
    ).astype(jnp.bfloat16)
    up_pre_grad = (hidden_grad * silu_values).astype(jnp.bfloat16)
    gate_grad = product_first(owner_rows, gate_pre_grad)
    up_grad = product_first(owner_rows, up_pre_grad)
    owner_row_grad = product_last(gate_pre_grad, gate_weight) + product_last(up_pre_grad, up_weight)
    mlp_back = collect_sums(
        return_sums(owner_row_grad.reshape(groups, capacity, width)), mlp_targets, experts, members
    ).reshape(tok_rows, top_count, width)
    mlp_gate_part = jnp.sum(out_grad[:, None, :] * mlp_pairs, axis=2)
    mlp_norm_grad, mlp_gate_grad = shard_pair(jnp.sum(mlp_back, axis=1), mlp_gate_part)
    mlp_logit_grad = logit_grad(mlp_gates, mlp_gate_grad, mlp_onehot)
    mlp_norm_grad = mlp_norm_grad + product_last(mlp_logit_grad, mlp_router)
    mlp_router_grad = product_first(mlp_normed, mlp_logit_grad)
    middle_part, mlp_gain_grad = norm_backward(middle, mlp_scale, mlp_gain, mlp_norm_grad)
    middle_grad = out_grad + middle_part
    attn_pair_grad = (
        (attn_gates[:, :, None] * middle_grad[:, None, :])
        .astype(jnp.bfloat16)
        .reshape(tok_rows * top_count, width)
    )
    attn_grad_buffer = fan_out(pack_rows(attn_pair_grad, attn_targets, experts, capacity), members)
    arrived_attn_grad, arrived_attended = send_both(attn_grad_buffer, attended_out)
    owner_mixed = arrived_attended.reshape(-1, piece_cols)
    owner_attn_grad = arrived_attn_grad.reshape(-1, width)
    owner_mixed_grad = product(owner_attn_grad, output_weight).astype(jnp.bfloat16)
    output_grad = product_first(owner_attn_grad, owner_mixed)
    mixed_pieces = collect_pieces(
        return_rows(owner_mixed_grad.reshape(groups, capacity, piece_cols)),
        attn_targets,
        experts,
        members,
    )
    mixed_grad = heads_to_tokens(mixed_pieces)
    attn_gate_part = jnp.sum(middle_grad[:, None, :] * attn_pairs, axis=2)

    def backward_head(parts):
        return head_backward(parts[0], parts[1], parts[2], parts[3], parts[4], visible)

    query_heads_grad, key_heads_grad, value_heads_grad = lax.map(
        backward_head, (head_queries, head_keys, head_values, log_total, split_heads(mixed_grad))
    )
    query_pair_grad = join_heads(query_heads_grad)
    key_part, value_part = (
        lax.psum_scatter(
            join_heads(key_heads_grad).astype(jnp.bfloat16), "dp", scatter_dimension=0, tiled=True
        ).astype(jnp.float32),
        lax.psum_scatter(
            join_heads(value_heads_grad).astype(jnp.bfloat16), "dp", scatter_dimension=0, tiled=True
        ).astype(jnp.float32),
    )
    key_part = key_part.astype(jnp.bfloat16)
    value_part = value_part.astype(jnp.bfloat16)
    key_grad = product_first(normed, key_part)
    value_grad = product_first(normed, value_part)
    kv_norm_grad = product_last(key_part, key_weight) + product_last(value_part, value_weight)
    query_buffer = spread_pieces(
        heads_to_members(query_pair_grad, members, shards), attn_targets, experts, capacity, members
    )
    arrived_query_grad, arrived_normed = send_both(query_buffer, normed_out)
    owner_inputs = arrived_normed.reshape(-1, width)
    owner_query_grad = arrived_query_grad.reshape(-1, piece_cols)
    query_grad = product_first(owner_inputs, owner_query_grad)
    owner_input_grad = product_last(owner_query_grad, query_weight)
    query_back = collect_sums(
        return_sums(owner_input_grad.reshape(groups, capacity, width)),
        attn_targets,
        experts,
        members,
    ).reshape(tok_rows, top_count, width)
    attn_norm_grad, attn_gate_grad = shard_pair(
        kv_norm_grad + jnp.sum(query_back, axis=1), attn_gate_part
    )
    attn_logit_grad = logit_grad(attn_gates, attn_gate_grad, attn_onehot)
    attn_norm_grad = attn_norm_grad + product_last(attn_logit_grad, attn_router)
    attn_router_grad = product_first(normed, attn_logit_grad)
    input_part, attn_gain_grad = norm_backward(inputs, attn_scale, attn_gain, attn_norm_grad)
    tokens_grad = (middle_grad + input_part)[None]
    key_sum, value_sum, attn_router_sum, mlp_router_sum, attn_gain_sum, mlp_gain_sum = (
        lax.psum_scatter(key_grad, ("dp", "expert"), scatter_dimension=0, tiled=True),
        lax.psum_scatter(value_grad, ("dp", "expert"), scatter_dimension=0, tiled=True),
        lax.psum_scatter(attn_router_grad, ("dp", "expert"), scatter_dimension=0, tiled=True),
        lax.psum_scatter(mlp_router_grad, ("dp", "expert"), scatter_dimension=0, tiled=True),
        lax.psum_scatter(attn_gain_grad, ("dp", "expert"), scatter_dimension=0, tiled=True),
        lax.psum_scatter(mlp_gain_grad, ("dp", "expert"), scatter_dimension=0, tiled=True),
    )
    return (
        layer_out,
        tokens_grad,
        attn_gain_sum,
        mlp_gain_sum,
        key_sum,
        value_sum,
        query_grad,
        output_grad,
        attn_router_sum,
        gate_grad,
        up_grad,
        down_grad,
        mlp_router_sum,
    )


def solution(mesh):
    in_specs = (
        P("expert", "dp", None),
        P("expert", "dp", None),
        P(),
        P(),
        P(None, "shard"),
        P(None, "shard"),
        P(None, ("dp", "expert", "shard")),
        P(None, ("dp", "expert", "shard")),
        P(),
        P(None, ("dp", "expert", "shard")),
        P(None, ("dp", "expert", "shard")),
        P(None, ("dp", "expert", "shard")),
        P(),
        P("expert", None),
        P("expert", None),
        P("expert", "dp", None),
        P("expert", "dp", None),
        P("expert", "dp", None),
    )
    out_specs = (
        P("expert", "dp", None),
        P("expert", "dp", None),
        P(("dp", "expert")),
        P(("dp", "expert")),
        P(("dp", "expert"), "shard"),
        P(("dp", "expert"), "shard"),
        P(None, ("dp", "expert", "shard")),
        P(None, ("dp", "expert", "shard")),
        P(("dp", "expert"), None),
        P(None, ("dp", "expert", "shard")),
        P(None, ("dp", "expert", "shard")),
        P(None, ("dp", "expert", "shard")),
        P(("dp", "expert"), None),
    )
    return jax.shard_map(
        per_device, mesh=mesh, in_specs=in_specs, out_specs=out_specs, check_vma=False
    )
```

profile of v0, /device:TPU:0, one launch (start us, length us, event | category | flops | bytes accessed | tf_op | source)
XLA Modules:
  0.0 1798.9 jit_solution(12131727939745256674)
XLA Ops:
  26.9 7.5 all-to-all-start
  38.1 63.7 %all-to-all-done = bf16[16,40,2048]{2,1,0:T(8,128)(2,1)} async-done(((bf16[16,40,2048]{2,1,0:T(8,128)(2,1)}), bf16[16,40,2048]{2,1,0:T(8,128)(2,1)}, u32[]{:S(2)}, u32[]{:S(2)}) %all-to-all-start) | async-done | bytes 2621472 | tf_op jit(solution)/shard_map/all_to_all | solution.py:149
  106.6 14.1 all-to-all-start.1
  124.7 17.2 all-to-all-done.1
  164.4 44.2 %while.28 = (s32[]{:T(128)}, bf16[8,256,128]{1,2,0:T(8,128)(2,1)}, f32[8,256,1]{1,2,0:T(1,128)}, bf16[8,256,128]{2,1,0:T(8,128)(2,1)}, bf16[8,1024,128]{2,1,0:T(...) while((s32[]{:T(128)}, bf16[8,256,128]{1,2,0:T(8,128)(2,1)}, ...), condition=%wide.region_11.13_spmd.clone, body=%wide.region_8.0_spmd.clone.sunk | while | flops 136347392 | bytes 5254249 | solution.py:261
  208.6 11.4 all_to_all.106
  228.2 28.5 %all_to_all.99 = bf16[16,40,512]{2,1,0:T(8,128)(2,1)S(1)} all-to-all(bf16[16,40,512]{2,1,0:T(8,128)(2,1)S(1)} %bitcast.299), channel_id=1, replica_groups=mesh['dp'=8,'expert'=2,'shard'=2] {'dp','expert'}, dimensions={0} | all-to-all | bytes 1310720 | tf_op jit(solution)/shard_map/all_to_all | solution.py:149
  267.2 94.9 %all-to-all-done.5 = f32[16,40,2048]{2,1,0:T(8,128)} async-done(((f32[16,40,2048]{2,1,0:T(8,128)}), f32[16,40,2048]{2,1,0:T(8,128)}, u32[]{:S(2)}, u32[]{:S(2)}) %all-to-all-start.5) | async-done | bytes 5242912 | tf_op jit(solution)/shard_map/all_to_all | solution.py:164
  384.7 58.1 %all-reduce.8.cloned.1.call-done = f32[128,2048]{1,0:T(8,128)} async-done(((f32[128,2048]{1,0:T(8,128)}), f32[128,2048]{1,0:T(8,128)}) %all-reduce.8.cloned.1.call-update) | async-done | bytes 1048592 | tf_op jit(solution)/shard_map/psum | solution.py:168
  454.9 64.4 %all_to_all.100 = bf16[16,40,2048]{2,1,0:T(8,128)(2,1)S(1)} all-to-all(bf16[16,40,2048]{2,1,0:T(8,128)(2,1)S(1)} %bitcast.280), channel_id=1, replica_groups=mesh['dp'=8,'expert'=2,'shard'=2] {'dp','expert'}, dimensions={0} | all-to-all | bytes 5242880 | tf_op jit(solution)/shard_map/all_to_all | solution.py:149
  519.4 7.6 fusion.95
  553.3 87.1 %all-to-all-done.7 = f32[16,40,2048]{2,1,0:T(8,128)} async-done(((f32[16,40,2048]{2,1,0:T(8,128)}), f32[16,40,2048]{2,1,0:T(8,128)}, u32[]{:S(2)}, u32[]{:S(2)}) %all-to-all-start.7) | async-done | bytes 5242912 | tf_op jit(solution)/shard_map/all_to_all | solution.py:164
  666.3 82.5 %all_to_all.101 = bf16[16,40,2048]{2,1,0:T(8,128)(2,1)S(1)} all-to-all(bf16[16,40,2048]{2,1,0:T(8,128)(2,1)S(1)} %bitcast.281), channel_id=1, replica_groups=mesh['dp'=8,'expert'=2,'shard'=2] {'dp','expert'}, dimensions={0} | all-to-all | bytes 5242880 | tf_op jit(solution)/shard_map/all_to_all | solution.py:154
  748.8 8.7 multiply_convert_fusion.1
  766.1 119.7 %all_to_all.102 = f32[16,40,2048]{2,1,0:T(8,128)S(1)} all-to-all(f32[16,40,2048]{2,1,0:T(8,128)S(1)} %bitcast.284), channel_id=1, replica_groups=mesh['dp'=8,'expert'=2,'shard'=2] {'dp','expert'}, dimensions={0} | all-to-all | bytes 10485760 | tf_op jit(solution)/shard_map/all_to_all | solution.py:164
  915.4 17.8 all-reduce.12.cloned.1.call-done
  935.8 40.3 %all-reduce.10.cloned.1.call-done = f32[128,2048]{1,0:T(8,128)} async-done(((f32[128,2048]{1,0:T(8,128)}), f32[128,2048]{1,0:T(8,128)}) %all-reduce.10.cloned.1.call-update) | async-done | bytes 1048592 | tf_op jit(solution)/shard_map/psum | solution.py:168
  990.1 64.0 %all_to_all.103 = bf16[16,40,2048]{2,1,0:T(8,128)(2,1)S(1)} all-to-all(bf16[16,40,2048]{2,1,0:T(8,128)(2,1)S(1)} %bitcast.282), channel_id=1, replica_groups=mesh['dp'=8,'expert'=2,'shard'=2] {'dp','expert'}, dimensions={0} | all-to-all | bytes 5242880 | tf_op jit(solution)/shard_map/all_to_all | solution.py:154
  1055.6 23.2 %all_to_all.104 = bf16[16,40,512]{2,1,0:T(8,128)(2,1)S(1)} all-to-all(bf16[16,40,512]{2,1,0:T(8,128)(2,1)S(1)} %bitcast.313), channel_id=1, replica_groups=mesh['dp'=8,'expert'=2,'shard'=2] {'dp','expert'}, dimensions={0} | all-to-all | bytes 1310720 | tf_op jit(solution)/shard_map/all_to_all | solution.py:160
  1085.5 8.7 all-to-all-done.12
  1095.0 76.7 %while.29 = (s32[]{:T(128)}, bf16[8,256,128]{1,2,0:T(8,128)(2,1)}, bf16[8,1024,128]{1,2,0:T(8,128)(2,1)}, bf16[8,1024,128]{1,2,0:T(8,128)(2,1)}, bf16[8,256,128]...) while((s32[]{:T(128)}, bf16[8,256,128]{1,2,0:T(8,128)(2,1)}, ...), condition=%wide.region_37.40_spmd.clone, body=%wide.region_35.39_spmd.clone.sunk | while | flops 338198272 | bytes 11478145 | solution.py:346
  1171.7 11.4 all_to_all.107
  1185.9 21.1 %all_to_all.105 = bf16[16,40,512]{2,1,0:T(8,128)(2,1)S(1)} all-to-all(bf16[16,40,512]{2,1,0:T(8,128)(2,1)S(1)} %bitcast.303), channel_id=1, replica_groups=mesh['dp'=8,'expert'=2,'shard'=2] {'dp','expert'}, dimensions={0} | all-to-all | bytes 1310720 | tf_op jit(solution)/shard_map/all_to_all | solution.py:154
  1224.2 135.8 %reduce-scatter.19.cloned.1.call-done = bf16[128,1024]{1,0:T(8,128)(2,1)} async-done(((bf16[1024,1024]{1,0:T(8,128)(2,1)}), bf16[128,1024]{1,0:T(8,128)(2,1)}) %reduce-scatter.19.cloned.1.call-update) | async-done | bytes 262160
  1380.5 50.4 %reduce-scatter.21.cloned.1.call-done = bf16[128,1024]{1,0:T(8,128)(2,1)} async-done(((bf16[1024,1024]{1,0:T(8,128)(2,1)}), bf16[128,1024]{1,0:T(8,128)(2,1)}) %reduce-scatter.21.cloned.1.call-update) | async-done | bytes 262160
  1457.5 9.8 fusion.103
  1467.3 7.8 fusion.102
  1475.1 7.8 fusion.101
  1495.2 57.6 %all-reduce.2 = (f32[2048]{0:T(1024)S(1)}, f32[2048]{0:T(1024)S(1)}) all-reduce(f32[2048]{0:T(1024)S(1)} %get-tuple-element.205, f32[2048]{0:T(1024)S(1)} %get-tuple-element.203), channel_id=4, replica_groups=mesh['dp'=8,'expert'=2,'shard'=2] {'dp','expert'}, use_global_device_ids=true, to_apply=%region_50.53.clone | all-reduce | flops 4096 | bytes 32768
  1556.7 17.9 reduce-scatter.15.cloned.1.call-done
  1574.6 108.3 %reduce-scatter.13.cloned.1.call-done = f32[128,1024]{1,0:T(8,128)} async-done(((f32[2048,1024]{1,0:T(8,128)}), f32[128,1024]{1,0:T(8,128)}) %reduce-scatter.13.cloned.1.call-update) | async-done | bytes 524304 | tf_op jit(solution)/shard_map/reduce_scatter | solution.py:387
  1682.9 108.9 %reduce-scatter.11.cloned.1.call-done = f32[128,1024]{1,0:T(8,128)} async-done(((f32[2048,1024]{1,0:T(8,128)}), f32[128,1024]{1,0:T(8,128)}) %reduce-scatter.11.cloned.1.call-update) | async-done | bytes 524304 | tf_op jit(solution)/shard_map/reduce_scatter | solution.py:386
  (481 shorter events, 426.0 us)
Async XLA Ops:
  7.2 250.4 %copy-start = (bf16[2048,512]{1,0:T(8,128)(2,1)S(1)}, bf16[2048,512]{1,0:T(8,128)(2,1)}, u32[]{:S(2)}) copy-start(bf16[2048,512]{1,0:T(8,128)(2,1)} %param.33) | copy-start | bytes 6291460
  7.2 114.1 %all-gather.5.cloned.1.call-start = ((), (), s32[]{:S(2)}) async-start(), calls=%async_computation.23 | async-start | bytes 2359296 | tf_op jit(solution)/shard_map/all_gather | solution.py:240
  10.4 256.3 %copy-start.2 = (bf16[128,2048]{1,0:T(8,128)(2,1)}, bf16[128,2048]{1,0:T(8,128)(2,1)S(1)}, u32[]{:S(2)}) copy-start(bf16[128,2048]{1,0:T(8,128)(2,1)S(1)} %fusion.53) | copy-start | bytes 1572868
  26.9 74.9 %all-to-all-start = ((bf16[16,40,2048]{2,1,0:T(8,128)(2,1)}), bf16[16,40,2048]{2,1,0:T(8,128)(2,1)}, u32[]{:S(2)}, u32[]{:S(2)}) async-start(bf16[16,40,2048]{2,1,0:T(8,128)(2,1)} %bitcast.279), calls=%async_computation | async-start | bytes 5242880 | tf_op jit(solution)/shard_map/all_to_all | solution.py:149
  34.4 121.8 %all-gather.3.cloned.1.call-start = ((), (), s32[]{:S(2)}) async-start(), calls=%async_computation.22 | async-start | bytes 2359296 | tf_op jit(solution)/shard_map/all_gather | solution.py:239
  106.6 35.2 %all-to-all-start.1 = ((bf16[16,40,512]{2,1,0:T(8,128)(2,1)}), bf16[16,40,512]{2,1,0:T(8,128)(2,1)}, u32[]{:S(2)}, u32[]{:S(2)}) async-start(bf16[16,40,512]{2,1,0:T(8,128)(2,1)} %bitcast.312), calls=%async_computation.1 | async-start | bytes 1310720 | tf_op jit(solution)/shard_map/all_to_all | solution.py:160
  120.8 246.0 %copy-start.28 = (s32[1024]{0:T(1024)}, s32[1024]{0:T(1024)S(1)}, u32[]{:S(2)}) copy-start(s32[1024]{0:T(1024)S(1)} %pad_clamp_fusion.1) | copy-start | bytes 12292
  150.1 12.4 all-to-all-start.2
  261.5 100.6 %all-to-all-start.5 = ((f32[16,40,2048]{2,1,0:T(8,128)}), f32[16,40,2048]{2,1,0:T(8,128)}, u32[]{:S(2)}, u32[]{:S(2)}) async-start(f32[16,40,2048]{2,1,0:T(8,128)} %fusion.47), calls=%async_computation.5 | async-start | bytes 10485760 | tf_op jit(solution)/shard_map/all_to_all | solution.py:164
  266.2 176.6 %all-reduce.8.cloned.1.call-start = ((), (), s32[]{:S(2)}) async-start(), calls=%async_computation.24 | async-start | bytes 2097152 | tf_op jit(solution)/shard_map/psum | solution.py:168
  267.0 99.8 %copy-start.23 = (f32[128,2]{0,1:T(2,128)}, f32[128,2]{0,1:T(2,128)S(1)}, u32[]{:S(2)}) copy-start(f32[128,2]{0,1:T(2,128)S(1)} %select_reduce_fusion.5) | copy-start | bytes 3076
  267.0 99.7 %copy-start.38 = (f32[128]{0:T(128)}, f32[128]{0:T(128)S(1)}, u32[]{:S(2)}) copy-start(f32[128]{0:T(128)S(1)} %reduce_max.27) | copy-start | bytes 1540
  267.0 99.7 %copy-start.40 = (f32[128]{0:T(128)}, f32[128]{0:T(128)S(1)}, u32[]{:S(2)}) copy-start(f32[128]{0:T(128)S(1)} %fusion.88) | copy-start | bytes 1540
  454.9 72.1 %slice-start.4 = ((s8[5767168]{0:T(1024)(128)(4,1)}), s8[4194304]{0:T(1024)(128)(4,1)S(1)}, s32[]{:S(2)}) async-start(s8[5767168]{0:T(1024)(128)(4,1)} %bitcast.334), calls=%async_computation.38 | async-start | bytes 8388608
  539.2 101.1 %all-to-all-start.7 = ((f32[16,40,2048]{2,1,0:T(8,128)}), f32[16,40,2048]{2,1,0:T(8,128)}, u32[]{:S(2)}, u32[]{:S(2)}) async-start(f32[16,40,2048]{2,1,0:T(8,128)} %bitcast.283), calls=%async_computation.7 | async-start | bytes 10485760 | tf_op jit(solution)/shard_map/all_to_all | solution.py:164
  544.4 388.9 %all-reduce.12.cloned.1.call-start = ((), (), s32[]{:S(2)}) async-start(), calls=%async_computation.26 | async-start | bytes 1048576 | tf_op jit(solution)/shard_map/psum | solution.py:173
  664.4 84.4 %copy-start.56 = (f32[640,1408]{1,0:T(8,128)S(1)}, f32[640,1408]{1,0:T(8,128)}, u32[]{:S(2)}) copy-start(f32[640,1408]{1,0:T(8,128)} %copy-done.55) | copy-start | bytes 10813444
  664.4 84.4 %copy-start.57 = (f32[640,1408]{1,0:T(8,128)S(1)}, f32[640,1408]{1,0:T(8,128)}, u32[]{:S(2)}) copy-start(f32[640,1408]{1,0:T(8,128)} %get-tuple-element.267) | copy-start | bytes 10813444
  666.3 91.3 %slice-start.2 = ((s8[5767168]{0:T(1024)(128)(4,1)}), s8[4194304]{0:T(1024)(128)(4,1)S(1)}, s32[]{:S(2)}) async-start(s8[5767168]{0:T(1024)(128)(4,1)} %bitcast.332), calls=%async_computation.36 | async-start | bytes 8388608
  666.3 95.6 %slice-start.6 = ((s8[5767168]{0:T(1024)(128)(4,1)}), s8[4194304]{0:T(1024)(128)(4,1)S(1)}, s32[]{:S(2)}) async-start(s8[5767168]{0:T(1024)(128)(4,1)} %bitcast.336), calls=%async_computation.40 | async-start | bytes 8388608
  904.8 71.3 %all-reduce.10.cloned.1.call-start = ((), (), s32[]{:S(2)}) async-start(), calls=%async_computation.25 | async-start | bytes 2097152 | tf_op jit(solution)/shard_map/psum | solution.py:168
  1081.8 12.4 all-to-all-start.12
  1210.9 153.9 %all-to-all-start.15 = ((f32[16,40,2048]{2,1,0:T(8,128)}), f32[16,40,2048]{2,1,0:T(8,128)}, u32[]{:S(2)}, u32[]{:S(2)}) async-start(f32[16,40,2048]{2,1,0:T(8,128)} %fusion.45), calls=%async_computation.15 | async-start | bytes 10485760 | tf_op jit(solution)/shard_map/all_to_all | solution.py:164
  1215.5 144.5 %reduce-scatter.19.cloned.1.call-start = ((), (), s32[]{:S(2)}) async-start(), calls=%async_computation.32 | async-start | bytes 2359296
  1219.6 211.4 %reduce-scatter.21.cloned.1.call-start = ((), (), s32[]{:S(2)}) async-start(), calls=%async_computation.33 | async-start | bytes 2359296
  1223.8 268.6 %all-reduce.14.cloned.1.call-start = ((), (), s32[]{:S(2)}) async-start(), calls=%async_computation.27 | async-start | bytes 1048576 | tf_op jit(solution)/shard_map/psum | solution.py:173
  1435.8 120.9 %reduce-scatter.17.cloned.1.call-start = ((), (), s32[]{:S(2)}) async-start(), calls=%async_computation.31 | async-start | bytes 69632 | tf_op jit(solution)/shard_map/reduce_scatter | solution.py:389
  1436.8 137.8 %reduce-scatter.15.cloned.1.call-start = ((), (), s32[]{:S(2)}) async-start(), calls=%async_computation.30 | async-start | bytes 69632 | tf_op jit(solution)/shard_map/reduce_scatter | solution.py:388
  1445.6 237.3 %reduce-scatter.13.cloned.1.call-start = ((), (), s32[]{:S(2)}) async-start(), calls=%async_computation.29 | async-start | bytes 8912896 | tf_op jit(solution)/shard_map/reduce_scatter | solution.py:387
  1450.2 341.6 %reduce-scatter.11.cloned.1.call-start = ((), (), s32[]{:S(2)}) async-start(), calls=%async_computation.28 | async-start | bytes 8912896 | tf_op jit(solution)/shard_map/reduce_scatter | solution.py:386
  1492.4 61.7 %copy-start.5 = (f32[128,2048]{1,0:T(8,128)S(1)}, f32[128,2048]{1,0:T(8,128)}, u32[]{:S(2)}) copy-start(f32[128,2048]{1,0:T(8,128)} %copy-done.4) | copy-start | bytes 3145732
  1492.4 299.5 %copy-start.1 = (bf16[2048,512]{1,0:T(8,128)(2,1)S(1)}, bf16[2048,512]{1,0:T(8,128)(2,1)}, u32[]{:S(2)}) copy-start(bf16[2048,512]{1,0:T(8,128)(2,1)} %param.33) | copy-start | bytes 6291460
  (53 other events, 470.8 us)
Sparse Core Ops, SparseCore 0:
  14.4 79.5 all-gather.4
  96.7 59.4 all-gather.2
  384.6 58.2 all-reduce.7
  904.9 28.3 all-reduce.11
  936.0 40.0 all-reduce.9
  1220.0 139.9 reduce-scatter.18
  1364.0 66.9 reduce-scatter.20
  1435.9 27.6 all-reduce.13
  1467.6 51.8 reduce-scatter.16
  1523.6 50.9 reduce-scatter.14
  1579.2 103.5 reduce-scatter.12
  1687.4 104.4 reduce-scatter.10
where the time goes:
time: 1810 us; the launch traced here: 1800 us
  waiting for transfers between devices  815 us (45%)
  blocking collectives  494 us (27%)
  matrix products  197 us (11%)
  local copies, waits for them, and re-layouts  156 us (9%)
  other arithmetic  75.2 us (4%)
  starting transfers between devices  44.9 us (2%)
    unnamed x14, waiting for transfers between devices  186 us
    all_to_all x3, waiting for transfers between devices, return_sums(): lax.all_to_all(buffers, ('dp', 'expert'), split_axis=0, concat_axis=0, ti...  182 us
    all_to_all x3, blocking collectives, send_both(): lax.all_to_all(grad_buffer, ('dp', 'expert'), split_axis=0, concat_axis=0...  168 us
    all_to_all x1, blocking collectives, return_sums(): lax.all_to_all(buffers, ('dp', 'expert'), split_axis=0, concat_axis=0, ti...  120 us
    reduce_scatter x1, waiting for transfers between devices, per_device(): lax.psum_scatter(key_grad, ('dp', 'expert'), scatter_dimension=0, tiled=T...  109 us
    reduce_scatter x1, waiting for transfers between devices, per_device(): lax.psum_scatter(value_grad, ('dp', 'expert'), scatter_dimension=0, tiled...  108 us
    psum x2, waiting for transfers between devices, shard_total(): return lax.psum(values, 'shard')  98.4 us
    all_to_all x2, blocking collectives, send_rows(): lax.all_to_all(buffers, ('dp', 'expert'), split_axis=0, concat_axis=0, ti...  92.9 us
  transfers between devices with their start and end apart: 19, of which 15 were waited for; matrix products, arithmetic and copies ran while one was open for 8% of the time, Pallas kernels for 0%

commit v1 on v0

v1 whole, which is shorter than its diff:
```python
import functools

import jax
import jax.numpy as jnp
from jax import lax
from jax.experimental import pallas as pl
from jax.experimental.pallas import tpu as pltpu
from jax.sharding import PartitionSpec as P

HEAD = 128

epsilon = 1e-06
negative = -1e30
scale = HEAD ** (-0.5)
bf16 = jnp.bfloat16
f32 = jnp.float32


def product(former, latter):
    return jnp.dot(former, latter, preferred_element_type=f32)


def product_last(former, latter):
    return lax.dot_general(
        former, latter, (((1,), (1,)), ((), ())), preferred_element_type=f32
    )


def product_first(former, latter):
    return lax.dot_general(
        former, latter, (((0,), (0,)), ((), ())), preferred_element_type=f32
    )


def swap(values, axis):
    return lax.ppermute(values, axis, [(0, 1), (1, 0)])


def pair_all_to_all(parts, axis):
    me = lax.axis_index(axis)
    mine = lax.dynamic_index_in_dim(parts, me, 0, keepdims=False)
    theirs = lax.dynamic_index_in_dim(parts, 1 - me, 0, keepdims=False)
    got = swap(theirs, axis)
    first = me == 0
    return jnp.stack([jnp.where(first, mine, got), jnp.where(first, got, mine)])


def ring_order(count):
    return list(range(0, count, 2)) + list(range(1, count, 2))[::-1]


def ring_gather(block, axis, width):
    count = lax.axis_size(axis)
    order = ring_order(count)
    order_of = jnp.array(order, jnp.int32)
    place = jnp.array([order.index(i) for i in range(count)], jnp.int32)[lax.axis_index(axis)]
    right = [(order[i], order[(i + 1) % count]) for i in range(count)]
    left = [(order[i], order[(i - 1) % count]) for i in range(count)]
    rows, columns = block.shape
    half = rows // 2
    out = jnp.zeros((count, rows, width), block.dtype)
    marks = jnp.zeros((count, 16, columns - width), block.dtype)

    def put(out, marks, piece, source, row):
        out = lax.dynamic_update_slice(out, piece[None, :, :width], (source, row, 0))
        if row == 0:
            marks = lax.dynamic_update_slice(marks, piece[None, :16, width:], (source, 0, 0))
        return out, marks

    out, marks = put(out, marks, block, lax.axis_index(axis), 0)
    forward, backward = block, block
    for step in range(1, count // 2 + 1):
        last = step == count // 2
        if last:
            forward, backward = forward[:half], backward[half:]
        forward = lax.ppermute(forward, axis, right)
        backward = lax.ppermute(backward, axis, left)
        out, marks = put(out, marks, forward, order_of[(place - step) % count], 0)
        out, marks = put(out, marks, backward, order_of[(place + step) % count], half if last else 0)
    return out.reshape(count * rows, width), marks


def after(values, *events):
    return lax.optimization_barrier((values,) + events)[0]


def all_to_all_permutes(parts, axis):
    count = lax.axis_size(axis)
    me = lax.axis_index(axis)
    out = parts
    for step in range(1, count):
        sent = lax.dynamic_index_in_dim(parts, (me + step) % count, 0, keepdims=True)
        got = lax.ppermute(sent, axis, [(i, (i + step) % count) for i in range(count)])
        out = lax.dynamic_update_slice_in_dim(out, got, (me - step) % count, 0)
    return out


def ring_scatter(chunks, count, stride):
    order = ring_order(count)
    order_of = jnp.array(order, jnp.int32)
    member = lax.axis_index("dp") // stride
    place = jnp.array([order.index(i) for i in range(count)], jnp.int32)[member]

    def moves(by):
        return [
            (order[i] * stride + j, order[(i + by) % count] * stride + j)
            for i in range(count)
            for j in range(stride)
        ]

    right, left = moves(1), moves(-1)
    half = chunks.shape[1] // 2
    far = count // 2

    def chunk(offset):
        return lax.dynamic_index_in_dim(chunks, order_of[(place + offset) % count], 0, keepdims=False)

    def added(sent, first, offset):
        own = chunk(offset).astype(f32)
        if first is None:
            return (own + sent.astype(f32)).astype(bf16)
        lower, upper = own[:half], own[half:]
        if first:
            lower = lower + sent.astype(f32)
        else:
            upper = upper + sent.astype(f32)
        return jnp.concatenate([lower, upper]).astype(bf16)

    forward, backward = chunk(far)[:half], chunk(-far)[half:]
    for step in range(far):
        event = forward
        forward = lax.ppermute(forward, "dp", right)
        backward = lax.ppermute(backward, "dp", left)
        offset = far - 1 - step
        if offset:
            forward = added(forward, True if step == 0 else None, offset)
            backward = added(backward, False if step == 0 else None, -offset)
    return chunk(0).astype(f32) + forward.astype(f32) + backward.astype(f32), event


def attend_body(tiles, keys_per_tile, q_ref, k_ref, v_ref, bias_ref, out_ref, total_ref):
    rows = q_ref.shape[0] // tiles
    for tile in range(tiles):
        here = pl.ds(tile * rows, rows)
        keys = (tile + 1) * keys_per_tile
        scores = product_last(q_ref[here, :], k_ref[:keys, :]) * scale
        scores = scores + bias_ref[here, :keys].astype(f32)
        highest = jnp.max(scores, axis=1, keepdims=True)
        expo = jnp.exp(scores - highest)
        summed = jnp.sum(expo, axis=1, keepdims=True)
        probs = (expo * (1.0 / summed)).astype(bf16)
        out_ref[here, :] = product(probs, v_ref[:keys, :]).astype(bf16)
        total_ref[0, here, :] = highest + jnp.log(summed)


def attend(queries, shared, bias, tiles):
    rows, columns = queries.shape
    length = shared.shape[0]
    heads = columns // HEAD
    return pl.pallas_call(
        functools.partial(attend_body, tiles, length // tiles),
        grid=(heads,),
        in_specs=[
            pl.BlockSpec((rows, HEAD), lambda h: (0, h)),
            pl.BlockSpec((length, HEAD), lambda h: (0, h)),
            pl.BlockSpec((length, HEAD), lambda h: (0, heads + h)),
            pl.BlockSpec((rows, length), lambda h: (0, 0)),
        ],
        out_specs=[
            pl.BlockSpec((rows, HEAD), lambda h: (0, h)),
            pl.BlockSpec((1, rows, 1), lambda h: (h, 0, 0)),
        ],
        out_shape=[
            jax.ShapeDtypeStruct((rows, columns), bf16),
            jax.ShapeDtypeStruct((heads, rows, 1), f32),
        ],
        compiler_params=pltpu.CompilerParams(vmem_limit_bytes=48 * 2**20),
        cost_estimate=pl.CostEstimate(
            flops=4 * rows * length * columns,
            bytes_accessed=2 * (rows * length + 2 * length * columns),
            transcendentals=rows * length * heads,
        ),
        name="attend",
    )(queries, shared, shared, bias)


def attend_back_body(
    tiles, keys_per_tile, q_ref, k_ref, v_ref, bias_ref, total_ref, grad_ref, dq_ref, dk_ref, dv_ref, dk_sum, dv_sum
):
    rows = q_ref.shape[0] // tiles
    dk_sum[...] = jnp.zeros_like(dk_sum)
    dv_sum[...] = jnp.zeros_like(dv_sum)
    for tile in range(tiles):
        here = pl.ds(tile * rows, rows)
        keys = (tile + 1) * keys_per_tile
        query, grad = q_ref[here, :], grad_ref[here, :]
        scores = product_last(query, k_ref[:keys, :]) * scale
        scores = scores + bias_ref[here, :keys].astype(f32)
        probs = jnp.exp(scores - total_ref[0, here, :])
        prob_grad = product_last(grad, v_ref[:keys, :])
        inner = jnp.sum(probs * prob_grad, axis=1, keepdims=True)
        score_grad = (probs * (prob_grad - inner) * scale).astype(bf16)
        dq_ref[here, :] = product(score_grad, k_ref[:keys, :]).astype(bf16)
        dk_sum[:keys, :] += product_first(score_grad, query)
        dv_sum[:keys, :] += product_first(probs.astype(bf16), grad)
    dk_ref[...] = dk_sum[...].astype(bf16)
    dv_ref[...] = dv_sum[...].astype(bf16)


def attend_back(queries, shared, bias, total, grads, tiles):
    rows, columns = queries.shape
    length = shared.shape[0]
    heads = columns // HEAD
    row_spec = pl.BlockSpec((rows, HEAD), lambda h: (0, h))
    key_spec = pl.BlockSpec((length, HEAD), lambda h: (0, h))
    return pl.pallas_call(
        functools.partial(attend_back_body, tiles, length // tiles),
        grid=(heads,),
        in_specs=[
            row_spec,
            key_spec,
            pl.BlockSpec((length, HEAD), lambda h: (0, heads + h)),
            pl.BlockSpec((rows, length), lambda h: (0, 0)),
            pl.BlockSpec((1, rows, 1), lambda h: (h, 0, 0)),
            row_spec,
        ],
        out_specs=[row_spec, key_spec, key_spec],
        out_shape=[
            jax.ShapeDtypeStruct((rows, columns), bf16),
            jax.ShapeDtypeStruct((length, columns), bf16),
            jax.ShapeDtypeStruct((length, columns), bf16),
        ],
        scratch_shapes=[pltpu.VMEM((length, HEAD), f32), pltpu.VMEM((length, HEAD), f32)],
        compiler_params=pltpu.CompilerParams(vmem_limit_bytes=48 * 2**20),
        cost_estimate=pl.CostEstimate(
            flops=10 * rows * length * columns,
            bytes_accessed=2 * (rows * length + 4 * length * columns),
            transcendentals=rows * length * heads,
        ),
        name="attend_back",
    )(queries, shared, shared, bias, total, grads)


def pair_slots(routes, ranking, capacity):
    flat_routes, flat_rank = routes.reshape(-1), ranking.reshape(-1)
    same_expert = flat_routes[:, None] == flat_routes[None, :]
    earlier = flat_rank[None, :] < flat_rank[:, None]
    slots = jnp.sum(jnp.logical_and(same_expert, earlier).astype(jnp.int32), axis=1)
    return jnp.minimum(slots, capacity).reshape(routes.shape)


def own_mask(routes, slots, experts, capacity):
    places = jnp.arange(experts * capacity)[:, None]
    hits = [
        (places // capacity == routes[k][None]) & (places % capacity == slots[k][None])
        for k in range(2)
    ]
    return jnp.logical_or(hits[0], hits[1]).astype(bf16)


def expert_mask(marks, expert, capacity):
    slots = jnp.arange(capacity, dtype=jnp.int32)[None, :, None]
    hits = [
        (marks[:, 2 * k][:, None] == expert) & (marks[:, 2 * k + 1][:, None] == slots)
        for k in range(2)
    ]
    other = sum(
        jnp.sum(jnp.where(hits[k], marks[:, 2 - 2 * k][:, None], 0), axis=2) for k in range(2)
    )
    return jnp.logical_or(hits[0], hits[1]), other.reshape(-1)


def gate_of(rows, router, expert, other):
    logits = product(rows, router)
    range_of = jnp.arange(router.shape[1])[None, :]
    own_hot = (range_of == expert).astype(f32)
    other_hot = (range_of == other[:, None]).astype(f32)
    difference = own_hot - other_hot
    gate = jax.nn.sigmoid(jnp.sum(logits * difference, axis=1, keepdims=True))
    return gate, difference


def row_bias(chosen, segments, parents):
    blocks, capacity, count = chosen.shape
    length = segments.shape[0]
    seg_blocks = segments.reshape(blocks, 1, count)
    here = jnp.arange(count)[None, None, :]
    own = jnp.sum(jnp.where(chosen, seg_blocks, 0), axis=2).reshape(-1, 1)
    place = jnp.sum(jnp.where(chosen, here, 0), axis=2) + jnp.arange(blocks)[:, None] * count
    place = place.reshape(-1, 1)
    range_of = jnp.arange(parents.shape[0])[None, :]
    one = jnp.sum(jnp.where(own == range_of, parents[None, :], 0), axis=1, keepdims=True)
    two = jnp.sum(jnp.where(one == range_of, parents[None, :], 0), axis=1, keepdims=True)
    keys = segments[None, :]
    visible = ((keys == own) | (keys == one) | (keys == two)) & (jnp.arange(length)[None, :] <= place)
    return jnp.where(visible, 0.0, negative).astype(bf16)


def per_device(
    tokens,
    cotangent,
    attn_gain,
    mlp_gain,
    key_weight,
    value_weight,
    query_weight,
    output_weight,
    attn_router,
    gate_weight,
    up_weight,
    down_weight,
    mlp_router,
    segment_ids,
    parent_ids,
    attn_routes,
    mlp_routes,
    slot_order,
):
    count, width = tokens.shape[1:]
    half = width // 2
    piece = query_weight.shape[1]
    experts = attn_router.shape[1]
    blocks = lax.axis_size("dp")
    members = blocks // experts
    capacity = min(count, 5 * count * attn_routes.shape[2] // (4 * experts))
    length, parents = segment_ids.shape[1], parent_ids.shape[1]
    tiles = blocks // 2
    dp, core, shard = lax.axis_index("dp"), lax.axis_index("expert"), lax.axis_index("shard")
    expert, member = dp // members, dp % members

    def my_half(values):
        return lax.dynamic_slice_in_dim(values, shard * half, half, values.ndim - 1)

    def their_half(values):
        return lax.dynamic_slice_in_dim(values, (1 - shard) * half, half, values.ndim - 1)

    def whole(mine):
        got = swap(mine, "shard")
        first = shard == 0
        return jnp.concatenate(
            [jnp.where(first, mine, got), jnp.where(first, got, mine)], axis=mine.ndim - 1
        )

    ranking = slot_order[0, 0].reshape(count, -1).T
    own_attn, own_mlp = attn_routes[0].T, mlp_routes[0].T
    attn_slots = pair_slots(own_attn, ranking, capacity)
    mlp_slots = pair_slots(own_mlp, ranking, capacity)
    attn_pack = own_mask(own_attn, attn_slots, experts, capacity)
    mlp_pack = own_mask(own_mlp, mlp_slots, experts, capacity)
    own_segments = lax.dynamic_slice_in_dim(segment_ids, dp * count, count, 1)
    marks = [own_attn[:1], attn_slots[:1], own_attn[1:], attn_slots[1:]]
    marks += [own_mlp[:1], mlp_slots[:1], own_mlp[1:], mlp_slots[1:]]
    marks += [own_segments, jnp.pad(parent_ids, ((0, 0), (0, count - parent_ids.shape[1])))]
    marks = jnp.pad(jnp.concatenate(marks), ((0, count - 10), (0, 0))).astype(bf16)

    def dispatch(values, pack, permutes=False):
        packed = product(pack, values).astype(bf16).reshape(experts, 1, capacity, half)
        packed = jnp.broadcast_to(packed, (experts, members, capacity, half))
        packed = packed.reshape(blocks, capacity, half)
        if permutes:
            arrived = all_to_all_permutes(packed, "dp")
        else:
            arrived = lax.all_to_all(packed, "dp", 0, 0, tiled=True)
        own = whole(arrived.reshape(blocks * capacity, half))
        return jnp.concatenate([own, swap(own, "expert")])

    def combine(rows, pack):
        own, other = jnp.split(rows, 2)
        got = swap(other, "expert")
        theirs = (their_half(own).astype(f32) + their_half(got).astype(f32)).astype(bf16)
        back = swap(theirs, "shard")
        mine = my_half(own).astype(f32) + my_half(got).astype(f32) + back.astype(f32)
        mine = mine.astype(bf16).reshape(blocks, capacity, half)
        back = lax.all_to_all(mine, "dp", 0, 0, tiled=True)
        if members > 1:
            back = back.reshape(experts, members, capacity, half).astype(f32)
            back = jnp.sum(back, axis=1).astype(bf16)
        return product_first(pack, back.reshape(experts * capacity, half))

    heads_at = (member * 2 + core) * 2 + shard
    holder = (member * 2 + core) // members
    offset = holder * 2 * members
    names = ("dp", "expert", "shard")
    sends = []
    for d in range(blocks):
        for c in range(2):
            at = (d * 2 + c) * 2
            source = ((d % members) * 2 + c) // members
            sends.append((at + source, at + 1 - source))
    partner_at = (member * 2 + core) * 2 + 1 - shard

    def head_columns(at):
        return jnp.concatenate(
            [
                lax.dynamic_slice_in_dim(weight, (at - offset) * piece, piece, 1)
                for weight in (key_weight, value_weight)
            ],
            axis=1,
        )

    inputs = tokens[0].astype(f32)
    attn_scale = lax.rsqrt(jnp.mean(inputs * inputs, axis=1, keepdims=True) + epsilon)
    normed = (inputs * attn_scale * attn_gain).astype(bf16)
    own_normed, own_marks = ring_gather(jnp.concatenate([normed, marks], axis=1), "dp", width)
    tree_normed = [own_normed, swap(own_normed, "expert")]
    tree_marks = [m.astype(jnp.int32) for m in (own_marks, swap(own_marks, "expert"))]
    got = lax.ppermute(after(head_columns(partner_at), normed), names, sends)
    shared_weight = jnp.where(shard == holder, head_columns(heads_at), got)
    grad_half = my_half(cotangent[0])
    grad_rows = dispatch(after(grad_half, own_normed), mlp_pack, permutes=True)

    attn_marks = [expert_mask(m[:, :4], expert, capacity) for m in tree_marks]
    mlp_marks = [expert_mask(m[:, 4:8], expert, capacity) for m in tree_marks]
    biases = [
        row_bias(attn_marks[t][0], tree_marks[t][:, 8].reshape(-1), tree_marks[t][0, 9, :parents])
        for t in range(2)
    ]
    attn_other = jnp.concatenate([attn_marks[0][1], attn_marks[1][1]])
    mlp_other = jnp.concatenate([mlp_marks[0][1], mlp_marks[1][1]])

    tree_rows, tree_shared = [], []
    for t in range(2):
        tree_shared.append(product(tree_normed[t], shared_weight).astype(bf16))
        picked = lax.dot_general(
            attn_marks[t][0].astype(bf16),
            tree_normed[t].reshape(blocks, count, width),
            (((2,), (1,)), ((0,), (0,))),
            preferred_element_type=f32,
        )
        tree_rows.append(picked.astype(bf16).reshape(blocks * capacity, width))
    rows = jnp.concatenate(tree_rows)
    queries = product(rows, query_weight).astype(bf16)
    tree_queries = jnp.split(queries, 2)
    forward = [
        attend(tree_queries[t], tree_shared[t], biases[t], tiles) for t in range(2)
    ]
    attended = jnp.concatenate([forward[0][0], forward[1][0]])
    attn_gate, attn_difference = gate_of(rows, attn_router, expert, attn_other)
    attn_terms = product_last(attended, output_weight)
    attn_terms = (attn_gate * attn_terms).astype(bf16)
    attn_mix = combine(attn_terms, attn_pack)
    middle = my_half(inputs) + attn_mix

    def feature_mean(values):
        part = jnp.sum(values, axis=1, keepdims=True)
        return (part + swap(part, "shard")) / width

    mlp_scale = lax.rsqrt(feature_mean(middle * middle) + epsilon)
    half_gain = my_half(mlp_gain)
    mlp_normed = (middle * mlp_scale * half_gain).astype(bf16)
    mlp_rows = dispatch(mlp_normed, mlp_pack)
    mlp_gate, mlp_difference = gate_of(mlp_rows, mlp_router, expert, mlp_other)
    gate_pre = product(mlp_rows, gate_weight)
    up_pre = product(mlp_rows, up_weight)
    gate_sigmoid = jax.nn.sigmoid(gate_pre)
    silu_values = gate_pre * gate_sigmoid
    hidden = (silu_values * up_pre).astype(bf16)
    plain_grad = product(after(grad_rows, attn_terms), down_weight)
    mlp_gate_grad = jnp.sum(hidden.astype(f32) * plain_grad, axis=1, keepdims=True)
    hidden_grad = mlp_gate * plain_grad
    gate_pre_grad = (
        hidden_grad * up_pre * gate_sigmoid * (1.0 + gate_pre * (1.0 - gate_sigmoid))
    ).astype(bf16)
    up_pre_grad = (hidden_grad * silu_values).astype(bf16)
    mlp_coefs = mlp_gate * (1.0 - mlp_gate) * mlp_gate_grad * mlp_difference
    row_grad = (
        product_last(gate_pre_grad, gate_weight)
        + product_last(up_pre_grad, up_weight)
        + product_last(mlp_coefs, mlp_router.astype(f32))
    ).astype(bf16)
    mlp_normed_grad = combine(row_grad, mlp_pack)
    late_hidden = after(hidden, row_grad)
    mlp_terms = (mlp_gate * product_last(late_hidden, down_weight)).astype(bf16)
    down_grad = product_first((mlp_gate * grad_rows.astype(f32)).astype(bf16), late_hidden)
    mlp_router_part = product_first(mlp_coefs, mlp_rows.astype(f32))

    mlp_n = middle * mlp_scale
    weighted = mlp_normed_grad * half_gain
    mlp_gain_part = jnp.sum(mlp_normed_grad * mlp_n, axis=0)
    middle_grad = grad_half.astype(f32) + mlp_scale * (
        weighted - mlp_n * feature_mean(weighted * mlp_n)
    )
    low_grad = middle_grad.astype(bf16)
    term_rows = dispatch(low_grad, attn_pack)
    late_rows = after(mlp_rows, low_grad)
    gate_grad = product_first(late_rows, gate_pre_grad)
    up_grad = product_first(late_rows, up_pre_grad)
    mlp_mix = combine(after(mlp_terms, term_rows), mlp_pack)
    layer_out = whole((middle + mlp_mix).astype(bf16))[None]
    plain_attended_grad = product(term_rows, output_weight)
    attn_gate_grad = jnp.sum(attended.astype(f32) * plain_attended_grad, axis=1, keepdims=True)
    attended_grad = jnp.split((attn_gate * plain_attended_grad).astype(bf16), 2)
    backward = [
        attend_back(
            tree_queries[t],
            tree_shared[t],
            biases[t],
            forward[t][1],
            attended_grad[t],
            tiles,
        )
        for t in range(2)
    ]
    query_rows_grad = jnp.concatenate([backward[0][0], backward[1][0]])
    part = length // experts
    key_chunks = jnp.concatenate(
        [backward[t][i].reshape(experts, part, piece) for i in (1, 2) for t in range(2)], axis=1
    )
    key_sums, event = ring_scatter(key_chunks, experts, members)
    key_sums = key_sums.astype(bf16)
    attn_coefs = attn_gate * (1.0 - attn_gate) * attn_gate_grad * attn_difference
    input_rows_grad = product_last(query_rows_grad, query_weight) + product_last(
        attn_coefs, attn_router.astype(f32)
    )
    input_rows_grad = input_rows_grad.astype(bf16)
    normed_grad = combine(input_rows_grad, attn_pack)
    weight_chunks = jnp.concatenate(
        [
            sum(product_first(tree_normed[t], backward[t][i]) for t in range(2))
            .astype(bf16)
            .reshape(experts, width // experts, piece)
            for i in (1, 2)
        ],
        axis=1,
    )
    weight_sums = ring_scatter(after(weight_chunks, event), experts, members)[0]
    query_grad = product_first(after(rows, input_rows_grad), query_rows_grad)
    late_terms = after(term_rows, input_rows_grad)
    output_grad = product_first((attn_gate * late_terms.astype(f32)).astype(bf16), attended)
    attn_router_part = product_first(attn_coefs, rows.astype(f32))

    def shared_part(t):
        keys_part = key_sums[t * part : (t + 1) * part]
        values_part = key_sums[(2 + t) * part : (3 + t) * part]
        return product_last(jnp.concatenate([keys_part, values_part], axis=1), shared_weight)

    shared = shared_part(0) + swap(shared_part(1).astype(bf16), "expert").astype(f32)
    if members > 1:
        groups = [[e * members + m for m in range(members)] for e in range(experts)]
        shared = lax.psum_scatter(
            shared, "dp", scatter_dimension=0, axis_index_groups=groups, tiled=True
        )
    shared = my_half(shared) + swap(their_half(shared).astype(bf16), "shard").astype(f32)
    normed_grad = normed_grad + shared

    attn_n = my_half(inputs) * attn_scale
    weighted = normed_grad * my_half(attn_gain)
    attn_gain_part = jnp.sum(normed_grad * attn_n, axis=0)
    tokens_grad = middle_grad + attn_scale * (weighted - attn_n * feature_mean(weighted * attn_n))
    got = swap(tokens_grad.astype(bf16), "shard").astype(f32)
    tokens_grad = jnp.concatenate(
        [jnp.where(shard == 0, tokens_grad, got), jnp.where(shard == 0, got, tokens_grad)], axis=1
    )[None]

    features = width // (2 * blocks)
    pieces = weight_sums.astype(bf16).reshape(2, members, 2, features, piece).transpose(1, 2, 0, 3, 4)
    if members > 1:
        groups = [[e * members + m for m in range(members)] for e in range(experts)]
        pieces = lax.all_to_all(pieces, "dp", 0, 0, axis_index_groups=groups, tiled=True)
    pieces = pair_all_to_all(pieces.transpose(1, 0, 2, 3, 4), "expert")
    pieces = pieces.transpose(1, 0, 2, 3, 4).reshape(2, members, 2, features, piece)
    pieces = pair_all_to_all(pieces, "shard")
    pieces = pieces.transpose(2, 3, 1, 0, 4).reshape(2, features, -1).astype(f32)

    def spread(values):
        return lax.dynamic_update_slice(jnp.zeros((1, width), f32), values[None], (0, shard * half))

    def small_sum(values):
        values = values + swap(values, "shard")
        values = values.reshape(-1, blocks, 2, features).transpose(2, 1, 0, 3)
        mine = lax.dynamic_index_in_dim(values, core, 0, keepdims=False)
        theirs = lax.dynamic_index_in_dim(values, 1 - core, 0, keepdims=False)
        mine = mine + swap(theirs, "expert")
        return jnp.sum(lax.all_to_all(mine, "dp", 0, 0, tiled=True), axis=0)

    routers = small_sum(jnp.concatenate([attn_router_part, mlp_router_part]))
    gains = jnp.concatenate([spread(attn_gain_part), spread(mlp_gain_part)])
    gains = small_sum(jnp.pad(gains, ((0, 6), (0, 0))))
    return (
        layer_out,
        tokens_grad,
        gains[0],
        gains[1],
        pieces[0],
        pieces[1],
        query_grad,
        output_grad,
        routers[:experts].T,
        gate_grad,
        up_grad,
        down_grad,
        routers[experts:].T,
    )


def solution(mesh):
    tree = P("expert", "dp", None)
    columns = P(None, ("dp", "expert", "shard"))
    spread = P(("dp", "expert"), None)
    in_specs = (
        tree,
        tree,
        P(),
        P(),
        P(None, "shard"),
        P(None, "shard"),
        columns,
        columns,
        P(),
        columns,
        columns,
        columns,
        P(),
        P("expert", None),
        P("expert", None),
        tree,
        tree,
        tree,
    )
    out_specs = (
        tree,
        tree,
        P(("dp", "expert")),
        P(("dp", "expert")),
        P(("dp", "expert"), "shard"),
        P(("dp", "expert"), "shard"),
        columns,
        columns,
        spread,
        columns,
        columns,
        columns,
        spread,
    )
    return jax.shard_map(
        per_device, mesh=mesh, in_specs=in_specs, out_specs=out_specs, check_vma=False
    )
```

time: 1810 us -> 652 us (0.36)
  waiting for transfers between devices: 815 us -> 141 us
  blocking collectives: 494 us -> 0 us
  local copies, waits for them, and re-layouts: 156 us -> 63.2 us
  starting transfers between devices: 44.9 us -> 114 us
  matrix products: 197 us -> 156 us
  Pallas kernels: 0 us -> 32.9 us
  between operations: 16.1 us -> 48.9 us
    all_to_all x9 -> x0, blocking collectives: 426 us -> none  [the longest x3 168 us: send_both(): lax.all_to_all(grad_buffer, ('dp', 'expert'), split_axis=0, concat_axis=0...]
    all_to_all x7 -> x8, waiting for transfers between devices: 275 us -> 35.5 us  [the longest x4 23.2 us: combine(): back = lax.all_to_all(mine, 'dp', 0, 0, tiled=True)]
    reduce_scatter x4 -> x0, waiting for transfers between devices: 235 us -> none  [the longest x1 109 us: per_device(): lax.psum_scatter(key_grad, ('dp', 'expert'), scatter_dimension=0, tiled=T...]
    unnamed x14 -> x0, waiting for transfers between devices: 186 us -> none
    psum x4 -> x0, waiting for transfers between devices: 116 us -> none  [the longest x2 98.4 us: shard_total(): return lax.psum(values, 'shard')]
    ppermute x0 -> x61, waiting for transfers between devices: none -> 105 us  [the longest x29 67.3 us: swap(): return lax.ppermute(values, axis, [(0, 1), (1, 0)])]
    ppermute x0 -> x61, starting transfers between devices: none -> 70.4 us  [the longest x29 22.4 us: swap(): return lax.ppermute(values, axis, [(0, 1), (1, 0)])]
    unnamed x1 -> x0, blocking collectives: 57.6 us -> none
  transfers between devices with their start and end apart: 19 -> 69, of which waited for: 15 -> 24; matrix products, arithmetic and copies ran while one was open for 8% -> 33% of each run, Pallas kernels for 0% -> 0%
where the time goes in v1:
time: 652 us; the launch traced here: 643 us
  matrix products  156 us (24%)
  waiting for transfers between devices  141 us (22%)
  starting transfers between devices  114 us (17%)
  other arithmetic  87.5 us (13%)
  local copies, waits for them, and re-layouts  63.2 us (10%)
  between operations  48.9 us (8%)
  Pallas kernels  32.9 us (5%)
    dot_general x15, matrix products, product_first(): lax.dot_general(former, latter, (((0,), (0,)), ((), ())), preferred_eleme...  69.2 us
    ppermute x29, waiting for transfers between devices, swap(): return lax.ppermute(values, axis, [(0, 1), (1, 0)])  67.3 us
    dot_general x12, matrix products, product(): return jnp.dot(former, latter, preferred_element_type=f32)  48.9 us
    dot_general x9, matrix products, product_last(): lax.dot_general(former, latter, (((1,), (1,)), ((), ())), preferred_eleme...  30.2 us
    all_to_all x4, waiting for transfers between devices, combine(): back = lax.all_to_all(mine, 'dp', 0, 0, tiled=True)  23.2 us
    all_to_all x4, starting transfers between devices, combine(): back = lax.all_to_all(mine, 'dp', 0, 0, tiled=True)  22.7 us
    ppermute x29, starting transfers between devices, swap(): return lax.ppermute(values, axis, [(0, 1), (1, 0)])  22.4 us
    ppermute x8, waiting for transfers between devices, ring_scatter(): forward = lax.ppermute(forward, 'dp', right)  19.4 us
  transfers between devices with their start and end apart: 69, of which 24 were waited for; matrix products, arithmetic and copies ran while one was open for 33% of the time, Pallas kernels for 0%

profile of v1, /device:TPU:0, one launch (start us, length us, event | category | flops | bytes accessed | tf_op | source)
XLA Modules:
  0.0 643.1 jit_solution(2834329276619319892)
XLA Ops:
  14.0 6.3 constant_dynamic-slice_fusion.13
  23.0 6.0 collective-permute-start.10
  70.8 6.9 %collective-permute-done.2 = bf16[128,2176]{1,0:T(8,128)(2,1)} collective-permute-done((bf16[128,2176]{1,0:T(8,128)(2,1)}, bf16[128,2176]{1,0:T(8,128)(2,1)}, u32[]{:S(2)}, u32[]{:S(2)}) %collective-permute-start.2) | collective-permute-done | bytes 557088 | tf_op jit(solution)/shard_map/ppermute | solution.py:76
  85.1 5.4 collective-permute-done.4
  116.1 8.4 %convolution_convert_fusion.4.k_ref.v_ref = bf16[1024,1024]{1,0:T(8,128)(2,1)S(1)} fusion(bf16[1024,2048]{1,0:T(8,128)(2,1)} %bitcast.61, bf16[2048,1024]{1,0:T(8,128)(2,1)S(1)} %maximum_select_fusion), kind=kOutput, calls=%fused_computation.31 | convolution fusion | flops 4296015872 | bytes 10485760 | tf_op jit(solution)/shard_map/dot_general | solution.py:20
  130.2 7.2 %attend.2 = (bf16[320,512]{1,0:T(8,128)(2,1)S(1)}, f32[4,320,1]{2,1,0:T(8,128)S(1)}) custom-call(bf16[320,512]{1,0:T(8,128)(2,1)S(1)} %get-tuple-element.190.q_ref, bf16[1024,1024]{1,0:T(8,128)(2,1)S(1)} %convolution_convert_fusion.4.k_ref.v_ref, bf16[1024,1024]{1,0:T(8,128)(2,1)S(1)} %convolution_convert_fusion.4.k_ref.v_ref, ...), custom_call_target="tpu_custom_call" | custom-call | flops 671088640 | bytes 2752512 | tf_op jit(solution)/shard_map/attend/pallas_call | solution.py:160
  138.3 6.9 %convolution_convert_fusion.3.k_ref.v_ref = bf16[1024,1024]{1,0:T(8,128)(2,1)S(1)} fusion(bf16[1024,2048]{1,0:T(8,128)(2,1)} %collective-permute-done.9, bf16[2048,1024]{1,0:T(8,128)(2,1)S(1)} %maximum_select_fusion), kind=kOutput, calls=%fused_computation.30 | convolution fusion | flops 4296015872 | bytes 10485760 | tf_op jit(solution)/shard_map/dot_general | solution.py:20
  145.3 7.2 %attend.3 = (bf16[320,512]{1,0:T(8,128)(2,1)S(1)}, f32[4,320,1]{2,1,0:T(8,128)S(1)}) custom-call(bf16[320,512]{1,0:T(8,128)(2,1)S(1)} %get-tuple-element.189.q_ref, bf16[1024,1024]{1,0:T(8,128)(2,1)S(1)} %convolution_convert_fusion.3.k_ref.v_ref, bf16[1024,1024]{1,0:T(8,128)(2,1)S(1)} %convolution_convert_fusion.3.k_ref.v_ref, ...), custom_call_target="tpu_custom_call" | custom-call | flops 671088640 | bytes 2752512 | tf_op jit(solution)/shard_map/attend/pallas_call | solution.py:160
  167.3 15.4 %collective-permute-done.12 = bf16[320,1024]{1,0:T(8,128)(2,1)} collective-permute-done((bf16[320,1024]{1,0:T(8,128)(2,1)}, bf16[320,1024]{1,0:T(8,128)(2,1)}, u32[]{:S(2)}, u32[]{:S(2)}) %collective-permute-start.12) | collective-permute-done | bytes 655392 | tf_op jit(solution)/shard_map/ppermute | solution.py:36
  185.3 5.7 all-to-all-start
  195.4 12.7 %all-to-all-done = bf16[8,40,1024]{2,1,0:T(8,128)(2,1)} async-done(((bf16[8,40,1024]{2,1,0:T(8,128)(2,1)}), bf16[8,40,1024]{2,1,0:T(8,128)(2,1)}, u32[]{:S(2)}, u32[]{:S(2)}) %all-to-all-start) | async-done | bytes 655392 | tf_op jit(solution)/shard_map/all_to_all | solution.py:374
  246.1 13.9 %collective-permute-done.23 = bf16[320,1024]{1,0:T(8,128)(2,1)} collective-permute-done((bf16[320,1024]{1,0:T(8,128)(2,1)}, bf16[320,1024]{1,0:T(8,128)(2,1)}, u32[]{:S(2)}, u32[]{:S(2)}) %collective-permute-start.23) | collective-permute-done | bytes 655392 | tf_op jit(solution)/shard_map/ppermute | solution.py:36
  262.8 6.9 %collective-permute-done.14 = bf16[320,1024]{1,0:T(8,128)(2,1)} collective-permute-done((bf16[320,1024]{1,0:T(8,128)(2,1)}, bf16[320,1024]{1,0:T(8,128)(2,1)}, u32[]{:S(2)}, u32[]{:S(2)}) %collective-permute-start.14) | collective-permute-done | bytes 655392 | tf_op jit(solution)/shard_map/ppermute | solution.py:36
  278.2 9.7 %fusion.118 = f32[640,1408]{1,0:T(8,128)} fusion(bf16[640,2048]{1,0:T(8,128)(2,1)S(1)} %pad_maximum_fusion.4, bf16[2048,1408]{1,0:T(8,128)(2,1)} %param.34), kind=kOutput, calls=%fused_computation.386 | convolution fusion | flops 3690987520 | bytes 11993088 | tf_op jit(solution)/shard_map/dot_general | solution.py:20
  288.0 6.1 fusion.117
  294.9 9.7 %multiply_reduce_fusion = (f32[640]{0:T(1024)S(1)}, bf16[640,1408]{1,0:T(8,128)(2,1)}, bf16[640,1408]{1,0:T(8,128)(2,1)S(1)}, bf16[640,1408]{1,0:T(8,128)(2,1)}) fusion(f32[640,1408]{1,0:T(8,128)} %fusion.118, f32[640,1408]{1,0:T(8,128)} %fusion.117, f32[640]{0:T(1024)S(1)} %add_divide_fusion.1, bf16[640,2048]{1,0:T(8,128)(2,1)S(1)} %pad_maximum_fusion.5, ...), kind=kOutput, calls=%fused_computation.12 | convolution fusion | flops 3708108288 | bytes 21009408 | tf_op jit(solution)/shard_map/dot_general | solution.py:20
  318.5 16.3 %collective-permute-done.26 = bf16[320,1024]{1,0:T(8,128)(2,1)S(1)} collective-permute-done((bf16[320,1024]{1,0:T(8,128)(2,1)S(1)}, bf16[320,1024]{1,0:T(8,128)(2,1)S(1)}, u32[]{:S(2)}, u32[]{:S(2)}) %collective-permute-start.26) | collective-permute-done | bytes 655392 | tf_op jit(solution)/shard_map/ppermute | solution.py:36
  336.0 8.6 %all-to-all-start.2 = ((bf16[8,40,1024]{2,1,0:T(8,128)(2,1)}), bf16[8,40,1024]{2,1,0:T(8,128)(2,1)}, u32[]{:S(2)}, u32[]{:S(2)}) async-start(bf16[8,40,1024]{2,1,0:T(8,128)(2,1)} %bitcast.430), calls=%async_computation.2 | async-start | bytes 1310720 | tf_op jit(solution)/shard_map/all_to_all | solution.py:374
  369.8 6.4 %all-to-all-start.3 = ((bf16[8,40,1024]{2,1,0:T(8,128)(2,1)}), bf16[8,40,1024]{2,1,0:T(8,128)(2,1)}, u32[]{:S(2)}, u32[]{:S(2)}) async-start(bf16[8,40,1024]{2,1,0:T(8,128)(2,1)} %bitcast.428), calls=%async_computation.3 | async-start | bytes 1310720 | tf_op jit(solution)/shard_map/all_to_all | solution.py:363
  378.6 8.3 %multiply_convert_fusion.2 = bf16[640,2048]{1,0:T(8,128)(2,1)} fusion(bf16[640,1408]{1,0:T(8,128)(2,1)S(1)} %copy-done.106, bf16[2048,1408]{1,0:T(8,128)(2,1)} %param.35, f32[640]{0:T(1024)S(1)} %copy-done.93), kind=kOutput, calls=%fused_computation.3 | convolution fusion | flops 3693608960 | bytes 10193408 | tf_op jit(solution)/shard_map/dot_general | solution.py:24
  386.9 5.8 all-to-all-done.3
  394.1 11.8 %fusion.2 = f32[2048,1408]{1,0:T(8,128)} fusion(bf16[640,1408]{1,0:T(8,128)(2,1)} %get-tuple-element.37, f32[640]{0:T(1024)S(1)} %copy-done.93, bf16[320,2048]{1,0:T(8,128)(2,1)} %collective-permute-done.24, bf16[320,1024]{1,0:T(8,128)(2,1)} %copy-done.19, bf16[320,1024]{1,0:T(8,128)(2,1)} %copy-done.18), kind=kOutput, calls=%fused_computation.21 | convolution fusion | flops 3701473280 | bytes 15960576 | tf_op jit(solution)/shard_map/dot_general | solution.py:30
  408.9 7.8 %fusion.125 = f32[2048,1408]{1,0:T(8,128)} fusion(bf16[640,2048]{1,0:T(8,128)(2,1)S(1)} %copy-done.13, bf16[640,1408]{1,0:T(8,128)(2,1)S(1)} %copy-done.105), kind=kOutput, calls=%fused_computation.393 | convolution fusion | flops 3690987520 | bytes 15958016 | tf_op jit(solution)/shard_map/dot_general | solution.py:30
  416.6 7.9 %fusion.126 = f32[2048,1408]{1,0:T(8,128)} fusion(bf16[640,2048]{1,0:T(8,128)(2,1)S(1)} %copy-done.13, bf16[640,1408]{1,0:T(8,128)(2,1)S(1)} %copy-done.103), kind=kOutput, calls=%fused_computation.394 | convolution fusion | flops 3690987520 | bytes 15958016 | tf_op jit(solution)/shard_map/dot_general | solution.py:30
  426.3 9.2 %attend_back.2 = (bf16[320,512]{1,0:T(8,128)(2,1)S(1)}, bf16[1024,512]{1,0:T(8,128)(2,1)S(1)}, bf16[1024,512]{1,0:T(8,128)(2,1)S(1)}) custom-call(bf16[320,512]{1,0:T(8,128)(2,1)S(1)} %copy-done.6, bf16[1024,1024]{1,0:T(8,128)(2,1)} %copy-done.1, bf16[1024,1024]{1,0:T(8,128)(2,1)} %copy-done.1, bf16[320,1024]{1,0:T(8,128)(2,1)S(1)} %select_convert_fusion.1.bias_ref, ...), custom_call_target="tpu_custom_call" | custom-call | flops 1677721600 | bytes 4849664 | tf_op jit(solution)/shard_map/attend_back/pallas_call | solution.py:216
  435.6 9.3 %attend_back.3 = (bf16[320,512]{1,0:T(8,128)(2,1)S(1)}, bf16[1024,512]{1,0:T(8,128)(2,1)S(1)}, bf16[1024,512]{1,0:T(8,128)(2,1)S(1)}) custom-call(bf16[320,512]{1,0:T(8,128)(2,1)S(1)} %copy-done.4, bf16[1024,1024]{1,0:T(8,128)(2,1)} %copy-done.2, bf16[1024,1024]{1,0:T(8,128)(2,1)} %copy-done.2, bf16[320,1024]{1,0:T(8,128)(2,1)S(1)} %select_convert_fusion.bias_ref, ...), custom_call_target="tpu_custom_call" | custom-call | flops 1677721600 | bytes 4849664 | tf_op jit(solution)/shard_map/attend_back/pallas_call | solution.py:216
  462.3 5.9 add_convert_fusion.2
  472.8 6.0 add_convert_fusion.3
  492.0 8.4 %collective-permute-done.36 = bf16[512,512]{1,0:T(8,128)(2,1)} collective-permute-done((bf16[512,512]{1,0:T(8,128)(2,1)}, bf16[512,512]{1,0:T(8,128)(2,1)}, u32[]{:S(2)}, u32[]{:S(2)}) %collective-permute-start.36) | collective-permute-done | bytes 524320 | tf_op jit(solution)/shard_map/ppermute | solution.py:132
  537.2 8.2 %collective-permute-done.49 = bf16[256,512]{1,0:T(8,128)(2,1)S(1)} collective-permute-done((bf16[256,512]{1,0:T(8,128)(2,1)S(1)}, bf16[256,512]{1,0:T(8,128)(2,1)S(1)}, u32[]{:S(2)}, u32[]{:S(2)}) %collective-permute-start.49) | collective-permute-done | bytes 262176 | tf_op jit(solution)/shard_map/ppermute | solution.py:132
  572.2 10.4 %all-to-all-done.4 = bf16[8,40,1024]{2,1,0:T(8,128)(2,1)} async-done(((bf16[8,40,1024]{2,1,0:T(8,128)(2,1)}), bf16[8,40,1024]{2,1,0:T(8,128)(2,1)}, u32[]{:S(2)}, u32[]{:S(2)}) %all-to-all-start.4) | async-done | bytes 655392 | tf_op jit(solution)/shard_map/all_to_all | solution.py:374
  631.4 6.7 %collective-permute-done.58 = bf16[1,2,128,512]{3,2,1,0:T(8,128)(2,1)S(1)} collective-permute-done((bf16[1,2,128,512]{3,2,1,0:T(8,128)(2,1)S(1)}, bf16[1,2,128,512]{3,2,1,0:T(8,128)(2,1)S(1)}, u32[]{:S(2)}, u32[]{:S(2)}) %collective-permute-start.58) | collective-permute-done | bytes 262176 | tf_op jit(solution)/shard_map/ppermute | solution.py:36
  (577 shorter events, 322.7 us)
Async XLA Ops:
  10.9 52.6 %collective-permute-start = (bf16[128,2176]{1,0:T(8,128)(2,1)S(1)}, bf16[128,2176]{1,0:T(8,128)(2,1)}, u32[]{:S(2)}, u32[]{:S(2)}) collective-permute-start(bf16[128,2176]{1,0:T(8,128)(2,1)S(1)} %pad_maximum_fusion.10), channel_id=1, source_target_pairs={{0,8},{8,16},{16,24},{24,28},{28,20},{20,12},{12,4},{4,0},{1,9},{9... | collective-permute-start | bytes 1671176 | tf_op jit(solution)/shard_map/ppermute | solution.py:76
  14.0 50.2 %collective-permute-start.1 = (bf16[128,2176]{1,0:T(8,128)(2,1)S(1)}, bf16[128,2176]{1,0:T(8,128)(2,1)}, u32[]{:S(2)}, u32[]{:S(2)}) collective-permute-start(bf16[128,2176]{1,0:T(8,128)(2,1)S(1)} %pad_maximum_fusion.10), channel_id=1, source_target_pairs={{0,4},{8,0},{16,8},{24,16},{28,24},{20,28},{12,20},{4,12},{1,5},{9... | collective-permute-start | bytes 1671176 | tf_op jit(solution)/shard_map/ppermute | solution.py:77
  23.0 89.3 %collective-permute-start.10 = (bf16[2048,1024]{1,0:T(8,128)(2,1)}, bf16[2048,1024]{1,0:T(8,128)(2,1)}, u32[]{:S(2)}, u32[]{:S(2)}) collective-permute-start(bf16[2048,1024]{1,0:T(8,128)(2,1)} %pad_maximum_fusion), channel_id=1, source_target_pairs={{0,1},{3,2},{4,5},{7,6},{8,9},{11,10},{12,13},{15,14},{16,17},{19,... | collective-permute-start | bytes 12582920 | tf_op jit(solution)/shard_map/ppermute | solution.py:407
  102.2 22.3 %collective-permute-start.9 = (bf16[1024,2048]{1,0:T(8,128)(2,1)}, bf16[1024,2048]{1,0:T(8,128)(2,1)}, u32[]{:S(2)}, u32[]{:S(2)}) collective-permute-start(bf16[1024,2048]{1,0:T(8,128)(2,1)} %bitcast.61), channel_id=1, source_target_pairs={{0,2},{2,0},{1,3},{3,1},{4,6},{6,4},{5,7},{7,5},{8,10},{10,8},{9,1... | collective-permute-start | bytes 12582920 | tf_op jit(solution)/shard_map/ppermute | solution.py:36
  162.3 20.4 %collective-permute-start.12 = (bf16[320,1024]{1,0:T(8,128)(2,1)}, bf16[320,1024]{1,0:T(8,128)(2,1)}, u32[]{:S(2)}, u32[]{:S(2)}) collective-permute-start(bf16[320,1024]{1,0:T(8,128)(2,1)} %add_convert_fusion.11), channel_id=1, source_target_pairs={{0,1},{1,0},{2,3},{3,2},{4,5},{5,4},{6,7},{7,6},{8,9},{9,8},{10,11... | collective-permute-start | bytes 1966088 | tf_op jit(solution)/shard_map/ppermute | solution.py:36
  185.3 22.9 %all-to-all-start = ((bf16[8,40,1024]{2,1,0:T(8,128)(2,1)}), bf16[8,40,1024]{2,1,0:T(8,128)(2,1)}, u32[]{:S(2)}, u32[]{:S(2)}) async-start(bf16[8,40,1024]{2,1,0:T(8,128)(2,1)} %bitcast.429), calls=%async_computation | async-start | bytes 1310720 | tf_op jit(solution)/shard_map/all_to_all | solution.py:374
  193.4 18.2 %collective-permute-start.16 = (bf16[1,40,1024]{2,1,0:T(8,128)(2,1)S(1)}, bf16[1,40,1024]{2,1,0:T(8,128)(2,1)}, u32[]{:S(2)}, u32[]{:S(2)}) collective-permute-start(bf16[1,40,1024]{2,1,0:T(8,128)(2,1)S(1)} %constant_dynamic-slice_fusion.10), channel_id=1, source_target_pairs={{0,4},{4,8},{8,12},{12,16},{16,20},{20,24},{24,28},{28,0},{1,5},{5... | collective-permute-start | bytes 245768 | tf_op jit(solution)/shard_map/ppermute | solution.py:93
  215.8 19.4 %collective-permute-start.18 = (bf16[1,40,1024]{2,1,0:T(8,128)(2,1)}, bf16[1,40,1024]{2,1,0:T(8,128)(2,1)}, u32[]{:S(2)}, u32[]{:S(2)}) collective-permute-start(bf16[1,40,1024]{2,1,0:T(8,128)(2,1)} %get-tuple-element.186), channel_id=1, source_target_pairs={{0,12},{4,16},{8,20},{12,24},{16,28},{20,0},{24,4},{28,8},{1,13},{... | collective-permute-start | bytes 245768 | tf_op jit(solution)/shard_map/ppermute | solution.py:93
  216.2 20.5 %collective-permute-start.19 = (bf16[1,40,1024]{2,1,0:T(8,128)(2,1)}, bf16[1,40,1024]{2,1,0:T(8,128)(2,1)}, u32[]{:S(2)}, u32[]{:S(2)}) collective-permute-start(bf16[1,40,1024]{2,1,0:T(8,128)(2,1)} %get-tuple-element.185), channel_id=1, source_target_pairs={{0,16},{4,20},{8,24},{12,28},{16,0},{20,4},{24,8},{28,12},{1,17},{... | collective-permute-start | bytes 245768 | tf_op jit(solution)/shard_map/ppermute | solution.py:93
  220.5 19.3 %collective-permute-start.21 = (bf16[1,40,1024]{2,1,0:T(8,128)(2,1)}, bf16[1,40,1024]{2,1,0:T(8,128)(2,1)}, u32[]{:S(2)}, u32[]{:S(2)}) collective-permute-start(bf16[1,40,1024]{2,1,0:T(8,128)(2,1)} %get-tuple-element.183), channel_id=1, source_target_pairs={{0,24},{4,28},{8,0},{12,4},{16,8},{20,12},{24,16},{28,20},{1,25},{... | collective-permute-start | bytes 245768 | tf_op jit(solution)/shard_map/ppermute | solution.py:93
  224.8 20.8 %all-to-all-start.1 = ((bf16[8,40,1024]{2,1,0:T(8,128)(2,1)}), bf16[8,40,1024]{2,1,0:T(8,128)(2,1)}, u32[]{:S(2)}, u32[]{:S(2)}) async-start(bf16[8,40,1024]{2,1,0:T(8,128)(2,1)} %bitcast.427), calls=%async_computation.1 | async-start | bytes 1310720 | tf_op jit(solution)/shard_map/all_to_all | solution.py:363
  242.0 18.0 %collective-permute-start.23 = (bf16[320,1024]{1,0:T(8,128)(2,1)}, bf16[320,1024]{1,0:T(8,128)(2,1)}, u32[]{:S(2)}, u32[]{:S(2)}) collective-permute-start(bf16[320,1024]{1,0:T(8,128)(2,1)} %bitcast.418), channel_id=1, source_target_pairs={{0,1},{1,0},{2,3},{3,2},{4,5},{5,4},{6,7},{7,6},{8,9},{9,8},{10,11... | collective-permute-start | bytes 1966088 | tf_op jit(solution)/shard_map/ppermute | solution.py:36
  245.6 24.1 %collective-permute-start.14 = (bf16[320,1024]{1,0:T(8,128)(2,1)}, bf16[320,1024]{1,0:T(8,128)(2,1)}, u32[]{:S(2)}, u32[]{:S(2)}) collective-permute-start(bf16[320,1024]{1,0:T(8,128)(2,1)} %bitcast.81), channel_id=1, source_target_pairs={{0,1},{1,0},{2,3},{3,2},{4,5},{5,4},{6,7},{7,6},{8,9},{9,8},{10,11... | collective-permute-start | bytes 1966088 | tf_op jit(solution)/shard_map/ppermute | solution.py:36
  336.0 26.1 %all-to-all-start.2 = ((bf16[8,40,1024]{2,1,0:T(8,128)(2,1)}), bf16[8,40,1024]{2,1,0:T(8,128)(2,1)}, u32[]{:S(2)}, u32[]{:S(2)}) async-start(bf16[8,40,1024]{2,1,0:T(8,128)(2,1)} %bitcast.430), calls=%async_computation.2 | async-start | bytes 1310720 | tf_op jit(solution)/shard_map/all_to_all | solution.py:374
  369.8 22.9 %all-to-all-start.3 = ((bf16[8,40,1024]{2,1,0:T(8,128)(2,1)}), bf16[8,40,1024]{2,1,0:T(8,128)(2,1)}, u32[]{:S(2)}, u32[]{:S(2)}) async-start(bf16[8,40,1024]{2,1,0:T(8,128)(2,1)} %bitcast.428), calls=%async_computation.3 | async-start | bytes 1310720 | tf_op jit(solution)/shard_map/all_to_all | solution.py:363
  453.6 72.1 %collective-permute-start.30 = (bf16[320,2048]{1,0:T(8,128)(2,1)}, bf16[320,2048]{1,0:T(8,128)(2,1)}, u32[]{:S(2)}, u32[]{:S(2)}) collective-permute-start(bf16[320,2048]{1,0:T(8,128)(2,1)} %get-tuple-element.159), channel_id=1, source_target_pairs={{0,2},{2,0},{1,3},{3,1},{4,6},{6,4},{5,7},{7,5},{8,10},{10,8},{9,1... | collective-permute-start | bytes 3932168 | tf_op jit(solution)/shard_map/ppermute | solution.py:36
  455.4 28.7 %collective-permute-start.35 = (bf16[256,512]{1,0:T(8,128)(2,1)S(1)}, bf16[256,512]{1,0:T(8,128)(2,1)S(1)}, u32[]{:S(2)}, u32[]{:S(2)}) collective-permute-start(bf16[256,512]{1,0:T(8,128)(2,1)S(1)} %get-tuple-element.148), channel_id=1, source_target_pairs={{0,8},{8,16},{16,24},{24,28},{28,20},{20,12},{12,4},{4,0},{1,9},{9... | collective-permute-start | bytes 786440 | tf_op jit(solution)/shard_map/ppermute | solution.py:132
  455.4 28.7 %collective-permute-start.39 = (bf16[256,512]{1,0:T(8,128)(2,1)S(1)}, bf16[256,512]{1,0:T(8,128)(2,1)S(1)}, u32[]{:S(2)}, u32[]{:S(2)}) collective-permute-start(bf16[256,512]{1,0:T(8,128)(2,1)S(1)} %get-tuple-element.150), channel_id=1, source_target_pairs={{0,4},{8,0},{16,8},{24,16},{28,24},{20,28},{12,20},{4,12},{1,5},{9... | collective-permute-start | bytes 786440 | tf_op jit(solution)/shard_map/ppermute | solution.py:133
  457.7 72.8 %collective-permute-start.33 = (bf16[320,2048]{1,0:T(8,128)(2,1)}, bf16[320,2048]{1,0:T(8,128)(2,1)}, u32[]{:S(2)}, u32[]{:S(2)}) collective-permute-start(bf16[320,2048]{1,0:T(8,128)(2,1)} %get-tuple-element.157), channel_id=1, source_target_pairs={{0,2},{2,0},{1,3},{3,1},{4,6},{6,4},{5,7},{7,5},{8,10},{10,8},{9,1... | collective-permute-start | bytes 3932168 | tf_op jit(solution)/shard_map/ppermute | solution.py:36
  487.7 20.1 %collective-permute-start.60 = (f32[8,16,128]{2,1,0:T(8,128)S(1)}, f32[8,16,128]{2,1,0:T(8,128)S(1)}, u32[]{:S(2)}, u32[]{:S(2)}) collective-permute-start(f32[8,16,128]{2,1,0:T(8,128)S(1)} %bitcast.441), channel_id=1, source_target_pairs={{0,2},{2,0},{1,3},{3,1},{4,6},{6,4},{5,7},{7,5},{8,10},{10,8},{9,1... | collective-permute-start | bytes 196616 | tf_op jit(solution)/shard_map/ppermute | solution.py:36
  490.0 23.8 %collective-permute-start.40 = (bf16[512,512]{1,0:T(8,128)(2,1)}, bf16[512,512]{1,0:T(8,128)(2,1)}, u32[]{:S(2)}, u32[]{:S(2)}) collective-permute-start(bf16[512,512]{1,0:T(8,128)(2,1)} %pad_maximum_fusion.12), channel_id=1, source_target_pairs={{0,4},{8,0},{16,8},{24,16},{28,24},{20,28},{12,20},{4,12},{1,5},{9... | collective-permute-start | bytes 1572872 | tf_op jit(solution)/shard_map/ppermute | solution.py:133
  527.2 23.1 %collective-permute-start.31 = (bf16[320,1024]{1,0:T(8,128)(2,1)S(1)}, bf16[320,1024]{1,0:T(8,128)(2,1)S(1)}, u32[]{:S(2)}, u32[]{:S(2)}) collective-permute-start(bf16[320,1024]{1,0:T(8,128)(2,1)S(1)} %add_convert_fusion.7), channel_id=1, source_target_pairs={{0,1},{1,0},{2,3},{3,2},{4,5},{5,4},{6,7},{7,6},{8,9},{9,8},{10,11... | collective-permute-start | bytes 1966088 | tf_op jit(solution)/shard_map/ppermute | solution.py:36
  528.2 29.4 %collective-permute-start.38 = (bf16[512,512]{1,0:T(8,128)(2,1)}, bf16[512,512]{1,0:T(8,128)(2,1)}, u32[]{:S(2)}, u32[]{:S(2)}) collective-permute-start(bf16[512,512]{1,0:T(8,128)(2,1)} %get-tuple-element.144), channel_id=1, source_target_pairs={{0,8},{8,16},{16,24},{24,28},{28,20},{20,12},{12,4},{4,0},{1,9},{9... | collective-permute-start | bytes 1572872 | tf_op jit(solution)/shard_map/ppermute | solution.py:132
  534.0 33.3 %collective-permute-start.34 = (bf16[320,1024]{1,0:T(8,128)(2,1)}, bf16[320,1024]{1,0:T(8,128)(2,1)}, u32[]{:S(2)}, u32[]{:S(2)}) collective-permute-start(bf16[320,1024]{1,0:T(8,128)(2,1)} %add_convert_fusion.5), channel_id=1, source_target_pairs={{0,1},{1,0},{2,3},{3,2},{4,5},{5,4},{6,7},{7,6},{8,9},{9,8},{10,11... | collective-permute-start | bytes 1966088 | tf_op jit(solution)/shard_map/ppermute | solution.py:36
  548.2 21.7 %collective-permute-start.50 = (bf16[512,512]{1,0:T(8,128)(2,1)}, bf16[512,512]{1,0:T(8,128)(2,1)}, u32[]{:S(2)}, u32[]{:S(2)}) collective-permute-start(bf16[512,512]{1,0:T(8,128)(2,1)} %pad_maximum_fusion.13), channel_id=1, source_target_pairs={{0,8},{8,16},{16,24},{24,28},{28,20},{20,12},{12,4},{4,0},{1,9},{9... | collective-permute-start | bytes 1572872 | tf_op jit(solution)/shard_map/ppermute | solution.py:132
  550.3 43.3 %collective-permute-start.54 = (bf16[512,512]{1,0:T(8,128)(2,1)}, bf16[512,512]{1,0:T(8,128)(2,1)}, u32[]{:S(2)}, u32[]{:S(2)}) collective-permute-start(bf16[512,512]{1,0:T(8,128)(2,1)} %pad_maximum_fusion.14), channel_id=1, source_target_pairs={{0,4},{8,0},{16,8},{24,16},{28,24},{20,28},{12,20},{4,12},{1,5},{9... | collective-permute-start | bytes 1572872 | tf_op jit(solution)/shard_map/ppermute | solution.py:133
  553.3 29.3 %all-to-all-start.4 = ((bf16[8,40,1024]{2,1,0:T(8,128)(2,1)}), bf16[8,40,1024]{2,1,0:T(8,128)(2,1)}, u32[]{:S(2)}, u32[]{:S(2)}) async-start(bf16[8,40,1024]{2,1,0:T(8,128)(2,1)} %bitcast.432), calls=%async_computation.4 | async-start | bytes 1310720 | tf_op jit(solution)/shard_map/all_to_all | solution.py:374
  567.4 20.7 %collective-permute-start.43 = (bf16[128,2048]{1,0:T(8,128)(2,1)}, bf16[128,2048]{1,0:T(8,128)(2,1)}, u32[]{:S(2)}, u32[]{:S(2)}) collective-permute-start(bf16[128,2048]{1,0:T(8,128)(2,1)} %convolution_convert_fusion.2), channel_id=1, source_target_pairs={{0,2},{2,0},{1,3},{3,1},{4,6},{6,4},{5,7},{7,5},{8,10},{10,8},{9,1... | collective-permute-start | bytes 1572872 | tf_op jit(solution)/shard_map/ppermute | solution.py:36
  571.2 22.5 %collective-permute-start.51 = (bf16[512,512]{1,0:T(8,128)(2,1)S(1)}, bf16[512,512]{1,0:T(8,128)(2,1)}, u32[]{:S(2)}, u32[]{:S(2)}) collective-permute-start(bf16[512,512]{1,0:T(8,128)(2,1)S(1)} %fusion.12), channel_id=1, source_target_pairs={{0,8},{8,16},{16,24},{24,28},{28,20},{20,12},{12,4},{4,0},{1,9},{9... | collective-permute-start | bytes 1572872 | tf_op jit(solution)/shard_map/ppermute | solution.py:132
  582.6 18.8 %all-to-all-start.5 = ((bf16[8,40,1024]{2,1,0:T(8,128)(2,1)}), bf16[8,40,1024]{2,1,0:T(8,128)(2,1)}, u32[]{:S(2)}, u32[]{:S(2)}) async-start(bf16[8,40,1024]{2,1,0:T(8,128)(2,1)} %bitcast.431), calls=%async_computation.5 | async-start | bytes 1310720 | tf_op jit(solution)/shard_map/all_to_all | solution.py:374
  598.3 27.3 %collective-permute-start.52 = (bf16[512,512]{1,0:T(8,128)(2,1)}, bf16[512,512]{1,0:T(8,128)(2,1)}, u32[]{:S(2)}, u32[]{:S(2)}) collective-permute-start(bf16[512,512]{1,0:T(8,128)(2,1)} %get-tuple-element.136), channel_id=1, source_target_pairs={{0,8},{8,16},{16,24},{24,28},{28,20},{20,12},{12,4},{4,0},{1,9},{9... | collective-permute-start | bytes 1572872 | tf_op jit(solution)/shard_map/ppermute | solution.py:132
  600.1 27.2 %collective-permute-start.32 = (bf16[128,1024]{1,0:T(8,128)(2,1)S(1)}, bf16[128,1024]{1,0:T(8,128)(2,1)}, u32[]{:S(2)}, u32[]{:S(2)}) collective-permute-start(bf16[128,1024]{1,0:T(8,128)(2,1)S(1)} %fusion.7), channel_id=1, source_target_pairs={{0,1},{1,0},{2,3},{3,2},{4,5},{5,4},{6,7},{7,6},{8,9},{9,8},{10,11... | collective-permute-start | bytes 786440 | tf_op jit(solution)/shard_map/ppermute | solution.py:36
  (150 other events, 1840.2 us)

commit v2 on v1

v2 whole, which is shorter than its diff:
```python
import functools

import jax
import jax.numpy as jnp
from jax import lax
from jax.experimental import pallas as pl
from jax.experimental.pallas import tpu as pltpu
from jax.sharding import PartitionSpec as P

HEAD = 128

epsilon = 1e-06
negative = -1e30
scale = HEAD ** (-0.5)
bf16 = jnp.bfloat16
f32 = jnp.float32


def product(former, latter):
    return jnp.dot(former, latter, preferred_element_type=f32)


def product_last(former, latter):
    return lax.dot_general(
        former, latter, (((1,), (1,)), ((), ())), preferred_element_type=f32
    )


def product_first(former, latter):
    return lax.dot_general(
        former, latter, (((0,), (0,)), ((), ())), preferred_element_type=f32
    )


def limit_of(rows):
    return min(56, max(40, rows * 24 // 640)) * 2**20


def swap(values, axis):
    return lax.ppermute(values, axis, [(0, 1), (1, 0)])


def pair_all_to_all(parts, axis):
    me = lax.axis_index(axis)
    mine = lax.dynamic_index_in_dim(parts, me, 0, keepdims=False)
    theirs = lax.dynamic_index_in_dim(parts, 1 - me, 0, keepdims=False)
    got = swap(theirs, axis)
    first = me == 0
    return jnp.stack([jnp.where(first, mine, got), jnp.where(first, got, mine)])


def ring_order(count):
    return list(range(0, count, 2)) + list(range(1, count, 2))[::-1]


def ring_member(place, count):
    place = lax.rem(place + 2 * count, count)
    return jnp.where(place < count // 2, 2 * place, 2 * (count - place) - 1)


def ring_place(member, count):
    return jnp.where(member % 2 == 0, member // 2, count - (member + 1) // 2)


def empty(shape, dtype):
    return pl.pallas_call(
        lambda ref: None,
        out_shape=jax.ShapeDtypeStruct(shape, dtype),
        out_specs=pl.BlockSpec(memory_space=pl.ANY),
        name="empty",
    )()


def ring_gather(block, axis, count, stride):
    order = ring_order(count)
    member = lax.axis_index(axis) // stride
    place = ring_place(member, count)
    right, left = ring_moves(order, 1, stride), ring_moves(order, -1, stride)
    rows, columns = block.shape
    half = rows // 2
    out = empty((count, rows, columns), block.dtype)

    def put(out, piece, source, row):
        return lax.dynamic_update_slice(out, piece[None], (source, row, 0))

    out = put(out, block, member, 0)
    forward, backward = block, block
    arrivals = []
    for step in range(1, count // 2 + 1):
        last = step == count // 2
        if last:
            forward, backward = forward[:half], backward[half:]
        forward = lax.ppermute(forward, axis, right)
        backward = lax.ppermute(backward, axis, left)
        arrivals.append(forward)
        out = put(out, forward, ring_member(place - step, count), 0)
        out = put(out, backward, ring_member(place + step, count), half if last else 0)
    return out, arrivals


def ring_moves(order, by, stride):
    count = len(order)
    return [
        (order[i] * stride + j, order[(i + by) % count] * stride + j)
        for i in range(count)
        for j in range(stride)
    ]


def after(values, *events):
    if events[0] is None:
        return values
    return lax.optimization_barrier((values,) + events)[0]


def ring_scatter(parts, count, stride):
    order = ring_order(count)
    place = ring_place(lax.axis_index("dp") // stride, count)
    right, left = ring_moves(order, 1, stride), ring_moves(order, -1, stride)
    far = count // 2

    def part(tree, offset):
        return lax.dynamic_index_in_dim(parts[tree], ring_member(place + offset, count), 0, keepdims=False)

    def added(sent, tree, offset):
        return (part(tree, offset).astype(f32) + sent.astype(f32)).astype(bf16)

    forward, backward = [part(0, far)], [part(1, -far)]
    first = None
    for step in range(far):
        forward = [lax.ppermute(v, "dp", right) for v in forward]
        backward = [lax.ppermute(v, "dp", left) for v in backward]
        first = forward[0] if first is None else first
        offset = far - 1 - step
        if step == 0:
            forward.append(part(1, offset))
            backward.insert(0, part(0, -offset))
            if offset:
                forward[0] = added(forward[0], 0, offset)
                backward[1] = added(backward[1], 1, -offset)
        elif offset:
            forward = [added(forward[t], t, offset) for t in range(2)]
            backward = [added(backward[t], t, -offset) for t in range(2)]
    total = [part(t, 0).astype(f32) + forward[t].astype(f32) + backward[t].astype(f32) for t in range(2)]
    return jnp.stack(total), first


def attend_body(tiles, keys_per_tile, q_ref, k_ref, v_ref, bias_ref, gate_ref, out_ref, total_ref):
    rows = q_ref.shape[0] // tiles
    for tile in range(tiles):
        here = pl.ds(tile * rows, rows)
        keys = (tile + 1) * keys_per_tile
        scores = product_last(q_ref[here, :], k_ref[:keys, :]) * scale
        scores = scores + bias_ref[here, :keys].astype(f32)
        highest = jnp.max(scores, axis=1, keepdims=True)
        expo = jnp.exp(scores - highest)
        summed = jnp.sum(expo, axis=1, keepdims=True)
        probs = (expo * (1.0 / summed)).astype(bf16)
        mixed = product(probs, v_ref[:keys, :]).astype(bf16).astype(f32)
        out_ref[here, :] = (mixed * gate_ref[here, :]).astype(bf16)
        total_ref[0, here, :] = highest + jnp.log(summed)


def attend(queries, shared, bias, gate, tiles):
    rows, columns = queries.shape[0] // 2, queries.shape[1]
    length = shared.shape[0] // 2
    heads = columns // HEAD
    return pl.pallas_call(
        functools.partial(attend_body, tiles, length // tiles),
        grid=(2, heads),
        in_specs=[
            pl.BlockSpec((rows, HEAD), lambda t, h: (t, h)),
            pl.BlockSpec((length, HEAD), lambda t, h: (t, 2 * h)),
            pl.BlockSpec((length, HEAD), lambda t, h: (t, 2 * h + 1)),
            pl.BlockSpec((rows, length), lambda t, h: (t, 0)),
            pl.BlockSpec((rows, 1), lambda t, h: (t, 0)),
        ],
        out_specs=[
            pl.BlockSpec((rows, HEAD), lambda t, h: (t, h)),
            pl.BlockSpec((1, rows, 1), lambda t, h: (t * heads + h, 0, 0)),
        ],
        out_shape=[
            jax.ShapeDtypeStruct((2 * rows, columns), bf16),
            jax.ShapeDtypeStruct((2 * heads, rows, 1), f32),
        ],
        compiler_params=pltpu.CompilerParams(vmem_limit_bytes=limit_of(2 * rows)),
        cost_estimate=pl.CostEstimate(
            flops=8 * rows * length * columns,
            bytes_accessed=4 * (rows * length + 2 * length * columns),
            transcendentals=2 * rows * length * heads,
        ),
        name="attend",
    )(queries, shared, shared, bias, gate)


def attend_back_body(
    tiles, keys_per_tile, q_ref, k_ref, v_ref, bias_ref, total_ref, grad_ref, dq_ref, both_ref, dk_sum, dv_sum
):
    rows = q_ref.shape[0] // tiles
    dk_sum[...] = jnp.zeros_like(dk_sum)
    dv_sum[...] = jnp.zeros_like(dv_sum)
    for tile in range(tiles):
        here = pl.ds(tile * rows, rows)
        keys = (tile + 1) * keys_per_tile
        query, grad = q_ref[here, :], grad_ref[here, :]
        scores = product_last(query, k_ref[:keys, :]) * scale
        scores = scores + bias_ref[here, :keys].astype(f32)
        probs = jnp.exp(scores - total_ref[0, here, :])
        prob_grad = product_last(grad, v_ref[:keys, :])
        inner = jnp.sum(probs * prob_grad, axis=1, keepdims=True)
        score_grad = (probs * (prob_grad - inner) * scale).astype(bf16)
        dq_ref[here, :] = product(score_grad, k_ref[:keys, :]).astype(bf16)
        dk_sum[:keys, :] += product_first(score_grad, query)
        dv_sum[:keys, :] += product_first(probs.astype(bf16), grad)
    both_ref[0, :, :HEAD] = dk_sum[...].astype(bf16)
    both_ref[0, :, HEAD:] = dv_sum[...].astype(bf16)


def attend_back(queries, shared, bias, total, grads, tiles):
    rows, columns = queries.shape[0] // 2, queries.shape[1]
    length = shared.shape[0] // 2
    heads = columns // HEAD
    row_spec = pl.BlockSpec((rows, HEAD), lambda t, h: (t, h))
    return pl.pallas_call(
        functools.partial(attend_back_body, tiles, length // tiles),
        grid=(2, heads),
        in_specs=[
            row_spec,
            pl.BlockSpec((length, HEAD), lambda t, h: (t, 2 * h)),
            pl.BlockSpec((length, HEAD), lambda t, h: (t, 2 * h + 1)),
            pl.BlockSpec((rows, length), lambda t, h: (t, 0)),
            pl.BlockSpec((1, rows, 1), lambda t, h: (t * heads + h, 0, 0)),
            row_spec,
        ],
        out_specs=[row_spec, pl.BlockSpec((1, length, 2 * HEAD), lambda t, h: (t, 0, h))],
        out_shape=[
            jax.ShapeDtypeStruct((2 * rows, columns), bf16),
            jax.ShapeDtypeStruct((2, length, 2 * columns), bf16),
        ],
        scratch_shapes=[pltpu.VMEM((length, HEAD), f32), pltpu.VMEM((length, HEAD), f32)],
        compiler_params=pltpu.CompilerParams(vmem_limit_bytes=limit_of(2 * rows)),
        cost_estimate=pl.CostEstimate(
            flops=20 * rows * length * columns,
            bytes_accessed=4 * (rows * length + 4 * length * columns),
            transcendentals=2 * rows * length * heads,
        ),
        name="attend_back",
    )(queries, shared, shared, bias, total, grads)


def chunk_of(rows):
    return 640 if rows % 640 == 0 else rows


def assemble(shard, pieces, out_ref, sems):
    rows, half = pieces[0].shape
    copies = []
    for i, piece in enumerate(pieces):
        at = pl.multiple_of((shard if i % 2 == 0 else 1 - shard) * half, 128)
        place = out_ref.at[pl.ds(i // 2 * rows, rows), pl.ds(at, half)]
        copies.append(pltpu.make_async_copy(piece, place, sems.at[i]))
    for copy in copies:
        copy.start()
    for copy in copies:
        copy.wait()


def plain_in_body(shard_ref, p0, p1, p2, p3, w_ref, x_ref, y_ref, sems):
    @pl.when(pl.program_id(0) == 0)
    def _():
        assemble(shard_ref[0], (p0, p1, p2, p3), x_ref, sems)

    chunk = chunk_of(x_ref.shape[0])

    @pl.loop(0, x_ref.shape[0] // chunk)
    def _(i):
        here = pl.ds(pl.multiple_of(i * chunk, 16), chunk)
        y_ref[here, :] = product(x_ref[here, :], w_ref[...])


def plain_in(shard, pieces, weight, tile=512):
    rows, half = pieces[0].shape
    columns = weight.shape[1]
    return pl.pallas_call(
        plain_in_body,
        grid_spec=pltpu.PrefetchScalarGridSpec(
            num_scalar_prefetch=1,
            grid=(pl.cdiv(columns, tile),),
            in_specs=[pl.BlockSpec(memory_space=pl.ANY)] * 4
            + [pl.BlockSpec((2 * half, tile), lambda j, s: (0, j))],
            out_specs=[
                pl.BlockSpec((2 * rows, 2 * half), lambda j, s: (0, 0)),
                pl.BlockSpec((2 * rows, tile), lambda j, s: (0, j)),
            ],
            scratch_shapes=[pltpu.SemaphoreType.DMA((4,))],
        ),
        out_shape=[
            jax.ShapeDtypeStruct((2 * rows, 2 * half), bf16),
            jax.ShapeDtypeStruct((2 * rows, columns), f32),
        ],
        compiler_params=pltpu.CompilerParams(vmem_limit_bytes=limit_of(2 * rows)),
        cost_estimate=pl.CostEstimate(
            flops=8 * rows * half * columns,
            bytes_accessed=16 * rows * half + 4 * half * columns + 8 * rows * columns,
            transcendentals=0,
        ),
        name="plain_in",
    )(shard, *pieces, weight)


def expert_begin_body(shard_ref, p0, p2, gw_ref, uw_ref, gate_ref, up_ref, x_ref, sems):
    rows = p0.shape[0]

    @pl.when(pl.program_id(0) == 0)
    def _():
        copies = [
            pltpu.make_async_copy(p, x_ref.at[pl.ds(i * rows, rows), :], sems.at[i])
            for i, p in enumerate((p0, p2))
        ]
        for copy in copies:
            copy.start()
        for copy in copies:
            copy.wait()

    chunk = chunk_of(x_ref.shape[0])

    @pl.loop(0, x_ref.shape[0] // chunk)
    def _(i):
        here = pl.ds(pl.multiple_of(i * chunk, 16), chunk)
        gate_ref[here, :] = product(x_ref[here, :], gw_ref[...])
        up_ref[here, :] = product(x_ref[here, :], uw_ref[...])


def expert_begin(shard, own, other, gate_weight, up_weight, tile=512):
    rows, half = own.shape
    columns = gate_weight.shape[1]
    weight_spec = pl.BlockSpec((half, tile), lambda j, s: (s[0], j))
    tile_spec = pl.BlockSpec((2 * rows, tile), lambda j, s: (0, j))
    return pl.pallas_call(
        expert_begin_body,
        grid_spec=pltpu.PrefetchScalarGridSpec(
            num_scalar_prefetch=1,
            grid=(pl.cdiv(columns, tile),),
            in_specs=[pl.BlockSpec(memory_space=pl.ANY)] * 2 + [weight_spec, weight_spec],
            out_specs=[tile_spec, tile_spec],
            scratch_shapes=[
                pltpu.VMEM((2 * rows, half), bf16),
                pltpu.SemaphoreType.DMA((2,)),
            ],
        ),
        out_shape=[jax.ShapeDtypeStruct((2 * rows, columns), f32)] * 2,
        compiler_params=pltpu.CompilerParams(vmem_limit_bytes=limit_of(2 * rows)),
        cost_estimate=pl.CostEstimate(
            flops=8 * rows * half * columns,
            bytes_accessed=8 * rows * half + 4 * half * columns + 16 * rows * columns,
            transcendentals=0,
        ),
        name="expert_begin",
    )(shard, own, other, gate_weight, up_weight)


def expert_in_body(
    columns, shard_ref, p0, p1, p2, p3, router_ref, diff_ref, plain_ref, gp_ref, up_ref, gw_ref, uw_ref,
    x_ref, gate_ref, total_ref, hidden_ref, dgate_ref, dup_ref, their_ref, sems,
):
    tile = gw_ref.shape[1]
    rows = p0.shape[0]
    step = pl.program_id(0)

    @pl.when(step == 0)
    def _():
        copies = [
            pltpu.make_async_copy(p, their_ref.at[pl.ds(i * rows, rows), :], sems.at[4 + i])
            for i, p in enumerate((p1, p3))
        ]
        for copy in copies:
            copy.start()
        assemble(shard_ref[0], (p0, p1, p2, p3), x_ref, sems)
        for copy in copies:
            copy.wait()
        logits = product(x_ref[...], router_ref[...])
        gate_ref[...] = jax.nn.sigmoid(jnp.sum(logits * diff_ref[...], axis=1, keepdims=True))
        total_ref[...] = jnp.zeros_like(total_ref)

    chunk = chunk_of(x_ref.shape[0])

    @pl.loop(0, x_ref.shape[0] // chunk)
    def _(i):
        here = pl.ds(pl.multiple_of(i * chunk, 16), chunk)
        their = their_ref[here, :]
        gate_pre = gp_ref[here, :] + product(their, gw_ref[...])
        up_pre = up_ref[here, :] + product(their, uw_ref[...])
        plain, gate = plain_ref[here, :], gate_ref[here, :]
        inside = lax.broadcasted_iota(jnp.int32, (1, tile), 1) + step * tile < columns
        sigmoid = jax.nn.sigmoid(gate_pre)
        silu = gate_pre * sigmoid
        hidden = (silu * up_pre).astype(bf16).astype(f32)
        gated = (gate * hidden).astype(bf16)
        hidden_ref[here, :] = gated
        total_ref[here, :] += jnp.sum(
            jnp.where(inside, gated.astype(f32) * plain, 0.0), axis=1, keepdims=True
        )
        hidden_grad = gate * plain
        up_grad = hidden_grad * silu
        dup_ref[here, :] = up_grad.astype(bf16)
        gate_grad = hidden_grad * up_pre * (sigmoid + silu * (1.0 - sigmoid))
        dgate_ref[here, :] = gate_grad.astype(bf16)


def expert_in(shard, pieces, router, difference, plain, begun, gate_weight, up_weight, tile=256):
    rows, half = pieces[0].shape
    columns = gate_weight.shape[1]
    weight_spec = pl.BlockSpec((half, tile), lambda j, s: (1 - s[0], j))
    tile_spec = pl.BlockSpec((2 * rows, tile), lambda j, s: (0, j))
    held_spec = pl.BlockSpec((2 * rows, 1), lambda j, s: (0, 0))
    hidden_shape = jax.ShapeDtypeStruct((2 * rows, columns), bf16)
    return pl.pallas_call(
        functools.partial(expert_in_body, columns),
        grid_spec=pltpu.PrefetchScalarGridSpec(
            num_scalar_prefetch=1,
            grid=(pl.cdiv(columns, tile),),
            in_specs=[pl.BlockSpec(memory_space=pl.ANY)] * 4
            + [
                pl.BlockSpec(router.shape, lambda j, s: (0, 0)),
                pl.BlockSpec(difference.shape, lambda j, s: (0, 0)),
                tile_spec,
                tile_spec,
                tile_spec,
                weight_spec,
                weight_spec,
            ],
            out_specs=[
                pl.BlockSpec((2 * rows, 2 * half), lambda j, s: (0, 0)),
                held_spec,
                held_spec,
                tile_spec,
                tile_spec,
                tile_spec,
            ],
            scratch_shapes=[
                pltpu.VMEM((2 * rows, half), bf16),
                pltpu.SemaphoreType.DMA((6,)),
            ],
        ),
        out_shape=[
            jax.ShapeDtypeStruct((2 * rows, 2 * half), bf16),
            jax.ShapeDtypeStruct((2 * rows, 1), f32),
            jax.ShapeDtypeStruct((2 * rows, 1), f32),
            hidden_shape,
            hidden_shape,
            hidden_shape,
        ],
        compiler_params=pltpu.CompilerParams(vmem_limit_bytes=limit_of(2 * rows)),
        cost_estimate=pl.CostEstimate(
            flops=8 * rows * half * columns,
            bytes_accessed=16 * rows * half + 4 * half * columns + 36 * rows * columns,
            transcendentals=2 * rows * columns,
        ),
        name="expert_in",
    )(shard, *pieces, router, difference, plain, *begun, gate_weight, up_weight)


def attended_in_body(
    shard_ref, p0, p1, p2, p3, gate_ref, mixed_ref, w_ref, x_ref, total_ref, y_ref, sems
):
    @pl.when(pl.program_id(0) == 0)
    def _():
        assemble(shard_ref[0], (p0, p1, p2, p3), x_ref, sems)
        total_ref[...] = jnp.zeros_like(total_ref)

    chunk = chunk_of(x_ref.shape[0])

    @pl.loop(0, x_ref.shape[0] // chunk)
    def _(i):
        here = pl.ds(pl.multiple_of(i * chunk, 16), chunk)
        plain = product(x_ref[here, :], w_ref[...])
        total_ref[here, :] += jnp.sum(mixed_ref[here, :].astype(f32) * plain, axis=1, keepdims=True)
        y_ref[here, :] = (gate_ref[here, :] * plain).astype(bf16)


def attended_in(shard, pieces, gate, mixed, weight):
    rows, half = pieces[0].shape
    columns = weight.shape[1]
    tile = min(256, columns)
    return pl.pallas_call(
        attended_in_body,
        grid_spec=pltpu.PrefetchScalarGridSpec(
            num_scalar_prefetch=1,
            grid=(columns // tile,),
            in_specs=[pl.BlockSpec(memory_space=pl.ANY)] * 4
            + [
                pl.BlockSpec((2 * rows, 1), lambda j, s: (0, 0)),
                pl.BlockSpec((2 * rows, tile), lambda j, s: (0, j)),
                pl.BlockSpec((2 * half, tile), lambda j, s: (0, j)),
            ],
            out_specs=[
                pl.BlockSpec((2 * rows, 2 * half), lambda j, s: (0, 0)),
                pl.BlockSpec((2 * rows, 1), lambda j, s: (0, 0)),
                pl.BlockSpec((2 * rows, tile), lambda j, s: (0, j)),
            ],
            scratch_shapes=[pltpu.SemaphoreType.DMA((4,))],
        ),
        out_shape=[
            jax.ShapeDtypeStruct((2 * rows, 2 * half), bf16),
            jax.ShapeDtypeStruct((2 * rows, 1), f32),
            jax.ShapeDtypeStruct((2 * rows, columns), bf16),
        ],
        compiler_params=pltpu.CompilerParams(vmem_limit_bytes=limit_of(2 * rows)),
        cost_estimate=pl.CostEstimate(
            flops=8 * rows * half * columns,
            bytes_accessed=16 * rows * half + 4 * half * columns + 8 * rows * columns,
            transcendentals=0,
        ),
        name="attended_in",
    )(shard, *pieces, gate, mixed, weight)


def rows_half_body(count, extra, shard_ref, *refs):
    lefts, weights = refs[:count], refs[count : 2 * count]
    rest = refs[2 * count :]
    if extra:
        total_ref, gate_ref, diff_ref, router_ref = rest[:4]
        rest = rest[4:]
        coef_ref = rest[2]

        @pl.when(pl.program_id(0) == 0)
        def _():
            coef_ref[...] = (1.0 - gate_ref[...]) * total_ref[...] * diff_ref[...]

    rows = rest[0].shape[0]
    chunk = chunk_of(rows)
    for t in range(2):

        @pl.loop(0, rows // chunk)
        def _(i):
            here = pl.ds(pl.multiple_of(t * rows + i * chunk, 16), chunk)
            there = pl.ds(pl.multiple_of(i * chunk, 16), chunk)
            value = sum(product_last(a[here, :], w[...]) for a, w in zip(lefts, weights))
            if extra:
                value = value + product_last(coef_ref[here, :].astype(bf16), router_ref[...])
            rest[t][there, :] = value.astype(bf16)


def rows_half(shard, mine, lefts, weights, extra=None, tile=512):
    rows, width = lefts[0].shape[0] // 2, weights[0].shape[0]
    half = width // 2
    steps = half // tile

    def at(j, s):
        return j + steps * (s[0] if mine else 1 - s[0])

    def whole_spec(array):
        return pl.BlockSpec(array.shape, lambda j, s: (0, 0))

    in_specs = [whole_spec(a) for a in lefts]
    in_specs += [pl.BlockSpec((tile, w.shape[1]), lambda j, s: (at(j, s), 0)) for w in weights]
    operands = list(lefts) + list(weights)
    out_specs = [pl.BlockSpec((rows, tile), lambda j, s: (0, j))] * 2
    out_shape = [jax.ShapeDtypeStruct((rows, half), bf16)] * 2
    if extra:
        total, gate, difference, router = extra
        in_specs += [whole_spec(total), whole_spec(gate), whole_spec(difference)]
        in_specs += [pl.BlockSpec((tile, router.shape[1]), lambda j, s: (at(j, s), 0))]
        operands += [total, gate, difference, router]
        out_specs.append(whole_spec(difference))
        out_shape.append(jax.ShapeDtypeStruct(difference.shape, f32))
    depth = sum(w.shape[1] for w in weights)
    return pl.pallas_call(
        functools.partial(rows_half_body, len(lefts), extra is not None),
        grid_spec=pltpu.PrefetchScalarGridSpec(
            num_scalar_prefetch=1, grid=(steps,), in_specs=in_specs, out_specs=out_specs
        ),
        out_shape=out_shape,
        compiler_params=pltpu.CompilerParams(vmem_limit_bytes=limit_of(2 * rows)),
        cost_estimate=pl.CostEstimate(
            flops=4 * rows * half * depth,
            bytes_accessed=4 * rows * depth + 2 * half * depth + 4 * rows * half,
            transcendentals=0,
        ),
        name="rows_mine" if mine else "rows_theirs",
    )(shard, *operands)


def prepare_body(
    capacity, scalars, tokens_ref, gain_ref, order_ref, attn_ref, mlp_ref, segment_ref, parent_ref,
    block_ref, attn_pack_ref, mlp_pack_ref, tile_ref,
):
    width = tokens_ref.shape[2]
    count = tokens_ref.shape[1]
    values = tokens_ref[0].astype(f32)
    scales = lax.rsqrt(jnp.mean(values * values, axis=1, keepdims=True) + epsilon)
    block_ref[:, :width] = (values * scales * gain_ref[...]).astype(bf16)

    ranks = order_ref[0].astype(f32)
    pairs = lax.broadcasted_iota(jnp.int32, (2 * count, count), 0)
    owners = lax.broadcasted_iota(jnp.int32, (2 * count, count), 1)
    turns = [(pairs == 2 * owners + k).astype(f32) for k in range(2)]
    rank_rows = [product(ranks, turn) for turn in turns]
    rank_columns = [
        lax.dot_general(turn, ranks, (((0,), (1,)), ((), ())), preferred_element_type=f32)
        for turn in turns
    ]
    same = (
        lax.broadcasted_iota(jnp.int32, (count, count), 0)
        == lax.broadcasted_iota(jnp.int32, (count, count), 1)
    ).astype(f32)
    places = lax.broadcasted_iota(jnp.int32, attn_pack_ref.shape, 0).astype(f32)
    tile_ref[...] = jnp.zeros_like(tile_ref)
    for at, (route_ref, pack_ref) in enumerate(((attn_ref, attn_pack_ref), (mlp_ref, mlp_pack_ref))):
        routes = route_ref[0].astype(f32)
        rows = product_first(routes, same)
        hit = None
        for k in range(2):
            route = rows[k : k + 1]
            slot = jnp.zeros((1, count), f32)
            for other in range(2):
                earlier = (routes[:, other : other + 1] == route) & (
                    rank_columns[other] < rank_rows[k]
                )
                slot = slot + jnp.sum(earlier.astype(f32), axis=0, keepdims=True)
            slot = jnp.minimum(slot, float(capacity))
            tile_ref[4 * at + 2 * k : 4 * at + 2 * k + 1, :] = route
            tile_ref[4 * at + 2 * k + 1 : 4 * at + 2 * k + 2, :] = slot
            code = jnp.where(slot < capacity, route * capacity + slot, -1.0)
            here = places == code
            hit = here if hit is None else hit | here
        pack_ref[...] = hit.astype(bf16)
    tile_ref[8:9, :] = segment_ref[...].astype(f32)
    tile_ref[9:10, : parent_ref.shape[1]] = parent_ref[...].astype(f32)
    block_ref[:, width:] = jnp.zeros((count, block_ref.shape[1] - width), bf16)
    block_ref[:16, width : width + count] = tile_ref[...].astype(bf16)


def prepare(place, tokens, gain, order, attn_routes, mlp_routes, segments, parents, experts, capacity):
    _, count, width = tokens.shape

    def whole_spec(array):
        return pl.BlockSpec(array.shape, lambda i, s: (0,) * array.ndim)

    pack = jax.ShapeDtypeStruct((experts * capacity, count), bf16)
    return pl.pallas_call(
        functools.partial(prepare_body, capacity),
        grid_spec=pltpu.PrefetchScalarGridSpec(
            num_scalar_prefetch=1,
            grid=(1,),
            in_specs=[whole_spec(a) for a in (tokens, gain, order, attn_routes, mlp_routes)]
            + [pl.BlockSpec((1, count), lambda i, s: (0, s[0])), whole_spec(parents)],
            out_specs=[
                pl.BlockSpec((count, width + 128), lambda i, s: (0, 0)),
                pl.BlockSpec(pack.shape, lambda i, s: (0, 0)),
                pl.BlockSpec(pack.shape, lambda i, s: (0, 0)),
            ],
            scratch_shapes=[pltpu.VMEM((16, count), f32)],
        ),
        out_shape=[jax.ShapeDtypeStruct((count, width + 128), bf16), pack, pack],
        compiler_params=pltpu.CompilerParams(vmem_limit_bytes=24 * 2**20),
        name="prepare",
    )(place, tokens, gain, order, attn_routes, mlp_routes, segments, parents)


def difference_of(expert, other, experts):
    range_of = lax.broadcasted_iota(jnp.int32, (other.shape[0], experts), 1).astype(f32)
    return (range_of == expert).astype(f32) - (range_of == other).astype(f32)


def front_body(
    capacity, scalars, rows_ref, marks_ref, router_ref, key_hbm, value_hbm, got_key_hbm, got_value_hbm, *refs
):
    shared_ref, picked_ref, gate_ref, bias_ref, attn_diff_ref, mlp_diff_ref, weight, sems = refs[-8:]
    piece = weight.shape[1] // 2
    heads = piece // HEAD

    step = pl.program_id(0)

    def fetch(sources, at):
        for h in range(heads):
            for i, source in enumerate(sources):
                from_here = source.at[:, pl.ds(pl.multiple_of(at + h * HEAD, HEAD), HEAD)]
                place = weight.at[:, pl.ds((2 * h + i) * HEAD, HEAD)]
                pltpu.make_async_copy(from_here, place, sems.at[h]).start()

    @pl.when((step == 0) & (scalars[0] == 1))
    def _():
        fetch((key_hbm, value_hbm), scalars[1] * piece)

    @pl.when((step == 0) & (scalars[0] == 0))
    def _():
        fetch((got_key_hbm, got_value_hbm), 0)

    count = rows_ref.shape[1]
    width = weight.shape[0]
    blocks = marks_ref.shape[0]
    rows = jnp.concatenate([rows_ref[0, :, :width], rows_ref[1, :, :width]])
    expert = scalars[2].astype(f32)
    index = lax.broadcasted_iota(jnp.int32, (2 * capacity, count), 0)
    lanes = lax.broadcasted_iota(jnp.int32, (2 * capacity, count), 1).astype(f32)
    first = index < capacity
    slots = jnp.where(first, index, index - capacity).astype(f32)
    upper = marks_ref[2 * step].astype(f32)
    lower = marks_ref[2 * step + 1].astype(f32)

    def mark(i):
        return jnp.where(first, upper[i : i + 1, :count], lower[i : i + 1, :count])

    def total(values):
        return jnp.sum(values, axis=1, keepdims=True)

    def hits_of(at):
        hits = [(mark(at + 2 * k) == expert) & (mark(at + 2 * k + 1) == slots) for k in range(2)]
        other = total(jnp.where(hits[0], mark(at + 2), 0.0) + jnp.where(hits[1], mark(at), 0.0))
        return hits[0] | hits[1], other

    experts = attn_diff_ref.shape[1]
    mlp_diff_ref[...] = difference_of(expert, hits_of(4)[1], experts)
    hit, other = hits_of(0)
    difference = difference_of(expert, other, experts)
    attn_diff_ref[...] = difference

    own = total(jnp.where(hit, mark(8), 0.0))
    parents = mark(9)
    one = total(jnp.where(lanes == own, parents, 0.0))
    two = total(jnp.where(lanes == one, parents, 0.0))
    start = jnp.where(first[:, :1], 2 * step * count, (2 * step + 1) * count).astype(f32)
    place = total(jnp.where(hit, lanes, 0.0)) + start
    for j in range(blocks):
        keys = marks_ref[j, 8:9, :count].astype(f32)
        seen = ((keys == own) | (keys == one) | (keys == two)) & (lanes + float(j * count) <= place)
        bias_ref[:, j * count : (j + 1) * count] = jnp.where(seen, 0.0, negative).astype(bf16)

    both = jnp.concatenate([(hit & first).astype(bf16), (hit & ~first).astype(bf16)], axis=1)
    picked = product(both, rows).astype(bf16)
    picked_ref[...] = picked
    logits = product(picked, router_ref[...])
    gate_ref[...] = jax.nn.sigmoid(total(logits * difference))

    @pl.when(step == 0)
    def _():
        for h in range(heads):
            here = pl.ds(2 * h * HEAD, 2 * HEAD)
            pltpu.make_async_copy(weight.at[:, here], weight.at[:, here], sems.at[h]).wait()
            shared_ref[:, here] = product(rows, weight[:, here]).astype(bf16)

    @pl.when(step > 0)
    def _():
        shared_ref[...] = product(rows, weight[...]).astype(bf16)


def front(tree, held, scalars, blocks_of, router, key_weight, value_weight, got_key, got_value, capacity):
    blocks, count, columns = blocks_of.shape
    width, piece = got_key.shape
    experts = router.shape[1]
    length = blocks * count
    rows = blocks * capacity
    steps = blocks // 2
    pinned = pl.BlockSpec(memory_space=pltpu.HBM)

    def out_spec(height, columns):
        return pl.BlockSpec((height, columns), lambda i, s: (tree * steps + i, 0))

    pair = 2 * capacity
    return pl.pallas_call(
        functools.partial(front_body, capacity),
        grid_spec=pltpu.PrefetchScalarGridSpec(
            num_scalar_prefetch=1,
            grid=(steps,),
            in_specs=[
                pl.BlockSpec((2, count, columns), lambda i, s: (i, 0, 0)),
                pl.BlockSpec((blocks, 16, 128), lambda i, s: (0, 0, width // 128)),
                pl.BlockSpec(router.shape, lambda i, s: (0, 0)),
            ]
            + [pinned] * 4
            + [pl.BlockSpec(memory_space=pl.ANY)] * len(held),
            out_specs=[
                out_spec(2 * count, 2 * piece),
                out_spec(pair, width),
                out_spec(pair, 1),
                out_spec(pair, length),
                out_spec(pair, experts),
                out_spec(pair, experts),
            ],
            scratch_shapes=[
                pltpu.VMEM((width, 2 * piece), bf16),
                pltpu.SemaphoreType.DMA((piece // HEAD,)),
            ],
        ),
        out_shape=[
            jax.ShapeDtypeStruct((2 * length, 2 * piece), bf16),
            jax.ShapeDtypeStruct((2 * rows, width), bf16),
            jax.ShapeDtypeStruct((2 * rows, 1), f32),
            jax.ShapeDtypeStruct((2 * rows, length), bf16),
            jax.ShapeDtypeStruct((2 * rows, experts), f32),
            jax.ShapeDtypeStruct((2 * rows, experts), f32),
        ],
        input_output_aliases={8 + i: i for i in range(len(held))},
        compiler_params=pltpu.CompilerParams(vmem_limit_bytes=limit_of(2 * rows)),
        cost_estimate=pl.CostEstimate(
            flops=4 * length * width * piece,
            bytes_accessed=2 * length * width + 4 * width * piece,
            transcendentals=0,
        ),
        name="front",
    )(scalars, blocks_of, blocks_of, router, key_weight, value_weight, got_key, got_value, *held)


def shared_out_body(steps, scalars, sums_ref, key_ref, value_ref, got_key_ref, got_value_ref, *outs):
    step = pl.program_id(0)
    sums = sums_ref[...]
    heads = sums.shape[2] // (2 * HEAD)

    def part(t, i):
        return jnp.concatenate(
            [sums[t, :, (2 * h + i) * HEAD : (2 * h + i + 1) * HEAD] for h in range(heads)], axis=1
        )

    def fill(pair, keys, values):
        for t in range(2):
            value = product_last(part(t, 0), keys[...]) + product_last(part(t, 1), values[...])
            pair[t][...] = value.astype(bf16)

    for side in range(2):
        for local in range(2):
            first = step < steps // 2 if side == 0 else step >= steps // 2

            @pl.when(first & (scalars[1] == local))
            def _():
                pair = (outs[side], outs[2 + side])
                if local:
                    fill(pair, key_ref, value_ref)
                else:
                    fill(pair, got_key_ref, got_value_ref)


def shared_out(scalars, sums, key_weight, value_weight, got_key, got_value, tile=512):
    _, rows, _ = sums.shape
    width, piece = got_key.shape
    half, steps = width // 2, width // tile

    def at(j, s):
        return lax.rem(j + steps // 2 * (1 - s[0]), steps)

    local = pl.BlockSpec((tile, piece), lambda j, s: (at(j, s), s[2]))
    sent = pl.BlockSpec((tile, piece), lambda j, s: (at(j, s), 0))
    theirs = pl.BlockSpec((rows, tile), lambda j, s: (0, jnp.minimum(j, steps // 2 - 1)))
    mine = pl.BlockSpec((rows, tile), lambda j, s: (0, jnp.maximum(j - steps // 2, 0)))
    return pl.pallas_call(
        functools.partial(shared_out_body, steps),
        grid_spec=pltpu.PrefetchScalarGridSpec(
            num_scalar_prefetch=1,
            grid=(steps,),
            in_specs=[pl.BlockSpec(sums.shape, lambda j, s: (0, 0, 0)), local, local, sent, sent],
            out_specs=[theirs, mine, theirs, mine],
        ),
        out_shape=[jax.ShapeDtypeStruct((rows, half), bf16)] * 4,
        compiler_params=pltpu.CompilerParams(vmem_limit_bytes=limit_of(2 * rows)),
        cost_estimate=pl.CostEstimate(
            flops=8 * rows * width * piece,
            bytes_accessed=8 * width * piece + 8 * rows * width,
            transcendentals=0,
        ),
        name="shared_out",
    )(scalars, sums, key_weight, value_weight, got_key, got_value)


def per_device(
    tokens,
    cotangent,
    attn_gain,
    mlp_gain,
    key_weight,
    value_weight,
    query_weight,
    output_weight,
    attn_router,
    gate_weight,
    up_weight,
    down_weight,
    mlp_router,
    segment_ids,
    parent_ids,
    attn_routes,
    mlp_routes,
    slot_order,
):
    count, width = tokens.shape[1:]
    half = width // 2
    piece = query_weight.shape[1]
    experts = attn_router.shape[1]
    blocks = lax.axis_size("dp")
    members = blocks // experts
    capacity = min(count, 5 * count * attn_routes.shape[2] // (4 * experts))
    length, parents = segment_ids.shape[1], parent_ids.shape[1]
    tiles = max(2, length // 512)
    dp, core, shard = lax.axis_index("dp"), lax.axis_index("expert"), lax.axis_index("shard")
    expert, member = dp // members, dp % members

    def my_half(values):
        return lax.dynamic_slice_in_dim(values, shard * half, half, values.ndim - 1)

    def whole(mine):
        got = swap(mine, "shard")
        first = shard == 0
        return jnp.concatenate(
            [jnp.where(first, mine, got), jnp.where(first, got, mine)], axis=mine.ndim - 1
        )

    block, attn_pack, mlp_pack = prepare(
        jnp.reshape(dp, (1,)).astype(jnp.int32),
        tokens,
        attn_gain[None],
        slot_order,
        attn_routes,
        mlp_routes,
        segment_ids,
        parent_ids,
        experts,
        capacity,
    )
    own_blocks, arrivals = ring_gather(block, "dp", blocks, 1)

    heads_at = (member * 2 + core) * 2 + shard
    holder = (member * 2 + core) // members
    offset = holder * 2 * members
    names = ("dp", "expert", "shard")
    sends = []
    for d in range(blocks):
        for c in range(2):
            at = (d * 2 + c) * 2
            source = ((d % members) * 2 + c) // members
            sends.append((at + source, at + 1 - source))
    partner_at = (member * 2 + core) * 2 + 1 - shard

    def partner_columns(weight):
        columns = lax.dynamic_slice_in_dim(weight, (partner_at - offset) * piece, piece, 1)
        return lax.ppermute(after(columns, block), names, sends)

    local = (shard == holder).astype(jnp.int32)
    local_at = local * (heads_at - offset)
    got_key, got_value = partner_columns(key_weight), partner_columns(value_weight)
    own_blocks, got_key, got_value = lax.optimization_barrier((own_blocks, got_key, got_value))
    tree_blocks = [own_blocks, swap(own_blocks, "expert")]

    shard_index = jnp.reshape(shard, (1,)).astype(jnp.int32)

    def pack_rows(values, pack):
        packed = product(pack, values).astype(bf16).reshape(experts, 1, capacity, half)
        packed = jnp.broadcast_to(packed, (experts, members, capacity, half))
        return packed.reshape(blocks, capacity, half)

    def dispatch(packed, work=None, begin=None):
        arrived = lax.all_to_all(packed, "dp", 0, 0, tiled=True)
        done = []
        if work:
            arrived, *done = lax.optimization_barrier((arrived, *work(packed)))
        arrived = arrived.reshape(blocks * capacity, half)
        other = swap(arrived, "expert")
        got = swap(arrived, "shard")
        begun = []
        if begin:
            got, *begun = lax.optimization_barrier((got, *begin(arrived, other)))
        return [arrived, got, other, swap(got, "expert")], done, begun

    def join_ends(sides, work=None):
        own, other, *_ = sides(False, None)
        theirs = (own.astype(f32) + swap(other, "expert").astype(f32)).astype(bf16)
        back = swap(theirs, "shard")
        own, other, *rest = sides(True, theirs)
        done = []
        if work:
            back, *done = lax.optimization_barrier((back, *work(theirs)))
        total = own.astype(f32) + swap(other, "expert").astype(f32) + back.astype(f32)
        return total, rest, done, theirs, own

    def sum_tokens(back, pack):
        if members > 1:
            back = back.reshape(experts, members, capacity, half).astype(f32)
            back = jnp.sum(back, axis=1).astype(bf16)
        return product_first(pack, back.reshape(experts * capacity, half))

    def send_back(joined, work=None):
        back = lax.all_to_all(joined, "dp", 0, 0, tiled=True)
        done = []
        if work:
            back, *done = lax.optimization_barrier((back, *work(joined)))
        return back, done

    def for_tokens(joined):
        return joined.astype(bf16).reshape(blocks, capacity, half)

    grad_half = my_half(cotangent[0])
    grad_packed = after(pack_rows(grad_half, mlp_pack), arrivals[2])
    grad_arrived = lax.all_to_all(grad_packed, "dp", 0, 0, tiled=True)
    grad_arrived = grad_arrived.reshape(blocks * capacity, half)
    scalars = jnp.stack([local, local_at, expert]).astype(jnp.int32)
    held = ()
    for t in range(2):
        held = front(
            t, held, scalars, tree_blocks[t], attn_router, key_weight, value_weight, got_key, got_value, capacity
        )
        if t == 0:
            grad_got = swap(after(grad_arrived, held[2]), "shard")
    shared, rows, attn_gate, bias, attn_difference, mlp_difference = held
    queries = product(rows, query_weight).astype(bf16)
    mixed, log_total = attend(queries, shared, bias, attn_gate, tiles)
    mixed, grad_got = lax.optimization_barrier((mixed, grad_got))
    grad_pieces = (grad_arrived, grad_got, swap(grad_arrived, "expert"), swap(grad_got, "expert"))

    def attn_sides(mine, event):
        return rows_half(shard_index, mine, [after(mixed, event)], [output_weight])

    def plain_work(event):
        return plain_in(shard_index, after(grad_pieces, event), down_weight)

    attn_joined, _, (grad_rows, plain_grad), *_ = join_ends(attn_sides, plain_work)
    back = send_back(for_tokens(attn_joined))[0]
    inputs = tokens[0].astype(f32)
    attn_scale = lax.rsqrt(jnp.mean(inputs * inputs, axis=1, keepdims=True) + epsilon)
    middle = my_half(inputs) + sum_tokens(back, attn_pack)

    def feature_mean(values):
        part = jnp.sum(values, axis=1, keepdims=True)
        return (part + swap(part, "shard")) / width

    mlp_scale = lax.rsqrt(feature_mean(middle * middle) + epsilon)
    half_gain = my_half(mlp_gain)
    mlp_normed = (middle * mlp_scale * half_gain).astype(bf16)

    def begin(own, other):
        return expert_begin(shard_index, own, other, gate_weight, up_weight)

    mlp_pieces, _, begun = dispatch(pack_rows(mlp_normed, mlp_pack), None, begin)
    mlp_rows, mlp_gate, mlp_total, gated_hidden, gate_pre_grad, up_pre_grad = expert_in(
        shard_index, mlp_pieces, mlp_router, mlp_difference, plain_grad, begun, gate_weight, up_weight
    )

    def mlp_sides(mine, event):
        return rows_half(
            shard_index,
            mine,
            after([gate_pre_grad, up_pre_grad], event),
            [gate_weight, up_weight],
            (mlp_total, mlp_gate, mlp_difference, mlp_router),
        )

    def down_work(event):
        return [product_first(after(grad_rows, event), gated_hidden)]

    row_joined, (mlp_coefs,), (down_grad,), *_ = join_ends(mlp_sides, down_work)
    row_joined = for_tokens(row_joined)

    def term_half(mine, event):
        return rows_half(shard_index, mine, [after(gated_hidden, event)], [down_weight])

    def gate_work(event):
        gate_grad = product_first(after(mlp_rows, event), gate_pre_grad)
        own, other = term_half(False, gate_grad)
        theirs = own.astype(f32) + swap(other, "expert").astype(f32)
        return [gate_grad, theirs.astype(bf16)]

    back, (gate_grad, term_theirs) = send_back(row_joined, gate_work)
    mlp_normed_grad = sum_tokens(back, mlp_pack)

    mlp_n = middle * mlp_scale
    weighted = mlp_normed_grad * half_gain
    mlp_gain_part = jnp.sum(mlp_normed_grad * mlp_n, axis=0)
    middle_grad = grad_half.astype(f32) + mlp_scale * (
        weighted - mlp_n * feature_mean(weighted * mlp_n)
    )
    low_grad = middle_grad.astype(bf16)

    def up_work(event):
        up_grad = product_first(after(mlp_rows, event), up_pre_grad)
        router_part = product_first(mlp_coefs, after(mlp_rows, event).astype(f32))
        term_back = swap(after(term_theirs, event), "shard")
        own, other = term_half(True, event)
        total = own.astype(f32) + swap(other, "expert").astype(f32) + term_back.astype(f32)
        return [up_grad, router_part, for_tokens(total)]

    term_pieces, (up_grad, mlp_router_part, term_joined), _ = dispatch(
        pack_rows(low_grad, attn_pack), up_work
    )
    term_back = lax.all_to_all(after(term_joined, term_pieces[0]), "dp", 0, 0, tiled=True)
    term_rows, attn_total, attended_grad = attended_in(
        shard_index, term_pieces, attn_gate, mixed, output_weight
    )
    query_rows_grad, held = attend_back(queries, shared, bias, log_total, attended_grad, tiles)
    held, term_back = lax.optimization_barrier((held, term_back))
    part = length // experts
    held = held.reshape(2, experts, part, 2 * piece)
    key_sums, first_key_sums = ring_scatter(held, experts, members)
    key_sums = key_sums.astype(bf16)

    def input_sides(mine, event):
        return rows_half(
            shard_index,
            mine,
            [after(query_rows_grad, first_key_sums if event is None else event)],
            [query_weight],
            (attn_total, attn_gate, attn_difference, attn_router),
        )

    def query_work(event):
        query_grad = product_first(after(rows, event), query_rows_grad)
        return [query_grad, product_first(after(term_rows, event), mixed)]

    input_joined, (attn_coefs,), (query_grad, output_grad), *_ = join_ends(input_sides, query_work)
    input_joined = for_tokens(input_joined)

    all_sums, arrivals = ring_gather(key_sums.reshape(2 * part, 2 * piece), "dp", experts, members)
    all_sums = all_sums.reshape(2 * length, 2 * piece)
    back = send_back(after(input_joined, key_sums))[0]
    normed_grad = sum_tokens(after(back, arrivals[2]), attn_pack)
    layer_out = whole((middle + sum_tokens(term_back, mlp_pack)).astype(bf16))[None]
    attn_router_part = product_first(attn_coefs, after(rows, arrivals[0]).astype(f32))
    slots = width // experts
    normed_part = jnp.stack(
        [
            lax.dynamic_slice_in_dim(own, expert * slots, slots, 2).reshape(experts, part, slots)
            for own in tree_blocks
        ],
        axis=1,
    ).reshape(2 * length, slots)
    weight_sums = product_first(normed_part, all_sums)

    scalars = jnp.stack([shard, local, local_at]).astype(jnp.int32)
    parts = shared_out(
        scalars,
        after(key_sums, arrivals[0]),
        key_weight,
        value_weight,
        got_key,
        got_value,
    )
    theirs = parts[0].astype(f32) + swap(parts[2], "expert").astype(f32)
    back = swap(theirs.astype(bf16), "shard")
    shared = parts[1].astype(f32) + swap(parts[3], "expert").astype(f32) + back.astype(f32)
    if members > 1:
        groups = [[e * members + m for m in range(members)] for e in range(experts)]
        shared = lax.psum_scatter(
            shared, "dp", scatter_dimension=0, axis_index_groups=groups, tiled=True
        )
    normed_grad = normed_grad + shared

    attn_n = my_half(inputs) * attn_scale
    weighted = normed_grad * my_half(attn_gain)
    attn_gain_part = jnp.sum(normed_grad * attn_n, axis=0)
    tokens_grad = middle_grad + attn_scale * (weighted - attn_n * feature_mean(weighted * attn_n))
    got = swap(tokens_grad.astype(bf16), "shard").astype(f32)
    tokens_grad = jnp.concatenate(
        [jnp.where(shard == 0, tokens_grad, got), jnp.where(shard == 0, got, tokens_grad)], axis=1
    )[None]

    features = width // (2 * blocks)
    heads = piece // HEAD
    pieces = weight_sums.astype(bf16).reshape(members, 2, features, 2 * piece)
    if members > 1:
        groups = [[e * members + m for m in range(members)] for e in range(experts)]
        pieces = lax.all_to_all(pieces, "dp", 0, 0, axis_index_groups=groups, tiled=True)
    pieces = pair_all_to_all(pieces.transpose(1, 0, 2, 3), "expert")
    pieces = pieces.transpose(1, 0, 2, 3).reshape(2, members, features, 2 * piece)
    pieces = pair_all_to_all(pieces, "shard").reshape(2, members, features, heads, 2, HEAD)
    pieces = pieces.transpose(4, 2, 1, 0, 3, 5).reshape(2, features, -1).astype(f32)

    def spread(values):
        return lax.dynamic_update_slice(jnp.zeros((1, width), f32), values[None], (0, shard * half))

    small = [attn_router_part, mlp_router_part, spread(attn_gain_part), spread(mlp_gain_part)]
    small = jnp.pad(jnp.concatenate(small), ((0, 6), (0, 0)))
    small = small + swap(after(small, weight_sums), "shard")
    small = small.reshape(-1, blocks, 2, features).transpose(2, 1, 0, 3)
    mine = lax.dynamic_index_in_dim(small, core, 0, keepdims=False)
    theirs = lax.dynamic_index_in_dim(small, 1 - core, 0, keepdims=False)
    mine = mine + swap(theirs, "expert")
    small = jnp.sum(lax.all_to_all(mine, "dp", 0, 0, tiled=True), axis=0)
    return (
        layer_out,
        tokens_grad,
        small[2 * experts],
        small[2 * experts + 1],
        pieces[0],
        pieces[1],
        query_grad,
        output_grad,
        small[:experts].T,
        gate_grad,
        up_grad,
        down_grad,
        small[experts : 2 * experts].T,
    )


def solution(mesh):
    tree = P("expert", "dp", None)
    columns = P(None, ("dp", "expert", "shard"))
    spread = P(("dp", "expert"), None)
    in_specs = (
        tree,
        tree,
        P(),
        P(),
        P(None, "shard"),
        P(None, "shard"),
        columns,
        columns,
        P(),
        columns,
        columns,
        columns,
        P(),
        P("expert", None),
        P("expert", None),
        tree,
        tree,
        tree,
    )
    out_specs = (
        tree,
        tree,
        P(("dp", "expert")),
        P(("dp", "expert")),
        P(("dp", "expert"), "shard"),
        P(("dp", "expert"), "shard"),
        columns,
        columns,
        spread,
        columns,
        columns,
        columns,
        spread,
    )
    return jax.shard_map(
        per_device, mesh=mesh, in_specs=in_specs, out_specs=out_specs, check_vma=False
    )
```

time: 652 us -> 523 us (0.80)
  matrix products: 156 us -> 50.3 us
  Pallas kernels: 32.9 us -> 114 us
  other arithmetic: 87.5 us -> 14.3 us
  between operations: 48.9 us -> 2.04 us
  starting transfers between devices: 114 us -> 93.1 us
  blocking collectives: 0 us -> 20.2 us
  local copies, waits for them, and re-layouts: 63.2 us -> 77 us
    pallas_call x0 -> x18, Pallas kernels: none -> 90.2 us  [the longest x8 26.4 us: rows_half(): pl.pallas_call(functools.partial(rows_half_body, len(lefts), extra is not...]
    dot_general x12 -> x4, matrix products: 48.9 us -> 6.41 us  [product(): return jnp.dot(former, latter, preferred_element_type=f32)]
    dot_general x11 -> x0, matrix products: 37.8 us -> none  [the longest x9 30.2 us: product_last(): lax.dot_general(former, latter, (((1,), (1,)), ((), ())), preferred_eleme...]
    unnamed x232 -> x173, local copies, waits for them, and re-layouts: 7.57 us -> 43.8 us
    ppermute x4 -> x8, waiting for transfers between devices: 0.01 us -> 36.2 us  [ring_gather(): backward = lax.ppermute(backward, axis, left)]
    dot_general x15 -> x12, matrix products: 69.2 us -> 43.9 us  [product_first(): lax.dot_general(former, latter, (((0,), (0,)), ((), ())), preferred_eleme...]
    convert_element_type x23 -> x18, other arithmetic: 32.6 us -> 8.17 us  [the longest x4 4.71 us: for_tokens(): return joined.astype(bf16).reshape(blocks, capacity, half)]
    concatenate x19 -> x1, other arithmetic: 21.5 us -> 0.03 us  [per_device(): small = jnp.pad(jnp.concatenate(small), ((0, 6), (0, 0)))]
  transfers between devices with their start and end apart: 69 -> 73, of which waited for: 24 -> 38; matrix products, arithmetic and copies ran while one was open for 33% -> 17% of each run, Pallas kernels for 0% -> 17%
where the time goes in v2:
time: 523 us; the launch traced here: 518 us
  waiting for transfers between devices  147 us (28%)
  Pallas kernels  114 us (22%)
  starting transfers between devices  93.1 us (18%)
  local copies, waits for them, and re-layouts  77 us (15%)
  matrix products  50.3 us (10%)
  blocking collectives  20.2 us (4%)
  other arithmetic  14.3 us (3%)
    ppermute x34, waiting for transfers between devices, swap(): return lax.ppermute(values, axis, [(0, 1), (1, 0)])  48 us
    dot_general x12, matrix products, product_first(): lax.dot_general(former, latter, (((0,), (0,)), ((), ())), preferred_eleme...  43.9 us
    unnamed x173, local copies, waits for them, and re-layouts  43.8 us
    ppermute x8, waiting for transfers between devices, ring_gather(): backward = lax.ppermute(backward, axis, left)  36.2 us
    pallas_call x8, Pallas kernels, rows_half(): pl.pallas_call(functools.partial(rows_half_body, len(lefts), extra is not...  26.4 us
    pallas_call x2, Pallas kernels, front(): pl.pallas_call(functools.partial(front_body, capacity), grid_spec=pltpu.P...  23 us
    all_to_all x1, blocking collectives, dispatch(): arrived = lax.all_to_all(packed, 'dp', 0, 0, tiled=True)  20.2 us
    dynamic_update_slice x18, local copies, waits for them, and re-layouts, put(): return lax.dynamic_update_slice(out, piece[None], (source, row, 0))  20 us
  transfers between devices with their start and end apart: 73, of which 38 were waited for; matrix products, arithmetic and copies ran while one was open for 17% of the time, Pallas kernels for 17%

profile of v2, /device:TPU:0, one launch (start us, length us, event | category | flops | bytes accessed | tf_op | source)
XLA Modules:
  0.0 517.9 jit_solution(8870971918696349073)
XLA Ops:
  27.1 9.1 %collective-permute-done.3 = bf16[128,2176]{1,0:T(8,128)(2,1)S(1)} collective-permute-done((bf16[128,2176]{1,0:T(8,128)(2,1)}, bf16[128,2176]{1,0:T(8,128)(2,1)S(1)}, u32[]{:S(2)}, u32[]{:S(2)}) %collective-permute-start.3) | collective-permute-done | bytes 557088 | tf_op jit(solution)/shard_map/ppermute | solution.py:94
  40.0 9.1 %collective-permute-done.5 = bf16[128,2176]{1,0:T(8,128)(2,1)S(1)} collective-permute-done((bf16[128,2176]{1,0:T(8,128)(2,1)S(1)}, bf16[128,2176]{1,0:T(8,128)(2,1)S(1)}, u32[]{:S(2)}, u32[]{:S(2)}) %collective-permute-start.5) | collective-permute-done | bytes 557088 | tf_op jit(solution)/shard_map/ppermute | solution.py:94
  58.5 5.6 %collective-permute-done.9.got_value_hbm.got_value_ref = bf16[2048,512]{1,0:T(8,128)(2,1)} collective-permute-done((bf16[2048,512]{1,0:T(8,128)(2,1)}, bf16[2048,512]{1,0:T(8,128)(2,1)}, u32[]{:S(2)}, u32[]{:S(2)}) %collective-permute-start.9) | collective-permute-done | bytes 2097184 | tf_op jit(solution)/shard_map/ppermute | solution.py:934
  66.3 6.4 %all-to-all-start = ((bf16[8,40,1024]{2,1,0:T(8,128)(2,1)}), bf16[8,40,1024]{2,1,0:T(8,128)(2,1)}, u32[]{:S(2)}, u32[]{:S(2)}) async-start(bf16[8,40,1024]{2,1,0:T(8,128)(2,1)} %bitcast.16), calls=%async_computation | async-start | bytes 1310720 | tf_op jit(solution)/shard_map/all_to_all | solution.py:991
  73.1 11.5 %front.2 = (bf16[2048,1024]{1,0:T(8,128)(2,1)S(1)}, bf16[640,2048]{1,0:T(8,128)(2,1)S(1)}, f32[640,1]{1,0:T(8,128)S(1)}, bf16[640,1024]{1,0:T(8,128)(2,1)S(1)}, ...) custom-call(s32[3]{0:T(128)S(1)} %pad_add_fusion.scalars, ...), custom_call_target="tpu_custom_call" | custom-call | flops 4294967296 | bytes 8388608 | tf_op jit(solution)/shard_map/front/pallas_call | solution.py:761
  99.5 11.5 %front.3 = (bf16[2048,1024]{1,0:T(8,128)(2,1)S(1)}, bf16[640,2048]{1,0:T(8,128)(2,1)S(1)}, f32[640,1]{1,0:T(8,128)S(1)}, bf16[640,1024]{1,0:T(8,128)(2,1)S(1)}, ...) custom-call(s32[3]{0:T(128)S(1)} %pad_add_fusion.scalars, ...), custom_call_target="tpu_custom_call", output_to_operand_aliasing={{0}: (8, {}), {1}: (9, {}), {2}: (10, {}), {3}: (11, {}), {... | custom-call | flops 4294967296 | bytes 8388608 | tf_op jit(solution)/shard_map/front/pallas_call | solution.py:761
  114.4 9.8 %attend.1 = (bf16[640,512]{1,0:T(8,128)(2,1)S(1)}, f32[8,320,1]{2,1,0:T(8,128)S(1)}) custom-call(bf16[640,512]{1,0:T(8,128)(2,1)S(1)} %convolution_convert_fusion.3.q_ref, bf16[2048,1024]{1,0:T(8,128)(2,1)S(1)} %get-tuple-element.133.k_ref.v_ref, bf16[2048,1024]{1,0:T(8,128)(2,1)S(1)} %get-tuple-element.133.k_ref.v_ref, ...), custom_call_target="tpu_custom_call" | custom-call | flops 1342177280 | bytes 5505024 | tf_op jit(solution)/shard_map/attend/pallas_call | solution.py:168
  130.7 8.0 %plain_in.1 = (bf16[640,2048]{1,0:T(8,128)(2,1)S(1)}, f32[640,1408]{1,0:T(8,128)S(1)}) custom-call(s32[1]{0:T(128)} %bitcast.3.shard_ref, bf16[320,1024]{1,0:T(8,128)(2,1)} %bitcast.17.p0, bf16[320,1024]{1,0:T(8,128)(2,1)S(1)} %collective-permute-done.11.p1, bf16[320,1024]{1,0:T(8,128)(2,1)S(1)} %collective-permute-done.15.p2, ...), custom_call_target="tpu_custom_call" | custom-call | flops 3690987520 | bytes 14614528 | tf_op jit(solution)/shard_map/plain_in/pallas_call | solution.py:284
  140.5 5.5 %collective-permute-done.14 = bf16[320,1024]{1,0:T(8,128)(2,1)S(1)} collective-permute-done((bf16[320,1024]{1,0:T(8,128)(2,1)S(1)}, bf16[320,1024]{1,0:T(8,128)(2,1)S(1)}, u32[]{:S(2)}, u32[]{:S(2)}) %collective-permute-start.14) | collective-permute-done | bytes 655392 | tf_op jit(solution)/shard_map/ppermute | solution.py:40
  147.2 5.2 %all-to-all-start.1 = ((bf16[8,40,1024]{2,1,0:T(8,128)(2,1)}), bf16[8,40,1024]{2,1,0:T(8,128)(2,1)}, u32[]{:S(2)}, u32[]{:S(2)}) async-start(bf16[8,40,1024]{2,1,0:T(8,128)(2,1)} %bitcast.18), calls=%async_computation.1 | async-start | bytes 1310720 | tf_op jit(solution)/shard_map/all_to_all | solution.py:980
  152.5 16.8 %all-to-all-done.1 = bf16[8,40,1024]{2,1,0:T(8,128)(2,1)} async-done(((bf16[8,40,1024]{2,1,0:T(8,128)(2,1)}), bf16[8,40,1024]{2,1,0:T(8,128)(2,1)}, u32[]{:S(2)}, u32[]{:S(2)}) %all-to-all-start.1) | async-done | bytes 655392 | tf_op jit(solution)/shard_map/all_to_all | solution.py:980
  174.9 20.2 %all_to_all.40 = bf16[8,40,1024]{2,1,0:T(8,128)(2,1)S(1)} all-to-all(bf16[8,40,1024]{2,1,0:T(8,128)(2,1)S(1)} %bitcast.257), channel_id=1, replica_groups=mesh['dp'=8,'expert'=2,'shard'=2] {'dp'}, dimensions={0} | all-to-all | bytes 1310720 | tf_op jit(solution)/shard_map/all_to_all | solution.py:950
  199.8 7.5 %expert_begin.1 = (f32[640,1408]{1,0:T(8,128)S(1)}, f32[640,1408]{1,0:T(8,128)S(1)}) custom-call(s32[1]{0:T(128)} %bitcast.3.shard_ref, bf16[320,1024]{1,0:T(8,128)(2,1)S(1)} %bitcast.239, bf16[320,1024]{1,0:T(8,128)(2,1)S(1)} %collective-permute-done.19.p2, bf16[2048,1408]{1,0:T(8,128)(2,1)S(1)} %copy-done, bf16[2048,1408]{1,0:T(8,128)(2,1)} %refs_3_.3), custom_call_target="tpu_custom_call" | custom-call | flops 3690987520 | bytes 15597568 | tf_op jit(solution)/shard_map/expert_begin/pallas_call | solution.py:339
  214.8 14.8 %expert_in.1 = (bf16[640,2048]{1,0:T(8,128)(2,1)S(1)}, f32[640,1]{1,0:T(8,128)S(1)}, f32[640,1]{1,0:T(8,128)S(1)}, bf16[640,1408]{1,0:T(8,128)(2,1)S(1)}, bf16[6...) custom-call(s32[1]{0:T(128)} %bitcast.3.shard_ref, bf16[320,1024]{1,0:T(8,128)(2,1)S(1)} %bitcast.240, ...), custom_call_target="tpu_custom_call" | custom-call | flops 3690987520 | bytes 27230208 | tf_op jit(solution)/shard_map/expert_in/pallas_call | solution.py:417
  230.9 8.2 %rows_theirs.5 = (bf16[320,1024]{1,0:T(8,128)(2,1)S(1)}, bf16[320,1024]{1,0:T(8,128)(2,1)S(1)}, f32[640,8]{1,0:T(8,128)}) custom-call(s32[1]{0:T(128)} %bitcast.3.shard_ref, bf16[640,1408]{1,0:T(8,128)(2,1)S(1)} %get-tuple-element.168.refs_0_, bf16[640,1408]{1,0:T(8,128)(2,1)S(1)} %get-tuple-element.169.refs_1_, bf16[2048,1408]{1,0:T(8,128)(2,1)S(1)} %bitcast.231, ...), custom_call_target="tpu_custom_call" | custom-call | flops 3690987520 | bytes 10682368 | tf_op jit(solution)/shard_map/rows_theirs/pallas_call | solution.py:568
  242.2 6.8 %rows_mine.5 = (bf16[320,1024]{1,0:T(8,128)(2,1)S(1)}, bf16[320,1024]{1,0:T(8,128)(2,1)S(1)}, f32[640,8]{1,0:T(8,128)S(1)}) custom-call(s32[1]{0:T(128)} %bitcast.3.shard_ref, bf16[640,1408]{1,0:T(8,128)(2,1)S(1)} %get-tuple-element.168.refs_0_, bf16[640,1408]{1,0:T(8,128)(2,1)S(1)} %get-tuple-element.169.refs_1_, bf16[2048,1408]{1,0:T(8,128)(2,1)S(1)} %bitcast.231, ...), custom_call_target="tpu_custom_call" | custom-call | flops 3690987520 | bytes 10682368 | tf_op jit(solution)/shard_map/rows_mine/pallas_call | solution.py:568
  249.1 7.8 %fusion.32 = f32[2048,1408]{1,0:T(8,128)} fusion(bf16[640,2048]{1,0:T(8,128)(2,1)S(1)} %copy-done.62, bf16[640,1408]{1,0:T(8,128)(2,1)S(1)} %copy-done.23), kind=kOutput, calls=%fused_computation.134 | convolution fusion | flops 3690987520 | bytes 15958016 | tf_op jit(solution)/shard_map/dot_general | solution.py:30
  263.9 9.8 %fusion.33 = f32[2048,1408]{1,0:T(8,128)} fusion(bf16[640,2048]{1,0:T(8,128)(2,1)} %copy-done.44, bf16[640,1408]{1,0:T(8,128)(2,1)} %copy-done.21), kind=kOutput, calls=%fused_computation.135 | convolution fusion | flops 3690987520 | bytes 15958016 | tf_op jit(solution)/shard_map/dot_general | solution.py:30
  288.6 4.7 all-to-all-start.4
  300.0 7.8 %fusion.34 = f32[2048,1408]{1,0:T(8,128)} fusion(bf16[640,2048]{1,0:T(8,128)(2,1)S(1)} %copy-done.45, bf16[640,1408]{1,0:T(8,128)(2,1)S(1)} %copy-done.20), kind=kOutput, calls=%fused_computation.136 | convolution fusion | flops 3690987520 | bytes 15958016 | tf_op jit(solution)/shard_map/dot_general | solution.py:30
  307.8 8.0 %collective-permute-done.27 = bf16[320,1024]{1,0:T(8,128)(2,1)S(1)} collective-permute-done((bf16[320,1024]{1,0:T(8,128)(2,1)S(1)}, bf16[320,1024]{1,0:T(8,128)(2,1)S(1)}, u32[]{:S(2)}, u32[]{:S(2)}) %collective-permute-start.27) | collective-permute-done | bytes 655392 | tf_op jit(solution)/shard_map/ppermute | solution.py:40
  317.8 6.5 %all-to-all-start.5 = ((bf16[8,40,1024]{2,1,0:T(8,128)(2,1)}), bf16[8,40,1024]{2,1,0:T(8,128)(2,1)}, u32[]{:S(2)}, u32[]{:S(2)}) async-start(bf16[8,40,1024]{2,1,0:T(8,128)(2,1)} %bitcast.29), calls=%async_computation.5 | async-start | bytes 1310720 | tf_op jit(solution)/shard_map/all_to_all | solution.py:1081
  324.3 9.2 %collective-permute-done.28.p1 = bf16[320,1024]{1,0:T(8,128)(2,1)} collective-permute-done((bf16[320,1024]{1,0:T(8,128)(2,1)}, bf16[320,1024]{1,0:T(8,128)(2,1)}, u32[]{:S(2)}, u32[]{:S(2)}) %collective-permute-start.28) | collective-permute-done | bytes 655392 | tf_op jit(solution)/shard_map/ppermute | solution.py:40
  344.0 13.8 %attend_back.1 = (bf16[640,512]{1,0:T(8,128)(2,1)S(1)}, bf16[2,1024,1024]{2,1,0:T(8,128)(2,1)S(1)}) custom-call(bf16[640,512]{1,0:T(8,128)(2,1)S(1)} %copy-done.47, bf16[2048,1024]{1,0:T(8,128)(2,1)S(1)} %copy-done.6, bf16[2048,1024]{1,0:T(8,128)(2,1)S(1)} %copy-done.6, bf16[640,1024]{1,0:T(8,128)(2,1)S(1)} %copy-done.32, f32[8,320,1]{2,1,0:T(8,128)S(1)} %copy-done.60, ...), custom_call_target="tpu_custom_call" | custom-call | flops 3355443200 | bytes 9699328 | tf_op jit(solution)/shard_map/attend_back/pallas_call | solution.py:224
  406.0 5.4 %collective-permute-done.47 = bf16[128,1024]{1,0:T(8,128)(2,1)S(1)} collective-permute-done((bf16[128,1024]{1,0:T(8,128)(2,1)S(1)}, bf16[128,1024]{1,0:T(8,128)(2,1)S(1)}, u32[]{:S(2)}, u32[]{:S(2)}) %collective-permute-start.47) | collective-permute-done | bytes 262176 | tf_op jit(solution)/shard_map/ppermute | solution.py:132
  428.8 4.8 all-to-all-start.6
  438.0 6.0 %shared_out.1 = (bf16[128,1024]{1,0:T(8,128)(2,1)S(1)}, bf16[128,1024]{1,0:T(8,128)(2,1)S(1)}, bf16[128,1024]{1,0:T(8,128)(2,1)S(1)}, bf16[128,1024]{1,0:T(8,128)(2,1)S(1)}) custom-call(s32[3]{0:T(128)S(1)} %pad_add_fusion.1.scalars, bf16[2,128,1024]{2,1,0:T(8,128)(2,1)S(1)} %maximum_convert_fusion.sums_ref, bf16[2048,1024]{1,0:T(8,128)(2,1)S(1)} %copy-done.1, ...), custom_call_target="tpu_custom_call" | custom-call | flops 1073741824 | bytes 10485760 | tf_op jit(solution)/shard_map/shared_out/pallas_call | solution.py:845
  451.0 9.4 %collective-permute-done.58 = bf16[256,1024]{1,0:T(8,128)(2,1)S(1)} collective-permute-done((bf16[256,1024]{1,0:T(8,128)(2,1)}, bf16[256,1024]{1,0:T(8,128)(2,1)S(1)}, u32[]{:S(2)}, u32[]{:S(2)}) %collective-permute-start.58) | collective-permute-done | bytes 524320 | tf_op jit(solution)/shard_map/ppermute | solution.py:94
  465.5 7.7 %collective-permute-done.59 = bf16[256,1024]{1,0:T(8,128)(2,1)S(1)} collective-permute-done((bf16[256,1024]{1,0:T(8,128)(2,1)S(1)}, bf16[256,1024]{1,0:T(8,128)(2,1)S(1)}, u32[]{:S(2)}, u32[]{:S(2)}) %collective-permute-start.59) | collective-permute-done | bytes 524320 | tf_op jit(solution)/shard_map/ppermute | solution.py:94
  493.3 5.7 %collective-permute-done.62 = f32[24,2048]{1,0:T(8,128)S(1)} collective-permute-done((f32[24,2048]{1,0:T(8,128)S(1)}, f32[24,2048]{1,0:T(8,128)S(1)}, u32[]{:S(2)}, u32[]{:S(2)}) %collective-permute-start.62) | collective-permute-done | bytes 196640 | tf_op jit(solution)/shard_map/ppermute | solution.py:40
  501.4 5.2 %all-to-all-start.7 = ((f32[8,24,128]{2,1,0:T(8,128)}), f32[8,24,128]{2,1,0:T(8,128)S(1)}, u32[]{:S(2)}, u32[]{:S(2)}) async-start(f32[8,24,128]{2,1,0:T(8,128)} %fusion.26), calls=%async_computation.7 | async-start | bytes 196608 | tf_op jit(solution)/shard_map/all_to_all | solution.py:1173
  508.3 5.5 %all-to-all-done.7 = f32[8,24,128]{2,1,0:T(8,128)S(1)} async-done(((f32[8,24,128]{2,1,0:T(8,128)}), f32[8,24,128]{2,1,0:T(8,128)S(1)}, u32[]{:S(2)}, u32[]{:S(2)}) %all-to-all-start.7) | async-done | bytes 98336 | tf_op jit(solution)/shard_map/all_to_all | solution.py:1173
  (410 shorter events, 242.5 us)
Async XLA Ops:
  6.4 15.8 %collective-permute-start.1 = (bf16[128,2176]{1,0:T(8,128)(2,1)S(1)}, bf16[128,2176]{1,0:T(8,128)(2,1)}, u32[]{:S(2)}, u32[]{:S(2)}) collective-permute-start(bf16[128,2176]{1,0:T(8,128)(2,1)S(1)} %get-tuple-element.120), channel_id=1, source_target_pairs={{0,4},{8,0},{16,8},{24,16},{28,24},{20,28},{12,20},{4,12},{1,5},{9... | collective-permute-start | bytes 1671176 | tf_op jit(solution)/shard_map/ppermute | solution.py:94
  9.4 14.5 %collective-permute-start = (bf16[128,2176]{1,0:T(8,128)(2,1)S(1)}, bf16[128,2176]{1,0:T(8,128)(2,1)S(1)}, u32[]{:S(2)}, u32[]{:S(2)}) collective-permute-start(bf16[128,2176]{1,0:T(8,128)(2,1)S(1)} %get-tuple-element.120), channel_id=1, source_target_pairs={{0,8},{8,16},{16,24},{24,28},{28,20},{20,12},{12,4},{4,0},{1,9},{9... | collective-permute-start | bytes 1671176 | tf_op jit(solution)/shard_map/ppermute | solution.py:93
  14.1 44.4 %collective-permute-start.8 = (bf16[2048,512]{1,0:T(8,128)(2,1)}, bf16[2048,512]{1,0:T(8,128)(2,1)S(1)}, u32[]{:S(2)}, u32[]{:S(2)}) collective-permute-start(bf16[2048,512]{1,0:T(8,128)(2,1)} %get-tuple-element.121), channel_id=1, source_target_pairs={{0,1},{3,2},{4,5},{7,6},{8,9},{11,10},{12,13},{15,14},{16,17},{19,... | collective-permute-start | bytes 6291464 | tf_op jit(solution)/shard_map/ppermute | solution.py:934
  18.0 46.2 %collective-permute-start.9 = (bf16[2048,512]{1,0:T(8,128)(2,1)}, bf16[2048,512]{1,0:T(8,128)(2,1)}, u32[]{:S(2)}, u32[]{:S(2)}) collective-permute-start(bf16[2048,512]{1,0:T(8,128)(2,1)} %get-tuple-element.122), channel_id=1, source_target_pairs={{0,1},{3,2},{4,5},{7,6},{8,9},{11,10},{12,13},{15,14},{16,17},{19,... | collective-permute-start | bytes 6291464 | tf_op jit(solution)/shard_map/ppermute | solution.py:934
  64.2 29.1 %collective-permute-start.10 = (bf16[8,128,2176]{2,1,0:T(8,128)(2,1)}, bf16[8,128,2176]{2,1,0:T(8,128)(2,1)}, u32[]{:S(2)}, u32[]{:S(2)}) collective-permute-start(bf16[8,128,2176]{2,1,0:T(8,128)(2,1)} %bitcast_dynamic-update-slice_fusion.14.rows_ref.marks_ref), channel_id=1, source_target_pairs={{0,2},{2,0},{1,3},{3,1},{4,6},{6,4},{5,7},{7,5},{8,10},{10,8},{9,1... | collective-permute-start | bytes 13369352 | tf_op jit(solution)/shard_map/ppermute | solution.py:40
  66.3 24.5 %all-to-all-start = ((bf16[8,40,1024]{2,1,0:T(8,128)(2,1)}), bf16[8,40,1024]{2,1,0:T(8,128)(2,1)}, u32[]{:S(2)}, u32[]{:S(2)}) async-start(bf16[8,40,1024]{2,1,0:T(8,128)(2,1)} %bitcast.16), calls=%async_computation | async-start | bytes 1310720 | tf_op jit(solution)/shard_map/all_to_all | solution.py:991
  90.7 34.7 %collective-permute-start.11 = (bf16[320,1024]{1,0:T(8,128)(2,1)}, bf16[320,1024]{1,0:T(8,128)(2,1)S(1)}, u32[]{:S(2)}, u32[]{:S(2)}) collective-permute-start(bf16[320,1024]{1,0:T(8,128)(2,1)} %bitcast.17.p0), channel_id=1, source_target_pairs={{0,1},{1,0},{2,3},{3,2},{4,5},{5,4},{6,7},{7,6},{8,9},{9,8},{10,11... | collective-permute-start | bytes 1966088 | tf_op jit(solution)/shard_map/ppermute | solution.py:40
  129.2 16.8 %collective-permute-start.14 = (bf16[320,1024]{1,0:T(8,128)(2,1)S(1)}, bf16[320,1024]{1,0:T(8,128)(2,1)S(1)}, u32[]{:S(2)}, u32[]{:S(2)}) collective-permute-start(bf16[320,1024]{1,0:T(8,128)(2,1)S(1)} %add_convert_fusion.7), channel_id=1, source_target_pairs={{0,1},{1,0},{2,3},{3,2},{4,5},{5,4},{6,7},{7,6},{8,9},{9,8},{10,11... | collective-permute-start | bytes 1966088 | tf_op jit(solution)/shard_map/ppermute | solution.py:40
  130.5 15.6 %collective-permute-start.13 = (bf16[320,1024]{1,0:T(8,128)(2,1)S(1)}, bf16[320,1024]{1,0:T(8,128)(2,1)S(1)}, u32[]{:S(2)}, u32[]{:S(2)}) collective-permute-start(bf16[320,1024]{1,0:T(8,128)(2,1)S(1)} %get-tuple-element.145), channel_id=1, source_target_pairs={{0,2},{2,0},{1,3},{3,1},{4,6},{6,4},{5,7},{7,5},{8,10},{10,8},{9,1... | collective-permute-start | bytes 1966088 | tf_op jit(solution)/shard_map/ppermute | solution.py:40
  147.2 22.1 %all-to-all-start.1 = ((bf16[8,40,1024]{2,1,0:T(8,128)(2,1)}), bf16[8,40,1024]{2,1,0:T(8,128)(2,1)}, u32[]{:S(2)}, u32[]{:S(2)}) async-start(bf16[8,40,1024]{2,1,0:T(8,128)(2,1)} %bitcast.18), calls=%async_computation.1 | async-start | bytes 1310720 | tf_op jit(solution)/shard_map/all_to_all | solution.py:980
  195.1 17.3 %collective-permute-start.18 = (bf16[320,1024]{1,0:T(8,128)(2,1)S(1)}, bf16[320,1024]{1,0:T(8,128)(2,1)}, u32[]{:S(2)}, u32[]{:S(2)}) collective-permute-start(bf16[320,1024]{1,0:T(8,128)(2,1)S(1)} %bitcast.238), channel_id=1, source_target_pairs={{0,1},{1,0},{2,3},{3,2},{4,5},{5,4},{6,7},{7,6},{8,9},{9,8},{10,11... | collective-permute-start | bytes 1966088 | tf_op jit(solution)/shard_map/ppermute | solution.py:40
  241.5 16.8 %collective-permute-start.23 = (bf16[320,1024]{1,0:T(8,128)(2,1)S(1)}, bf16[320,1024]{1,0:T(8,128)(2,1)S(1)}, u32[]{:S(2)}, u32[]{:S(2)}) collective-permute-start(bf16[320,1024]{1,0:T(8,128)(2,1)S(1)} %add_convert_fusion.5), channel_id=1, source_target_pairs={{0,1},{1,0},{2,3},{3,2},{4,5},{5,4},{6,7},{7,6},{8,9},{9,8},{10,11... | collective-permute-start | bytes 1966088 | tf_op jit(solution)/shard_map/ppermute | solution.py:40
  259.5 21.5 %all-to-all-start.3 = ((bf16[8,40,1024]{2,1,0:T(8,128)(2,1)}), bf16[8,40,1024]{2,1,0:T(8,128)(2,1)}, u32[]{:S(2)}, u32[]{:S(2)}) async-start(bf16[8,40,1024]{2,1,0:T(8,128)(2,1)} %bitcast.255), calls=%async_computation.3 | async-start | bytes 1310720 | tf_op jit(solution)/shard_map/all_to_all | solution.py:980
  288.6 28.3 %all-to-all-start.4 = ((bf16[8,40,1024]{2,1,0:T(8,128)(2,1)}), bf16[8,40,1024]{2,1,0:T(8,128)(2,1)}, u32[]{:S(2)}, u32[]{:S(2)}) async-start(bf16[8,40,1024]{2,1,0:T(8,128)(2,1)} %bitcast.256), calls=%async_computation.4 | async-start | bytes 1310720 | tf_op jit(solution)/shard_map/all_to_all | solution.py:950
  298.6 17.1 %collective-permute-start.27 = (bf16[320,1024]{1,0:T(8,128)(2,1)S(1)}, bf16[320,1024]{1,0:T(8,128)(2,1)S(1)}, u32[]{:S(2)}, u32[]{:S(2)}) collective-permute-start(bf16[320,1024]{1,0:T(8,128)(2,1)S(1)} %copy-done.75), channel_id=1, source_target_pairs={{0,1},{1,0},{2,3},{3,2},{4,5},{5,4},{6,7},{7,6},{8,9},{9,8},{10,11... | collective-permute-start | bytes 1966088 | tf_op jit(solution)/shard_map/ppermute | solution.py:40
  316.9 16.6 %collective-permute-start.28 = (bf16[320,1024]{1,0:T(8,128)(2,1)}, bf16[320,1024]{1,0:T(8,128)(2,1)}, u32[]{:S(2)}, u32[]{:S(2)}) collective-permute-start(bf16[320,1024]{1,0:T(8,128)(2,1)} %bitcast.30.p0), channel_id=1, source_target_pairs={{0,1},{1,0},{2,3},{3,2},{4,5},{5,4},{6,7},{7,6},{8,9},{9,8},{10,11... | collective-permute-start | bytes 1966088 | tf_op jit(solution)/shard_map/ppermute | solution.py:40
  317.8 19.3 %collective-permute-start.29 = (bf16[320,1024]{1,0:T(8,128)(2,1)}, bf16[320,1024]{1,0:T(8,128)(2,1)}, u32[]{:S(2)}, u32[]{:S(2)}) collective-permute-start(bf16[320,1024]{1,0:T(8,128)(2,1)} %bitcast.30.p0), channel_id=1, source_target_pairs={{0,2},{2,0},{1,3},{3,1},{4,6},{6,4},{5,7},{7,5},{8,10},{10,8},{9,1... | collective-permute-start | bytes 1966088 | tf_op jit(solution)/shard_map/ppermute | solution.py:40
  317.8 42.0 %all-to-all-start.5 = ((bf16[8,40,1024]{2,1,0:T(8,128)(2,1)}), bf16[8,40,1024]{2,1,0:T(8,128)(2,1)}, u32[]{:S(2)}, u32[]{:S(2)}) async-start(bf16[8,40,1024]{2,1,0:T(8,128)(2,1)} %bitcast.29), calls=%async_computation.5 | async-start | bytes 1310720 | tf_op jit(solution)/shard_map/all_to_all | solution.py:1081
  368.4 23.5 %collective-permute-start.39 = (bf16[128,1024]{1,0:T(8,128)(2,1)S(1)}, bf16[128,1024]{1,0:T(8,128)(2,1)S(1)}, u32[]{:S(2)}, u32[]{:S(2)}) collective-permute-start(bf16[128,1024]{1,0:T(8,128)(2,1)S(1)} %get-tuple-element.287), channel_id=1, source_target_pairs={{0,4},{8,0},{16,8},{24,16},{28,24},{20,28},{12,20},{4,12},{1,5},{9... | collective-permute-start | bytes 786440 | tf_op jit(solution)/shard_map/ppermute | solution.py:132
  368.9 16.2 %collective-permute-start.45 = (bf16[128,1024]{1,0:T(8,128)(2,1)S(1)}, bf16[128,1024]{1,0:T(8,128)(2,1)S(1)}, u32[]{:S(2)}, u32[]{:S(2)}) collective-permute-start(bf16[128,1024]{1,0:T(8,128)(2,1)S(1)} %get-tuple-element.292), channel_id=1, source_target_pairs={{0,4},{8,0},{16,8},{24,16},{28,24},{20,28},{12,20},{4,12},{1,5},{9... | collective-permute-start | bytes 786440 | tf_op jit(solution)/shard_map/ppermute | solution.py:132
  381.9 16.8 %collective-permute-start.33 = (bf16[320,1024]{1,0:T(8,128)(2,1)S(1)}, bf16[320,1024]{1,0:T(8,128)(2,1)S(1)}, u32[]{:S(2)}, u32[]{:S(2)}) collective-permute-start(bf16[320,1024]{1,0:T(8,128)(2,1)S(1)} %get-tuple-element.201), channel_id=1, source_target_pairs={{0,2},{2,0},{1,3},{3,1},{4,6},{6,4},{5,7},{7,5},{8,10},{10,8},{9,1... | collective-permute-start | bytes 1966088 | tf_op jit(solution)/shard_map/ppermute | solution.py:40
  391.7 25.4 %collective-permute-start.44 = (bf16[128,1024]{1,0:T(8,128)(2,1)S(1)}, bf16[128,1024]{1,0:T(8,128)(2,1)S(1)}, u32[]{:S(2)}, u32[]{:S(2)}) collective-permute-start(bf16[128,1024]{1,0:T(8,128)(2,1)S(1)} %get-tuple-element.289), channel_id=1, source_target_pairs={{0,8},{8,16},{16,24},{24,28},{28,20},{20,12},{12,4},{4,0},{1,9},{9... | collective-permute-start | bytes 786440 | tf_op jit(solution)/shard_map/ppermute | solution.py:131
  394.5 18.7 %collective-permute-start.38 = (bf16[128,1024]{1,0:T(8,128)(2,1)S(1)}, bf16[128,1024]{1,0:T(8,128)(2,1)S(1)}, u32[]{:S(2)}, u32[]{:S(2)}) collective-permute-start(bf16[128,1024]{1,0:T(8,128)(2,1)S(1)} %get-tuple-element.285), channel_id=1, source_target_pairs={{0,8},{8,16},{16,24},{24,28},{28,20},{20,12},{12,4},{4,0},{1,9},{9... | collective-permute-start | bytes 786440 | tf_op jit(solution)/shard_map/ppermute | solution.py:131
  396.9 14.4 %collective-permute-start.47 = (bf16[128,1024]{1,0:T(8,128)(2,1)S(1)}, bf16[128,1024]{1,0:T(8,128)(2,1)S(1)}, u32[]{:S(2)}, u32[]{:S(2)}) collective-permute-start(bf16[128,1024]{1,0:T(8,128)(2,1)S(1)} %fusion.2), channel_id=1, source_target_pairs={{0,4},{8,0},{16,8},{24,16},{28,24},{20,28},{12,20},{4,12},{1,5},{9... | collective-permute-start | bytes 786440 | tf_op jit(solution)/shard_map/ppermute | solution.py:132
  398.9 28.7 %collective-permute-start.35 = (bf16[320,1024]{1,0:T(8,128)(2,1)S(1)}, bf16[320,1024]{1,0:T(8,128)(2,1)S(1)}, u32[]{:S(2)}, u32[]{:S(2)}) collective-permute-start(bf16[320,1024]{1,0:T(8,128)(2,1)S(1)} %add_convert_fusion.1), channel_id=1, source_target_pairs={{0,1},{1,0},{2,3},{3,2},{4,5},{5,4},{6,7},{7,6},{8,9},{9,8},{10,11... | collective-permute-start | bytes 1966088 | tf_op jit(solution)/shard_map/ppermute | solution.py:40
  413.2 14.4 %collective-permute-start.34 = (bf16[320,1024]{1,0:T(8,128)(2,1)S(1)}, bf16[320,1024]{1,0:T(8,128)(2,1)S(1)}, u32[]{:S(2)}, u32[]{:S(2)}) collective-permute-start(bf16[320,1024]{1,0:T(8,128)(2,1)S(1)} %get-tuple-element.204), channel_id=1, source_target_pairs={{0,2},{2,0},{1,3},{3,1},{4,6},{6,4},{5,7},{7,5},{8,10},{10,8},{9,1... | collective-permute-start | bytes 1966088 | tf_op jit(solution)/shard_map/ppermute | solution.py:40
  420.8 25.8 %collective-permute-start.57 = (bf16[256,1024]{1,0:T(8,128)(2,1)S(1)}, bf16[256,1024]{1,0:T(8,128)(2,1)}, u32[]{:S(2)}, u32[]{:S(2)}) collective-permute-start(bf16[256,1024]{1,0:T(8,128)(2,1)S(1)} %bitcast.234), channel_id=1, source_target_pairs={{0,4},{8,0},{16,8},{24,16},{28,24},{20,28},{12,20},{4,12},{1,5},{9... | collective-permute-start | bytes 1572872 | tf_op jit(solution)/shard_map/ppermute | solution.py:94
  428.8 48.5 %all-to-all-start.6 = ((bf16[8,40,1024]{2,1,0:T(8,128)(2,1)}), bf16[8,40,1024]{2,1,0:T(8,128)(2,1)}, u32[]{:S(2)}, u32[]{:S(2)}) async-start(bf16[8,40,1024]{2,1,0:T(8,128)(2,1)} %bitcast.35), calls=%async_computation.6 | async-start | bytes 1310720 | tf_op jit(solution)/shard_map/all_to_all | solution.py:980
  443.9 33.3 %collective-permute-start.52 = (bf16[128,1024]{1,0:T(8,128)(2,1)S(1)}, bf16[128,1024]{1,0:T(8,128)(2,1)}, u32[]{:S(2)}, u32[]{:S(2)}) collective-permute-start(bf16[128,1024]{1,0:T(8,128)(2,1)S(1)} %get-tuple-element.213), channel_id=1, source_target_pairs={{0,2},{2,0},{1,3},{3,1},{4,6},{6,4},{5,7},{7,5},{8,10},{10,8},{9,1... | collective-permute-start | bytes 786440 | tf_op jit(solution)/shard_map/ppermute | solution.py:40
  444.0 18.4 %collective-permute-start.53 = (bf16[128,1024]{1,0:T(8,128)(2,1)S(1)}, bf16[128,1024]{1,0:T(8,128)(2,1)S(1)}, u32[]{:S(2)}, u32[]{:S(2)}) collective-permute-start(bf16[128,1024]{1,0:T(8,128)(2,1)S(1)} %get-tuple-element.215), channel_id=1, source_target_pairs={{0,2},{2,0},{1,3},{3,1},{4,6},{6,4},{5,7},{7,5},{8,10},{10,8},{9,1... | collective-permute-start | bytes 786440 | tf_op jit(solution)/shard_map/ppermute | solution.py:40
  444.5 16.2 %collective-permute-start.50 = (bf16[256,1024]{1,0:T(8,128)(2,1)}, bf16[256,1024]{1,0:T(8,128)(2,1)S(1)}, u32[]{:S(2)}, u32[]{:S(2)}) collective-permute-start(bf16[256,1024]{1,0:T(8,128)(2,1)} %collective-permute-done.49), channel_id=1, source_target_pairs={{0,8},{8,16},{16,24},{24,28},{28,20},{20,12},{12,4},{4,0},{1,9},{9... | collective-permute-start | bytes 1572872 | tf_op jit(solution)/shard_map/ppermute | solution.py:93
  491.6 15.1 %collective-permute-start.64 = (bf16[1,128,1024]{2,1,0:T(8,128)(2,1)S(1)}, bf16[1,128,1024]{2,1,0:T(8,128)(2,1)S(1)}, u32[]{:S(2)}, u32[]{:S(2)}) collective-permute-start(bf16[1,128,1024]{2,1,0:T(8,128)(2,1)S(1)} %dynamic-slice_bitcast_fusion.2), channel_id=1, source_target_pairs={{0,2},{2,0},{1,3},{3,1},{4,6},{6,4},{5,7},{7,5},{8,10},{10,8},{9,1... | collective-permute-start | bytes 786440 | tf_op jit(solution)/shard_map/ppermute | solution.py:40
  (124 other events, 1001.0 us)

commit v3 on v2

--- a/solution.py
+++ b/solution.py
@@ -11,6 +11,7 @@
 
 epsilon = 1e-06
 negative = -1e30
+ATTN, MLP, GATE = 0, 32, 64
 scale = HEAD ** (-0.5)
 bf16 = jnp.bfloat16
 f32 = jnp.float32
@@ -71,7 +72,13 @@
     )()
 
 
-def ring_gather(block, axis, count, stride):
+def pinned(values, work, event):
+    *values, made = lax.optimization_barrier((*values, work(event) if work else []))
+    return values, made
+
+
+def ring_gather(block, axis, count, stride, works=()):
+    works = list(works) + [None] * (count // 2)
     order = ring_order(count)
     member = lax.axis_index(axis) // stride
     place = ring_place(member, count)
@@ -85,17 +92,19 @@
 
     out = put(out, block, member, 0)
     forward, backward = block, block
-    arrivals = []
+    results = []
     for step in range(1, count // 2 + 1):
         last = step == count // 2
         if last:
             forward, backward = forward[:half], backward[half:]
+        event = forward
         forward = lax.ppermute(forward, axis, right)
         backward = lax.ppermute(backward, axis, left)
-        arrivals.append(forward)
+        (forward, backward), made = pinned((forward, backward), works[step - 1], event)
+        results.append(made)
         out = put(out, forward, ring_member(place - step, count), 0)
         out = put(out, backward, ring_member(place + step, count), half if last else 0)
-    return out, arrivals
+    return out, results
 
 
 def ring_moves(order, by, stride):
@@ -113,40 +122,40 @@
     return lax.optimization_barrier((values,) + events)[0]
 
 
-def ring_scatter(parts, count, stride):
+def ring_scatter(parts, count, stride, works=()):
+    works = list(works) + [None] * (count // 2)
     order = ring_order(count)
     place = ring_place(lax.axis_index("dp") // stride, count)
     right, left = ring_moves(order, 1, stride), ring_moves(order, -1, stride)
     far = count // 2
 
-    def part(tree, offset):
-        return lax.dynamic_index_in_dim(parts[tree], ring_member(place + offset, count), 0, keepdims=False)
-
-    def added(sent, tree, offset):
-        return (part(tree, offset).astype(f32) + sent.astype(f32)).astype(bf16)
-
-    forward, backward = [part(0, far)], [part(1, -far)]
-    first = None
+    def part(offset):
+        return lax.dynamic_index_in_dim(parts, ring_member(place + offset, count), 0, keepdims=False)
+
+    def added(sent, offset, first):
+        own = part(offset).astype(f32)
+        if first is not None:
+            sent = jnp.pad(sent, ((first, 1 - first), (0, 0), (0, 0)))
+        return (own + sent.astype(f32)).astype(bf16)
+
+    forward, backward = part(far)[:1], part(-far)[1:]
+    results = []
     for step in range(far):
-        forward = [lax.ppermute(v, "dp", right) for v in forward]
-        backward = [lax.ppermute(v, "dp", left) for v in backward]
-        first = forward[0] if first is None else first
+        event = forward
+        forward = lax.ppermute(forward, "dp", right)
+        backward = lax.ppermute(backward, "dp", left)
+        (forward, backward), made = pinned((forward, backward), works[step], event)
+        results.append(made)
         offset = far - 1 - step
-        if step == 0:
-            forward.append(part(1, offset))
-            backward.insert(0, part(0, -offset))
-            if offset:
-                forward[0] = added(forward[0], 0, offset)
-                backward[1] = added(backward[1], 1, -offset)
-        elif offset:
-            forward = [added(forward[t], t, offset) for t in range(2)]
-            backward = [added(backward[t], t, -offset) for t in range(2)]
-    total = [part(t, 0).astype(f32) + forward[t].astype(f32) + backward[t].astype(f32) for t in range(2)]
-    return jnp.stack(total), first
-
-
-def attend_body(tiles, keys_per_tile, q_ref, k_ref, v_ref, bias_ref, gate_ref, out_ref, total_ref):
+        if offset:
+            forward = added(forward, offset, 0 if step == 0 else None)
+            backward = added(backward, -offset, 1 if step == 0 else None)
+    return part(0).astype(f32) + forward.astype(f32) + backward.astype(f32), results
+
+
+def attend_body(tiles, keys_per_tile, q_ref, k_ref, v_ref, bias_ref, info_ref, out_ref, total_ref):
     rows = q_ref.shape[0] // tiles
+    lanes = lax.broadcasted_iota(jnp.int32, (rows, 128), 1)
     for tile in range(tiles):
         here = pl.ds(tile * rows, rows)
         keys = (tile + 1) * keys_per_tile
@@ -155,13 +164,14 @@
         highest = jnp.max(scores, axis=1, keepdims=True)
         expo = jnp.exp(scores - highest)
         summed = jnp.sum(expo, axis=1, keepdims=True)
-        probs = (expo * (1.0 / summed)).astype(bf16)
-        mixed = product(probs, v_ref[:keys, :]).astype(bf16).astype(f32)
-        out_ref[here, :] = (mixed * gate_ref[here, :]).astype(bf16)
-        total_ref[0, here, :] = highest + jnp.log(summed)
-
-
-def attend(queries, shared, bias, gate, tiles):
+        mixed = product(expo.astype(bf16), v_ref[:keys, :]) * (1.0 / summed)
+        mixed = mixed.astype(bf16).astype(f32)
+        out_ref[here, :] = (mixed * info_ref[here, GATE : GATE + 1]).astype(bf16)
+        total = highest + jnp.log(summed)
+        total_ref[here, :] = jnp.where(lanes == pl.program_id(1), total, total_ref[here, :])
+
+
+def attend(queries, shared, bias, info, tiles):
     rows, columns = queries.shape[0] // 2, queries.shape[1]
     length = shared.shape[0] // 2
     heads = columns // HEAD
@@ -173,15 +183,15 @@
             pl.BlockSpec((length, HEAD), lambda t, h: (t, 2 * h)),
             pl.BlockSpec((length, HEAD), lambda t, h: (t, 2 * h + 1)),
             pl.BlockSpec((rows, length), lambda t, h: (t, 0)),
-            pl.BlockSpec((rows, 1), lambda t, h: (t, 0)),
+            pl.BlockSpec((rows, 128), lambda t, h: (t, 0)),
         ],
         out_specs=[
             pl.BlockSpec((rows, HEAD), lambda t, h: (t, h)),
-            pl.BlockSpec((1, rows, 1), lambda t, h: (t * heads + h, 0, 0)),
+            pl.BlockSpec((rows, 128), lambda t, h: (t, 0)),
         ],
         out_shape=[
             jax.ShapeDtypeStruct((2 * rows, columns), bf16),
-            jax.ShapeDtypeStruct((2 * heads, rows, 1), f32),
+            jax.ShapeDtypeStruct((2 * rows, 128), f32),
         ],
         compiler_params=pltpu.CompilerParams(vmem_limit_bytes=limit_of(2 * rows)),
         cost_estimate=pl.CostEstimate(
@@ -190,13 +200,14 @@
             transcendentals=2 * rows * length * heads,
         ),
         name="attend",
-    )(queries, shared, shared, bias, gate)
+    )(queries, shared, shared, bias, info)
 
 
 def attend_back_body(
     tiles, keys_per_tile, q_ref, k_ref, v_ref, bias_ref, total_ref, grad_ref, dq_ref, both_ref, dk_sum, dv_sum
 ):
     rows = q_ref.shape[0] // tiles
+    lanes = lax.broadcasted_iota(jnp.int32, (rows, 128), 1)
     dk_sum[...] = jnp.zeros_like(dk_sum)
     dv_sum[...] = jnp.zeros_like(dv_sum)
     for tile in range(tiles):
@@ -205,15 +216,16 @@
         query, grad = q_ref[here, :], grad_ref[here, :]
         scores = product_last(query, k_ref[:keys, :]) * scale
         scores = scores + bias_ref[here, :keys].astype(f32)
-        probs = jnp.exp(scores - total_ref[0, here, :])
+        total = jnp.where(lanes == pl.program_id(1), total_ref[here, :], 0.0)
+        probs = jnp.exp(scores - jnp.sum(total, axis=1, keepdims=True))
         prob_grad = product_last(grad, v_ref[:keys, :])
         inner = jnp.sum(probs * prob_grad, axis=1, keepdims=True)
         score_grad = (probs * (prob_grad - inner) * scale).astype(bf16)
         dq_ref[here, :] = product(score_grad, k_ref[:keys, :]).astype(bf16)
         dk_sum[:keys, :] += product_first(score_grad, query)
         dv_sum[:keys, :] += product_first(probs.astype(bf16), grad)
-    both_ref[0, :, :HEAD] = dk_sum[...].astype(bf16)
-    both_ref[0, :, HEAD:] = dv_sum[...].astype(bf16)
+    both_ref[0, 0] = dk_sum[...].astype(bf16)
+    both_ref[1, 0] = dv_sum[...].astype(bf16)
 
 
 def attend_back(queries, shared, bias, total, grads, tiles):
@@ -229,16 +241,16 @@
             pl.BlockSpec((length, HEAD), lambda t, h: (t, 2 * h)),
             pl.BlockSpec((length, HEAD), lambda t, h: (t, 2 * h + 1)),
             pl.BlockSpec((rows, length), lambda t, h: (t, 0)),
-            pl.BlockSpec((1, rows, 1), lambda t, h: (t * heads + h, 0, 0)),
+            pl.BlockSpec((rows, 128), lambda t, h: (t, 0)),
             row_spec,
         ],
-        out_specs=[row_spec, pl.BlockSpec((1, length, 2 * HEAD), lambda t, h: (t, 0, h))],
+        out_specs=[row_spec, pl.BlockSpec((2, 1, length, HEAD), lambda t, h: (h, t, 0, 0))],
         out_shape=[
             jax.ShapeDtypeStruct((2 * rows, columns), bf16),
-            jax.ShapeDtypeStruct((2, length, 2 * columns), bf16),
+            jax.ShapeDtypeStruct((2 * heads, 2, length, HEAD), bf16),
         ],
         scratch_shapes=[pltpu.VMEM((length, HEAD), f32), pltpu.VMEM((length, HEAD), f32)],
-        compiler_params=pltpu.CompilerParams(vmem_limit_bytes=limit_of(2 * rows)),
+        compiler_params=pltpu.CompilerParams(vmem_limit_bytes=60 * 2**20),
         cost_estimate=pl.CostEstimate(
             flops=20 * rows * length * columns,
             bytes_accessed=4 * (rows * length + 4 * length * columns),
@@ -275,7 +287,7 @@
     @pl.loop(0, x_ref.shape[0] // chunk)
     def _(i):
         here = pl.ds(pl.multiple_of(i * chunk, 16), chunk)
-        y_ref[here, :] = product(x_ref[here, :], w_ref[...])
+        y_ref[here, :] = product(x_ref[here, :], w_ref[...]).astype(bf16)
 
 
 def plain_in(shard, pieces, weight, tile=512):
@@ -296,7 +308,7 @@
         ),
         out_shape=[
             jax.ShapeDtypeStruct((2 * rows, 2 * half), bf16),
-            jax.ShapeDtypeStruct((2 * rows, columns), f32),
+            jax.ShapeDtypeStruct((2 * rows, columns), bf16),
         ],
         compiler_params=pltpu.CompilerParams(vmem_limit_bytes=limit_of(2 * rows)),
         cost_estimate=pl.CostEstimate(
@@ -327,8 +339,8 @@
     @pl.loop(0, x_ref.shape[0] // chunk)
     def _(i):
         here = pl.ds(pl.multiple_of(i * chunk, 16), chunk)
-        gate_ref[here, :] = product(x_ref[here, :], gw_ref[...])
-        up_ref[here, :] = product(x_ref[here, :], uw_ref[...])
+        gate_ref[here, :] = product(x_ref[here, :], gw_ref[...]).astype(bf16)
+        up_ref[here, :] = product(x_ref[here, :], uw_ref[...]).astype(bf16)
 
 
 def expert_begin(shard, own, other, gate_weight, up_weight, tile=512):
@@ -348,8 +360,8 @@
                 pltpu.SemaphoreType.DMA((2,)),
             ],
         ),
-        out_shape=[jax.ShapeDtypeStruct((2 * rows, columns), f32)] * 2,
-        compiler_params=pltpu.CompilerParams(vmem_limit_bytes=limit_of(2 * rows)),
+        out_shape=[jax.ShapeDtypeStruct((2 * rows, columns), bf16)] * 2,
+        compiler_params=pltpu.CompilerParams(vmem_limit_bytes=60 * 2**20),
         cost_estimate=pl.CostEstimate(
             flops=8 * rows * half * columns,
             bytes_accessed=8 * rows * half + 4 * half * columns + 16 * rows * columns,
@@ -360,7 +372,7 @@
 
 
 def expert_in_body(
-    columns, shard_ref, p0, p1, p2, p3, router_ref, diff_ref, plain_ref, gp_ref, up_ref, gw_ref, uw_ref,
+    columns, shard_ref, p0, p1, p2, p3, router_ref, info_ref, plain_ref, gp_ref, up_ref, gw_ref, uw_ref,
     x_ref, gate_ref, total_ref, hidden_ref, dgate_ref, dup_ref, their_ref, sems,
 ):
     tile = gw_ref.shape[1]
@@ -379,7 +391,9 @@
         for copy in copies:
             copy.wait()
         logits = product(x_ref[...], router_ref[...])
-        gate_ref[...] = jax.nn.sigmoid(jnp.sum(logits * diff_ref[...], axis=1, keepdims=True))
+        difference = info_ref[:, MLP : MLP + router_ref.shape[1]]
+        gate = jax.nn.sigmoid(jnp.sum(logits * difference, axis=1, keepdims=True))
+        gate_ref[...] = jnp.broadcast_to(gate, gate_ref.shape)
         total_ref[...] = jnp.zeros_like(total_ref)
 
     chunk = chunk_of(x_ref.shape[0])
@@ -388,9 +402,9 @@
     def _(i):
         here = pl.ds(pl.multiple_of(i * chunk, 16), chunk)
         their = their_ref[here, :]
-        gate_pre = gp_ref[here, :] + product(their, gw_ref[...])
-        up_pre = up_ref[here, :] + product(their, uw_ref[...])
-        plain, gate = plain_ref[here, :], gate_ref[here, :]
+        gate_pre = gp_ref[here, :].astype(f32) + product(their, gw_ref[...])
+        up_pre = up_ref[here, :].astype(f32) + product(their, uw_ref[...])
+        plain, gate = plain_ref[here, :].astype(f32), gate_ref[here, :1]
         inside = lax.broadcasted_iota(jnp.int32, (1, tile), 1) + step * tile < columns
         sigmoid = jax.nn.sigmoid(gate_pre)
         silu = gate_pre * sigmoid
@@ -407,12 +421,12 @@
         dgate_ref[here, :] = gate_grad.astype(bf16)
 
 
-def expert_in(shard, pieces, router, difference, plain, begun, gate_weight, up_weight, tile=256):
+def expert_in(shard, pieces, router, info, plain, begun, gate_weight, up_weight, tile=256):
     rows, half = pieces[0].shape
     columns = gate_weight.shape[1]
     weight_spec = pl.BlockSpec((half, tile), lambda j, s: (1 - s[0], j))
     tile_spec = pl.BlockSpec((2 * rows, tile), lambda j, s: (0, j))
-    held_spec = pl.BlockSpec((2 * rows, 1), lambda j, s: (0, 0))
+    held_spec = pl.BlockSpec((2 * rows, 128), lambda j, s: (0, 0))
     hidden_shape = jax.ShapeDtypeStruct((2 * rows, columns), bf16)
     return pl.pallas_call(
         functools.partial(expert_in_body, columns),
@@ -422,7 +436,7 @@
             in_specs=[pl.BlockSpec(memory_space=pl.ANY)] * 4
             + [
                 pl.BlockSpec(router.shape, lambda j, s: (0, 0)),
-                pl.BlockSpec(difference.shape, lambda j, s: (0, 0)),
+                pl.BlockSpec(info.shape, lambda j, s: (0, 0)),
                 tile_spec,
                 tile_spec,
                 tile_spec,
@@ -444,24 +458,24 @@
         ),
         out_shape=[
             jax.ShapeDtypeStruct((2 * rows, 2 * half), bf16),
-            jax.ShapeDtypeStruct((2 * rows, 1), f32),
-            jax.ShapeDtypeStruct((2 * rows, 1), f32),
+            jax.ShapeDtypeStruct((2 * rows, 128), f32),
+            jax.ShapeDtypeStruct((2 * rows, 128), f32),
             hidden_shape,
             hidden_shape,
             hidden_shape,
         ],
-        compiler_params=pltpu.CompilerParams(vmem_limit_bytes=limit_of(2 * rows)),
+        compiler_params=pltpu.CompilerParams(vmem_limit_bytes=60 * 2**20),
         cost_estimate=pl.CostEstimate(
             flops=8 * rows * half * columns,
             bytes_accessed=16 * rows * half + 4 * half * columns + 36 * rows * columns,
             transcendentals=2 * rows * columns,
         ),
         name="expert_in",
-    )(shard, *pieces, router, difference, plain, *begun, gate_weight, up_weight)
+    )(shard, *pieces, router, info, plain, *begun, gate_weight, up_weight)
 
 
 def attended_in_body(
-    shard_ref, p0, p1, p2, p3, gate_ref, mixed_ref, w_ref, x_ref, total_ref, y_ref, sems
+    shard_ref, p0, p1, p2, p3, info_ref, mixed_ref, w_ref, x_ref, total_ref, y_ref, sems
 ):
     @pl.when(pl.program_id(0) == 0)
     def _():
@@ -475,10 +489,10 @@
         here = pl.ds(pl.multiple_of(i * chunk, 16), chunk)
         plain = product(x_ref[here, :], w_ref[...])
         total_ref[here, :] += jnp.sum(mixed_ref[here, :].astype(f32) * plain, axis=1, keepdims=True)
-        y_ref[here, :] = (gate_ref[here, :] * plain).astype(bf16)
-
-
-def attended_in(shard, pieces, gate, mixed, weight):
+        y_ref[here, :] = (info_ref[here, GATE : GATE + 1] * plain).astype(bf16)
+
+
+def attended_in(shard, pieces, info, mixed, weight):
     rows, half = pieces[0].shape
     columns = weight.shape[1]
     tile = min(256, columns)
@@ -489,20 +503,20 @@
             grid=(columns // tile,),
             in_specs=[pl.BlockSpec(memory_space=pl.ANY)] * 4
             + [
-                pl.BlockSpec((2 * rows, 1), lambda j, s: (0, 0)),
+                pl.BlockSpec((2 * rows, 128), lambda j, s: (0, 0)),
                 pl.BlockSpec((2 * rows, tile), lambda j, s: (0, j)),
                 pl.BlockSpec((2 * half, tile), lambda j, s: (0, j)),
             ],
             out_specs=[
                 pl.BlockSpec((2 * rows, 2 * half), lambda j, s: (0, 0)),
-                pl.BlockSpec((2 * rows, 1), lambda j, s: (0, 0)),
+                pl.BlockSpec((2 * rows, 128), lambda j, s: (0, 0)),
                 pl.BlockSpec((2 * rows, tile), lambda j, s: (0, j)),
             ],
             scratch_shapes=[pltpu.SemaphoreType.DMA((4,))],
         ),
         out_shape=[
             jax.ShapeDtypeStruct((2 * rows, 2 * half), bf16),
-            jax.ShapeDtypeStruct((2 * rows, 1), f32),
+            jax.ShapeDtypeStruct((2 * rows, 128), f32),
             jax.ShapeDtypeStruct((2 * rows, columns), bf16),
         ],
         compiler_params=pltpu.CompilerParams(vmem_limit_bytes=limit_of(2 * rows)),
@@ -512,10 +526,10 @@
             transcendentals=0,
         ),
         name="attended_in",
-    )(shard, *pieces, gate, mixed, weight)
-
-
-def rows_half_body(count, extra, shard_ref, *refs):
+    )(shard, *pieces, info, mixed, weight)
+
+
+def rows_half_body(count, extra, gate_at, diff_at, shard_ref, *refs):
     lefts, weights = refs[:count], refs[count : 2 * count]
     rest = refs[2 * count :]
     if extra:
@@ -525,7 +539,9 @@
 
         @pl.when(pl.program_id(0) == 0)
         def _():
-            coef_ref[...] = (1.0 - gate_ref[...]) * total_ref[...] * diff_ref[...]
+            gate = gate_ref[:, gate_at : gate_at + 1]
+            difference = diff_ref[:, diff_at : diff_at + router_ref.shape[1]]
+            coef_ref[...] = (1.0 - gate) * total_ref[:, :1] * difference
 
     rows = rest[0].shape[0]
     chunk = chunk_of(rows)
@@ -557,21 +573,23 @@
     operands = list(lefts) + list(weights)
     out_specs = [pl.BlockSpec((rows, tile), lambda j, s: (0, j))] * 2
     out_shape = [jax.ShapeDtypeStruct((rows, half), bf16)] * 2
+    gate_at = diff_at = 0
     if extra:
-        total, gate, difference, router = extra
+        total, gate, gate_at, difference, diff_at, router = extra
         in_specs += [whole_spec(total), whole_spec(gate), whole_spec(difference)]
         in_specs += [pl.BlockSpec((tile, router.shape[1]), lambda j, s: (at(j, s), 0))]
         operands += [total, gate, difference, router]
-        out_specs.append(whole_spec(difference))
-        out_shape.append(jax.ShapeDtypeStruct(difference.shape, f32))
+        coefs = jax.ShapeDtypeStruct((2 * rows, router.shape[1]), f32)
+        out_specs.append(whole_spec(coefs))
+        out_shape.append(coefs)
     depth = sum(w.shape[1] for w in weights)
     return pl.pallas_call(
-        functools.partial(rows_half_body, len(lefts), extra is not None),
+        functools.partial(rows_half_body, len(lefts), extra is not None, gate_at, diff_at),
         grid_spec=pltpu.PrefetchScalarGridSpec(
             num_scalar_prefetch=1, grid=(steps,), in_specs=in_specs, out_specs=out_specs
         ),
         out_shape=out_shape,
-        compiler_params=pltpu.CompilerParams(vmem_limit_bytes=limit_of(2 * rows)),
+        compiler_params=pltpu.CompilerParams(vmem_limit_bytes=limit_of(2 * rows) if len(lefts) == 1 else 60 * 2**20),
         cost_estimate=pl.CostEstimate(
             flops=4 * rows * half * depth,
             bytes_accessed=4 * rows * depth + 2 * half * depth + 4 * rows * half,
@@ -664,13 +682,13 @@
 
 
 def front_body(
-    capacity, scalars, rows_ref, marks_ref, router_ref, key_hbm, value_hbm, got_key_hbm, got_value_hbm, *refs
+    capacity, steps, scalars, own_ref, other_ref, own_marks_ref, other_marks_ref, router_ref,
+    key_hbm, value_hbm, got_key_hbm, got_value_hbm, shared_ref, picked_ref, bias_ref, info_ref, weight, sems,
 ):
-    shared_ref, picked_ref, gate_ref, bias_ref, attn_diff_ref, mlp_diff_ref, weight, sems = refs[-8:]
     piece = weight.shape[1] // 2
     heads = piece // HEAD
 
-    step = pl.program_id(0)
+    turn = pl.program_id(0)
 
     def fetch(sources, at):
         for h in range(heads):
@@ -679,14 +697,33 @@
                 place = weight.at[:, pl.ds((2 * h + i) * HEAD, HEAD)]
                 pltpu.make_async_copy(from_here, place, sems.at[h]).start()
 
-    @pl.when((step == 0) & (scalars[0] == 1))
+    @pl.when((turn == 0) & (scalars[0] == 1))
     def _():
         fetch((key_hbm, value_hbm), scalars[1] * piece)
 
-    @pl.when((step == 0) & (scalars[0] == 0))
+    @pl.when((turn == 0) & (scalars[0] == 0))
     def _():
         fetch((got_key_hbm, got_value_hbm), 0)
 
+    def one_step(step, rows_ref, marks_ref):
+        front_step(
+            capacity, heads, turn, step, scalars, rows_ref, marks_ref, router_ref,
+            shared_ref, picked_ref, bias_ref, info_ref, weight, sems,
+        )
+
+    @pl.when(turn < steps)
+    def _():
+        one_step(turn, own_ref, own_marks_ref)
+
+    @pl.when(turn >= steps)
+    def _():
+        one_step(turn - steps, other_ref, other_marks_ref)
+
+
+def front_step(
+    capacity, heads, turn, step, scalars, rows_ref, marks_ref, router_ref,
+    shared_ref, picked_ref, bias_ref, info_ref, weight, sems,
+):
     count = rows_ref.shape[1]
     width = weight.shape[0]
     blocks = marks_ref.shape[0]
@@ -710,11 +747,11 @@
         other = total(jnp.where(hits[0], mark(at + 2), 0.0) + jnp.where(hits[1], mark(at), 0.0))
         return hits[0] | hits[1], other
 
-    experts = attn_diff_ref.shape[1]
-    mlp_diff_ref[...] = difference_of(expert, hits_of(4)[1], experts)
+    experts = router_ref.shape[1]
+    info_ref[:, MLP : MLP + experts] = difference_of(expert, hits_of(4)[1], experts)
     hit, other = hits_of(0)
     difference = difference_of(expert, other, experts)
-    attn_diff_ref[...] = difference
+    info_ref[:, ATTN : ATTN + experts] = difference
 
     own = total(jnp.where(hit, mark(8), 0.0))
     parents = mark(9)
@@ -731,52 +768,51 @@
     picked = product(both, rows).astype(bf16)
     picked_ref[...] = picked
     logits = product(picked, router_ref[...])
-    gate_ref[...] = jax.nn.sigmoid(total(logits * difference))
-
-    @pl.when(step == 0)
+    info_ref[:, GATE : GATE + 1] = jax.nn.sigmoid(total(logits * difference))
+
+    @pl.when(turn == 0)
     def _():
         for h in range(heads):
             here = pl.ds(2 * h * HEAD, 2 * HEAD)
             pltpu.make_async_copy(weight.at[:, here], weight.at[:, here], sems.at[h]).wait()
             shared_ref[:, here] = product(rows, weight[:, here]).astype(bf16)
 
-    @pl.when(step > 0)
+    @pl.when(turn > 0)
     def _():
         shared_ref[...] = product(rows, weight[...]).astype(bf16)
 
 
-def front(tree, held, scalars, blocks_of, router, key_weight, value_weight, got_key, got_value, capacity):
-    blocks, count, columns = blocks_of.shape
+def front(scalars, own, other, router, key_weight, value_weight, got_key, got_value, capacity):
+    blocks, count, columns = own.shape
     width, piece = got_key.shape
-    experts = router.shape[1]
     length = blocks * count
     rows = blocks * capacity
     steps = blocks // 2
-    pinned = pl.BlockSpec(memory_space=pltpu.HBM)
+    pinned_spec = pl.BlockSpec(memory_space=pltpu.HBM)
+    marks_spec = pl.BlockSpec((blocks, 16, 128), lambda i, s: (0, 0, width // 128))
 
     def out_spec(height, columns):
-        return pl.BlockSpec((height, columns), lambda i, s: (tree * steps + i, 0))
+        return pl.BlockSpec((height, columns), lambda i, s: (i, 0))
 
     pair = 2 * capacity
     return pl.pallas_call(
-        functools.partial(front_body, capacity),
+        functools.partial(front_body, capacity, steps),
         grid_spec=pltpu.PrefetchScalarGridSpec(
             num_scalar_prefetch=1,
-            grid=(steps,),
+            grid=(2 * steps,),
             in_specs=[
-                pl.BlockSpec((2, count, columns), lambda i, s: (i, 0, 0)),
-                pl.BlockSpec((blocks, 16, 128), lambda i, s: (0, 0, width // 128)),
+                pl.BlockSpec((2, count, columns), lambda i, s: (jnp.minimum(i, steps - 1), 0, 0)),
+                pl.BlockSpec((2, count, columns), lambda i, s: (jnp.maximum(i - steps, 0), 0, 0)),
+                marks_spec,
+                marks_spec,
                 pl.BlockSpec(router.shape, lambda i, s: (0, 0)),
             ]
-            + [pinned] * 4
-            + [pl.BlockSpec(memory_space=pl.ANY)] * len(held),
+            + [pinned_spec] * 4,
             out_specs=[
                 out_spec(2 * count, 2 * piece),
                 out_spec(pair, width),
-                out_spec(pair, 1),
                 out_spec(pair, length),
-                out_spec(pair, experts),
-                out_spec(pair, experts),
+                out_spec(pair, 128),
             ],
             scratch_shapes=[
                 pltpu.VMEM((width, 2 * piece), bf16),
@@ -786,31 +822,26 @@
         out_shape=[
             jax.ShapeDtypeStruct((2 * length, 2 * piece), bf16),
             jax.ShapeDtypeStruct((2 * rows, width), bf16),
-            jax.ShapeDtypeStruct((2 * rows, 1), f32),
             jax.ShapeDtypeStruct((2 * rows, length), bf16),
-            jax.ShapeDtypeStruct((2 * rows, experts), f32),
-            jax.ShapeDtypeStruct((2 * rows, experts), f32),
+            jax.ShapeDtypeStruct((2 * rows, 128), f32),
         ],
-        input_output_aliases={8 + i: i for i in range(len(held))},
-        compiler_params=pltpu.CompilerParams(vmem_limit_bytes=limit_of(2 * rows)),
+        compiler_params=pltpu.CompilerParams(vmem_limit_bytes=60 * 2**20),
         cost_estimate=pl.CostEstimate(
-            flops=4 * length * width * piece,
-            bytes_accessed=2 * length * width + 4 * width * piece,
+            flops=8 * length * width * piece,
+            bytes_accessed=4 * length * width + 4 * width * piece,
             transcendentals=0,
         ),
         name="front",
-    )(scalars, blocks_of, blocks_of, router, key_weight, value_weight, got_key, got_value, *held)
+    )(scalars, own, other, own, other, router, key_weight, value_weight, got_key, got_value)
 
 
 def shared_out_body(steps, scalars, sums_ref, key_ref, value_ref, got_key_ref, got_value_ref, *outs):
     step = pl.program_id(0)
     sums = sums_ref[...]
-    heads = sums.shape[2] // (2 * HEAD)
+    heads = sums.shape[0] // 2
 
     def part(t, i):
-        return jnp.concatenate(
-            [sums[t, :, (2 * h + i) * HEAD : (2 * h + i + 1) * HEAD] for h in range(heads)], axis=1
-        )
+        return jnp.concatenate([sums[2 * h + i, t] for h in range(heads)], axis=1)
 
     def fill(pair, keys, values):
         for t in range(2):
@@ -831,7 +862,7 @@
 
 
 def shared_out(scalars, sums, key_weight, value_weight, got_key, got_value, tile=512):
-    _, rows, _ = sums.shape
+    rows = sums.shape[2]
     width, piece = got_key.shape
     half, steps = width // 2, width // tile
 
@@ -847,11 +878,11 @@
         grid_spec=pltpu.PrefetchScalarGridSpec(
             num_scalar_prefetch=1,
             grid=(steps,),
-            in_specs=[pl.BlockSpec(sums.shape, lambda j, s: (0, 0, 0)), local, local, sent, sent],
+            in_specs=[pl.BlockSpec(sums.shape, lambda j, s: (0, 0, 0, 0)), local, local, sent, sent],
             out_specs=[theirs, mine, theirs, mine],
         ),
         out_shape=[jax.ShapeDtypeStruct((rows, half), bf16)] * 4,
-        compiler_params=pltpu.CompilerParams(vmem_limit_bytes=limit_of(2 * rows)),
+        compiler_params=pltpu.CompilerParams(vmem_limit_bytes=60 * 2**20),
         cost_estimate=pl.CostEstimate(
             flops=8 * rows * width * piece,
             bytes_accessed=8 * width * piece + 8 * rows * width,
@@ -915,8 +946,6 @@
         experts,
         capacity,
     )
-    own_blocks, arrivals = ring_gather(block, "dp", blocks, 1)
-
     heads_at = (member * 2 + core) * 2 + shard
     holder = (member * 2 + core) // members
     offset = holder * 2 * members
@@ -933,18 +962,24 @@
         columns = lax.dynamic_slice_in_dim(weight, (partner_at - offset) * piece, piece, 1)
         return lax.ppermute(after(columns, block), names, sends)
 
-    local = (shard == holder).astype(jnp.int32)
-    local_at = local * (heads_at - offset)
-    got_key, got_value = partner_columns(key_weight), partner_columns(value_weight)
-    own_blocks, got_key, got_value = lax.optimization_barrier((own_blocks, got_key, got_value))
-    tree_blocks = [own_blocks, swap(own_blocks, "expert")]
-
-    shard_index = jnp.reshape(shard, (1,)).astype(jnp.int32)
+    grad_half = lax.dynamic_slice_in_dim(cotangent[0], shard * half, half, 1)
 
     def pack_rows(values, pack):
         packed = product(pack, values).astype(bf16).reshape(experts, 1, capacity, half)
         packed = jnp.broadcast_to(packed, (experts, members, capacity, half))
         return packed.reshape(blocks, capacity, half)
+
+    works = [None] * (blocks // 2)
+    works[-1] = lambda event: [pack_rows(after(grad_half, event), mlp_pack)]
+    own_blocks, made = ring_gather(block, "dp", blocks, 1, works)
+    grad_packed = made[-1][0]
+    got_key, got_value = partner_columns(key_weight), partner_columns(value_weight)
+    own_blocks, got_key, got_value = lax.optimization_barrier((own_blocks, got_key, got_value))
+    tree_blocks = [own_blocks, swap(own_blocks, "expert")]
+
+    local = (shard == holder).astype(jnp.int32)
+    local_at = local * (heads_at - offset)
+    shard_index = jnp.reshape(shard, (1,)).astype(jnp.int32)
 
     def dispatch(packed, work=None, begin=None):
         arrived = lax.all_to_all(packed, "dp", 0, 0, tiled=True)
@@ -962,13 +997,11 @@
     def join_ends(sides, work=None):
         own, other, *_ = sides(False, None)
         theirs = (own.astype(f32) + swap(other, "expert").astype(f32)).astype(bf16)
-        back = swap(theirs, "shard")
-        own, other, *rest = sides(True, theirs)
-        done = []
-        if work:
-            back, *done = lax.optimization_barrier((back, *work(theirs)))
+        back, own, other, *rest = lax.optimization_barrier(
+            (swap(theirs, "shard"), *sides(True, theirs), *(work(theirs) if work else []))
+        )
         total = own.astype(f32) + swap(other, "expert").astype(f32) + back.astype(f32)
-        return total, rest, done, theirs, own
+        return total, rest
 
     def sum_tokens(back, pack):
         if members > 1:
@@ -986,21 +1019,15 @@
     def for_tokens(joined):
         return joined.astype(bf16).reshape(blocks, capacity, half)
 
-    grad_half = my_half(cotangent[0])
-    grad_packed = after(pack_rows(grad_half, mlp_pack), arrivals[2])
     grad_arrived = lax.all_to_all(grad_packed, "dp", 0, 0, tiled=True)
     grad_arrived = grad_arrived.reshape(blocks * capacity, half)
     scalars = jnp.stack([local, local_at, expert]).astype(jnp.int32)
-    held = ()
-    for t in range(2):
-        held = front(
-            t, held, scalars, tree_blocks[t], attn_router, key_weight, value_weight, got_key, got_value, capacity
-        )
-        if t == 0:
-            grad_got = swap(after(grad_arrived, held[2]), "shard")
-    shared, rows, attn_gate, bias, attn_difference, mlp_difference = held
+    shared, rows, bias, info = front(
+        scalars, *tree_blocks, attn_router, key_weight, value_weight, got_key, got_value, capacity
+    )
+    grad_got = swap(after(grad_arrived, rows), "shard")
     queries = product(rows, query_weight).astype(bf16)
-    mixed, log_total = attend(queries, shared, bias, attn_gate, tiles)
+    mixed, log_total = attend(queries, shared, bias, info, tiles)
     mixed, grad_got = lax.optimization_barrier((mixed, grad_got))
     grad_pieces = (grad_arrived, grad_got, swap(grad_arrived, "expert"), swap(grad_got, "expert"))
 
@@ -1010,7 +1037,7 @@
     def plain_work(event):
         return plain_in(shard_index, after(grad_pieces, event), down_weight)
 
-    attn_joined, _, (grad_rows, plain_grad), *_ = join_ends(attn_sides, plain_work)
+    attn_joined, (grad_rows, plain_grad) = join_ends(attn_sides, plain_work)
     back = send_back(for_tokens(attn_joined))[0]
     inputs = tokens[0].astype(f32)
     attn_scale = lax.rsqrt(jnp.mean(inputs * inputs, axis=1, keepdims=True) + epsilon)
@@ -1029,7 +1056,7 @@
 
     mlp_pieces, _, begun = dispatch(pack_rows(mlp_normed, mlp_pack), None, begin)
     mlp_rows, mlp_gate, mlp_total, gated_hidden, gate_pre_grad, up_pre_grad = expert_in(
-        shard_index, mlp_pieces, mlp_router, mlp_difference, plain_grad, begun, gate_weight, up_weight
+        shard_index, mlp_pieces, mlp_router, info, plain_grad, begun, gate_weight, up_weight
     )
 
     def mlp_sides(mine, event):
@@ -1038,25 +1065,21 @@
             mine,
             after([gate_pre_grad, up_pre_grad], event),
             [gate_weight, up_weight],
-            (mlp_total, mlp_gate, mlp_difference, mlp_router),
+            (mlp_total, mlp_gate, 0, info, MLP, mlp_router),
         )
-
-    def down_work(event):
-        return [product_first(after(grad_rows, event), gated_hidden)]
-
-    row_joined, (mlp_coefs,), (down_grad,), *_ = join_ends(mlp_sides, down_work)
-    row_joined = for_tokens(row_joined)
 
     def term_half(mine, event):
         return rows_half(shard_index, mine, [after(gated_hidden, event)], [down_weight])
 
+    row_joined, (mlp_coefs,) = join_ends(mlp_sides)
+    row_joined = for_tokens(row_joined)
+
     def gate_work(event):
-        gate_grad = product_first(after(mlp_rows, event), gate_pre_grad)
-        own, other = term_half(False, gate_grad)
+        own, other = term_half(False, event)
         theirs = own.astype(f32) + swap(other, "expert").astype(f32)
-        return [gate_grad, theirs.astype(bf16)]
-
-    back, (gate_grad, term_theirs) = send_back(row_joined, gate_work)
+        return [theirs.astype(bf16), product_first(after(mlp_rows, own), gate_pre_grad)]
+
+    back, (term_theirs, gate_grad) = send_back(row_joined, gate_work)
     mlp_normed_grad = sum_tokens(back, mlp_pack)
 
     mlp_n = middle * mlp_scale
@@ -1070,107 +1093,143 @@
     def up_work(event):
         up_grad = product_first(after(mlp_rows, event), up_pre_grad)
         router_part = product_first(mlp_coefs, after(mlp_rows, event).astype(f32))
-        term_back = swap(after(term_theirs, event), "shard")
-        own, other = term_half(True, event)
-        total = own.astype(f32) + swap(other, "expert").astype(f32) + term_back.astype(f32)
-        return [up_grad, router_part, for_tokens(total)]
-
-    term_pieces, (up_grad, mlp_router_part, term_joined), _ = dispatch(
-        pack_rows(low_grad, attn_pack), up_work
-    )
-    term_back = lax.all_to_all(after(term_joined, term_pieces[0]), "dp", 0, 0, tiled=True)
+        return [up_grad, router_part]
+
+    def down_work(own, other):
+        return [product_first(after(grad_rows, own), gated_hidden)]
+
+    packed = pack_rows(low_grad, attn_pack)
+    term_pieces, (up_grad, mlp_router_part), (down_grad,) = dispatch(packed, up_work, down_work)
+    term_back = swap(after(term_theirs, packed), "shard")
+    own, other = term_half(True, packed)
+    total = own.astype(f32) + swap(other, "expert").astype(f32) + term_back.astype(f32)
+    term_joined = after(for_tokens(total), term_pieces[0])
+    term_back = lax.all_to_all(term_joined, "dp", 0, 0, tiled=True)
     term_rows, attn_total, attended_grad = attended_in(
-        shard_index, term_pieces, attn_gate, mixed, output_weight
+        shard_index, term_pieces, info, mixed, output_weight
     )
     query_rows_grad, held = attend_back(queries, shared, bias, log_total, attended_grad, tiles)
     held, term_back = lax.optimization_barrier((held, term_back))
     part = length // experts
-    held = held.reshape(2, experts, part, 2 * piece)
-    key_sums, first_key_sums = ring_scatter(held, experts, members)
-    key_sums = key_sums.astype(bf16)
-
-    def input_sides(mine, event):
+    cut = experts * HEAD // (2 * piece)
+
+    def cut_parts(values):
+        shape = values.shape
+        values = values.reshape(shape[:-1] + (cut, shape[-1] // cut))
+        return jnp.moveaxis(values, -2, 1).reshape((experts,) + shape[1:-1] + (-1,))
+
+    def join_parts(values):
+        shape = values.shape
+        values = jnp.moveaxis(values.reshape((experts // cut, cut) + shape[1:]), 1, -2)
+        return values.reshape(values.shape[:-2] + (-1,))
+
+    rings = None
+    if members > 1:
+        rings = [[e * members + m for e in range(experts)] for m in range(members)]
+
+    def to_experts(values):
+        return lax.all_to_all(values, "dp", 0, 0, axis_index_groups=rings, tiled=True)
+
+    held = cut_parts(held)
+    def input_rows(mine, event):
         return rows_half(
             shard_index,
             mine,
-            [after(query_rows_grad, first_key_sums if event is None else event)],
+            [after(query_rows_grad, event)],
             [query_weight],
-            (attn_total, attn_gate, attn_difference, attn_router),
+            (attn_total, info, GATE, info, ATTN, attn_router),
         )
 
-    def query_work(event):
-        query_grad = product_first(after(rows, event), query_rows_grad)
-        return [query_grad, product_first(after(term_rows, event), mixed)]
-
-    input_joined, (attn_coefs,), (query_grad, output_grad), *_ = join_ends(input_sides, query_work)
-    input_joined = for_tokens(input_joined)
-
-    all_sums, arrivals = ring_gather(key_sums.reshape(2 * part, 2 * piece), "dp", experts, members)
-    all_sums = all_sums.reshape(2 * length, 2 * piece)
-    back = send_back(after(input_joined, key_sums))[0]
-    normed_grad = sum_tokens(after(back, arrivals[2]), attn_pack)
-    layer_out = whole((middle + sum_tokens(term_back, mlp_pack)).astype(bf16))[None]
-    attn_router_part = product_first(attn_coefs, after(rows, arrivals[0]).astype(f32))
-    slots = width // experts
-    normed_part = jnp.stack(
-        [
-            lax.dynamic_slice_in_dim(own, expert * slots, slots, 2).reshape(experts, part, slots)
-            for own in tree_blocks
-        ],
-        axis=1,
-    ).reshape(2 * length, slots)
-    weight_sums = product_first(normed_part, all_sums)
-
+    kept = []
+
+    def theirs_work(event):
+        own, other, _ = input_rows(False, event)
+        theirs = own.astype(f32) + swap(other, "expert").astype(f32)
+        kept.append(theirs.astype(bf16))
+        return kept[:]
+
+    def mine_work(event):
+        kept.append(swap(after(kept[0], event), "shard"))
+        kept.extend(input_rows(True, event))
+        return kept[2:] + [product_first(after(rows, event), query_rows_grad)]
+
+    def output_work(event):
+        return [kept[1], product_first(after(term_rows, event), mixed)]
+
+    works = [None, theirs_work, mine_work, output_work]
+    key_sums, made = ring_scatter(held, experts, members, works)
+    key_sums = key_sums.astype(bf16)
+    _, _, (own, other, attn_coefs, query_grad), (back, output_grad) = made
+    total = own.astype(f32) + swap(other, "expert").astype(f32) + back.astype(f32)
+    input_joined = for_tokens(total)
     scalars = jnp.stack([shard, local, local_at]).astype(jnp.int32)
-    parts = shared_out(
-        scalars,
-        after(key_sums, arrivals[0]),
-        key_weight,
-        value_weight,
-        got_key,
-        got_value,
-    )
-    theirs = parts[0].astype(f32) + swap(parts[2], "expert").astype(f32)
-    back = swap(theirs.astype(bf16), "shard")
-    shared = parts[1].astype(f32) + swap(parts[3], "expert").astype(f32) + back.astype(f32)
+
+    def weight_work(event):
+        sums = after(key_sums, event)
+        sums = sum(product_first(tree_blocks[t].reshape(length, -1), sums[t]) for t in range(2))
+        return [sums[:width].astype(bf16).reshape(experts, width // experts, -1)]
+
+    def shared_work(event):
+        parts = shared_out(
+            scalars, after(token_sums, event), key_weight, value_weight, got_key, got_value
+        )
+        theirs = parts[0].astype(f32) + swap(parts[2], "expert").astype(f32)
+        shared = parts[1].astype(f32) + swap(parts[3], "expert").astype(f32)
+        return [shared, swap(theirs.astype(bf16), "shard")]
+
+    token_sums = key_sums.reshape(2, experts, part, -1).transpose(1, 0, 2, 3)
+    (token_sums,), (weight_sums,) = pinned((to_experts(token_sums),), weight_work, token_sums)
+    token_sums = join_parts(token_sums)
+    input_joined = after(input_joined, token_sums)
+    back = lax.all_to_all(input_joined, "dp", 0, 0, tiled=True)
+    (back,), (shared, theirs) = pinned((back,), shared_work, input_joined)
+    shared = shared + theirs.astype(f32)
     if members > 1:
         groups = [[e * members + m for m in range(members)] for e in range(experts)]
         shared = lax.psum_scatter(
             shared, "dp", scatter_dimension=0, axis_index_groups=groups, tiled=True
         )
-    normed_grad = normed_grad + shared
-
     attn_n = my_half(inputs) * attn_scale
-    weighted = normed_grad * my_half(attn_gain)
-    attn_gain_part = jnp.sum(normed_grad * attn_n, axis=0)
-    tokens_grad = middle_grad + attn_scale * (weighted - attn_n * feature_mean(weighted * attn_n))
-    got = swap(tokens_grad.astype(bf16), "shard").astype(f32)
+    features = width // (2 * blocks)
+
+    def spread(values):
+        return lax.dynamic_update_slice(jnp.zeros((1, width), f32), values[None], (0, shard * half))
+
+    def last_work(event):
+        normed_grad = sum_tokens(after(back, event), attn_pack) + shared
+        weighted = normed_grad * my_half(attn_gain)
+        gain_part = jnp.sum(normed_grad * attn_n, axis=0)
+        grad = middle_grad + attn_scale * (weighted - attn_n * feature_mean(weighted * attn_n))
+        small = [attn_router_part, mlp_router_part, spread(gain_part), spread(mlp_gain_part)]
+        small = jnp.pad(jnp.concatenate(small), ((0, 6), (0, 0)))
+        small = small + swap(small, "shard")
+        small = small.reshape(-1, blocks, 2, features).transpose(2, 1, 0, 3)
+        mine = lax.dynamic_index_in_dim(small, core, 0, keepdims=False)
+        theirs = lax.dynamic_index_in_dim(small, 1 - core, 0, keepdims=False)
+        return [grad, swap(grad.astype(bf16), "shard"), mine + swap(theirs, "expert")]
+
+    attn_router_part = product_first(attn_coefs, after(rows, key_sums).astype(f32))
+    weight_sums = after(weight_sums, back)
+    (weight_sums,), (tokens_grad, got, small) = pinned(
+        (to_experts(weight_sums),), last_work, weight_sums
+    )
+    weight_sums = join_parts(weight_sums)
+    layer_out = whole((middle + sum_tokens(term_back, mlp_pack)).astype(bf16))[None]
+    got = got.astype(f32)
     tokens_grad = jnp.concatenate(
         [jnp.where(shard == 0, tokens_grad, got), jnp.where(shard == 0, got, tokens_grad)], axis=1
     )[None]
-
-    features = width // (2 * blocks)
+    small = jnp.sum(lax.all_to_all(small, "dp", 0, 0, tiled=True), axis=0)
+
     heads = piece // HEAD
-    pieces = weight_sums.astype(bf16).reshape(members, 2, features, 2 * piece)
+    pieces = weight_sums.reshape(2 * heads, members, 2, features, HEAD).transpose(1, 2, 0, 3, 4)
     if members > 1:
-        groups = [[e * members + m for m in range(members)] for e in range(experts)]
         pieces = lax.all_to_all(pieces, "dp", 0, 0, axis_index_groups=groups, tiled=True)
-    pieces = pair_all_to_all(pieces.transpose(1, 0, 2, 3), "expert")
-    pieces = pieces.transpose(1, 0, 2, 3).reshape(2, members, features, 2 * piece)
-    pieces = pair_all_to_all(pieces, "shard").reshape(2, members, features, heads, 2, HEAD)
-    pieces = pieces.transpose(4, 2, 1, 0, 3, 5).reshape(2, features, -1).astype(f32)
-
-    def spread(values):
-        return lax.dynamic_update_slice(jnp.zeros((1, width), f32), values[None], (0, shard * half))
-
-    small = [attn_router_part, mlp_router_part, spread(attn_gain_part), spread(mlp_gain_part)]
-    small = jnp.pad(jnp.concatenate(small), ((0, 6), (0, 0)))
-    small = small + swap(after(small, weight_sums), "shard")
-    small = small.reshape(-1, blocks, 2, features).transpose(2, 1, 0, 3)
-    mine = lax.dynamic_index_in_dim(small, core, 0, keepdims=False)
-    theirs = lax.dynamic_index_in_dim(small, 1 - core, 0, keepdims=False)
-    mine = mine + swap(theirs, "expert")
-    small = jnp.sum(lax.all_to_all(mine, "dp", 0, 0, tiled=True), axis=0)
+    pieces = pair_all_to_all(pieces.transpose(1, 0, 2, 3, 4), "expert")
+    pieces = pieces.transpose(1, 0, 2, 3, 4).reshape(2, members, 2 * heads, features, HEAD)
+    pieces = pair_all_to_all(pieces, "shard").reshape(2, members, heads, 2, features, HEAD)
+    pieces = pieces.transpose(3, 4, 1, 0, 2, 5).reshape(2, features, -1).astype(f32)
+
     return (
         layer_out,
         tokens_grad,

time: 523 us -> 503 us (0.962)
  local copies, waits for them, and re-layouts: 77 us -> 44.3 us
  other arithmetic: 14.3 us -> 32.8 us
  waiting for transfers between devices: 147 us -> 130 us
  matrix products: 50.3 us -> 56.9 us
    ppermute x8 -> x4, waiting for transfers between devices: 36.2 us -> 4.09 us  [ring_gather(): backward = lax.ppermute(backward, axis, left)]
    unnamed x173 -> x145, local copies, waits for them, and re-layouts: 43.8 us -> 25 us
    all_to_all x2 -> x5, starting transfers between devices: 11.7 us -> 26.1 us  [the longest x2 9.56 us: to_experts(): lax.all_to_all(values, 'dp', 0, 0, axis_index_groups=rings, tiled=True)]
    ppermute x8 -> x4, waiting for transfers between devices: 4.02 us -> 17.5 us  [ring_gather(): forward = lax.ppermute(forward, axis, right)]
    dynamic_update_slice x18 -> x9, local copies, waits for them, and re-layouts: 20 us -> 9.69 us  [put(): return lax.dynamic_update_slice(out, piece[None], (source, row, 0))]
    ppermute x14 -> x8, starting transfers between devices: 16.3 us -> 8.4 us  [the longest x4 6.75 us: ring_scatter(): backward = lax.ppermute(backward, 'dp', left)]
    ppermute x34, starting transfers between devices: 15.1 us -> 21.8 us  [swap(): return lax.ppermute(values, axis, [(0, 1), (1, 0)])]
    convert_element_type x12 -> x8, other arithmetic: 4 us -> 10.1 us  [the longest x3 5.58 us: added(): return (own + sent.astype(f32)).astype(bf16)]
  transfers between devices with their start and end apart: 73 -> 61, of which waited for: 38 -> 39; matrix products, arithmetic and copies ran while one was open for 17% -> 19% of each run, Pallas kernels for 17% -> 18%
where the time goes in v3:
time: 503 us; the launch traced here: 498 us
  waiting for transfers between devices  130 us (26%)
  Pallas kernels  118 us (23%)
  starting transfers between devices  92.9 us (18%)
  matrix products  56.9 us (11%)
  local copies, waits for them, and re-layouts  44.3 us (9%)
  other arithmetic  32.8 us (7%)
  blocking collectives  20.5 us (4%)
    ppermute x34, waiting for transfers between devices, swap(): return lax.ppermute(values, axis, [(0, 1), (1, 0)])  52.7 us
    dot_general x13, matrix products, product_first(): lax.dot_general(former, latter, (((0,), (0,)), ((), ())), preferred_eleme...  49.7 us
    pallas_call x8, Pallas kernels, rows_half(): pl.pallas_call(functools.partial(rows_half_body, len(lefts), extra is not...  30.9 us
    unnamed x145, local copies, waits for them, and re-layouts  25 us
    ppermute x4, waiting for transfers between devices, ring_scatter(): backward = lax.ppermute(backward, 'dp', left)  22.1 us
    ppermute x34, starting transfers between devices, swap(): return lax.ppermute(values, axis, [(0, 1), (1, 0)])  21.8 us
    pallas_call x1, Pallas kernels, front(): pl.pallas_call(functools.partial(front_body, capacity, steps), grid_spec=...  21 us
    all_to_all x1, blocking collectives, dispatch(): arrived = lax.all_to_all(packed, 'dp', 0, 0, tiled=True)  20.5 us
  transfers between devices with their start and end apart: 61, of which 39 were waited for; matrix products, arithmetic and copies ran while one was open for 19% of the time, Pallas kernels for 18%

profile of v3, /device:TPU:0, one launch (start us, length us, event | category | flops | bytes accessed | tf_op | source)
XLA Modules:
  0.0 497.6 jit_solution(1325050893635806545)
XLA Ops:
  9.6 4.5 constant_dynamic-slice_fusion.2
  29.5 7.5 %collective-permute-done.2 = bf16[128,2176]{1,0:T(8,128)(2,1)S(1)} collective-permute-done((bf16[128,2176]{1,0:T(8,128)(2,1)}, bf16[128,2176]{1,0:T(8,128)(2,1)S(1)}, u32[]{:S(2)}, u32[]{:S(2)}) %collective-permute-start.2) | collective-permute-done | bytes 557088 | tf_op jit(solution)/shard_map/ppermute | solution.py:101
  41.3 8.4 %collective-permute-done.4 = bf16[128,2176]{1,0:T(8,128)(2,1)S(1)} collective-permute-done((bf16[128,2176]{1,0:T(8,128)(2,1)S(1)}, bf16[128,2176]{1,0:T(8,128)(2,1)S(1)}, u32[]{:S(2)}, u32[]{:S(2)}) %collective-permute-start.4) | collective-permute-done | bytes 557088 | tf_op jit(solution)/shard_map/ppermute | solution.py:101
  64.2 6.1 %all-to-all-start = ((bf16[8,40,1024]{2,1,0:T(8,128)(2,1)}), bf16[8,40,1024]{2,1,0:T(8,128)(2,1)}, u32[]{:S(2)}, u32[]{:S(2)}) async-start(bf16[8,40,1024]{2,1,0:T(8,128)(2,1)} %bitcast.14), calls=%async_computation | async-start | bytes 1310720 | tf_op jit(solution)/shard_map/all_to_all | solution.py:1022
  72.1 21.0 %front.1 = (bf16[2048,1024]{1,0:T(8,128)(2,1)}, bf16[640,2048]{1,0:T(8,128)(2,1)}, bf16[640,1024]{1,0:T(8,128)(2,1)}, f32[640,128]{1,0:T(8,128)}) custom-call(s32[3]{0:T(128)} %pad_add_fusion.scalars, bf16[8,128,2176]{2,1,0:T(8,128)(2,1)} %bitcast_dynamic-update-slice_fusion.7.own_ref.own_marks_ref, ...), custom_call_target="tpu_custom_call" | custom-call | flops 8589934592 | bytes 12582912 | tf_op jit(solution)/shard_map/front/pallas_call | solution.py:798
  99.1 8.4 %attend.1 = (bf16[640,512]{1,0:T(8,128)(2,1)S(1)}, f32[640,128]{1,0:T(8,128)S(1)}) custom-call(bf16[640,512]{1,0:T(8,128)(2,1)S(1)} %convolution_convert_fusion.3.q_ref, bf16[2048,1024]{1,0:T(8,128)(2,1)S(1)} %copy-done.5, bf16[2048,1024]{1,0:T(8,128)(2,1)S(1)} %copy-done.5, bf16[640,1024]{1,0:T(8,128)(2,1)S(1)} %copy-done.18, f32[640,128]{1,0:T(8,128)S(1)} %copy-done), custom_call_target="tpu_custom_call" | custom-call | flops 1342177280 | bytes 5505024 | tf_op jit(solution)/shard_map/attend/pallas_call | solution.py:178
  117.6 6.6 %plain_in.1 = (bf16[640,2048]{1,0:T(8,128)(2,1)S(1)}, bf16[640,1408]{1,0:T(8,128)(2,1)S(1)}) custom-call(s32[1]{0:T(128)} %bitcast.3.shard_ref, bf16[320,1024]{1,0:T(8,128)(2,1)} %bitcast.17.p0, bf16[320,1024]{1,0:T(8,128)(2,1)S(1)} %collective-permute-done.11.p1, bf16[320,1024]{1,0:T(8,128)(2,1)S(1)} %collective-permute-done.14.p2, ...), custom_call_target="tpu_custom_call" | custom-call | flops 3690987520 | bytes 14614528 | tf_op jit(solution)/shard_map/plain_in/pallas_call | solution.py:296
  125.4 6.0 %collective-permute-done.13 = bf16[320,1024]{1,0:T(8,128)(2,1)S(1)} collective-permute-done((bf16[320,1024]{1,0:T(8,128)(2,1)S(1)}, bf16[320,1024]{1,0:T(8,128)(2,1)S(1)}, u32[]{:S(2)}, u32[]{:S(2)}) %collective-permute-start.13) | collective-permute-done | bytes 655392 | tf_op jit(solution)/shard_map/ppermute | solution.py:41
  134.7 6.0 %all-to-all-start.1 = ((bf16[8,40,1024]{2,1,0:T(8,128)(2,1)}), bf16[8,40,1024]{2,1,0:T(8,128)(2,1)}, u32[]{:S(2)}, u32[]{:S(2)}) async-start(bf16[8,40,1024]{2,1,0:T(8,128)(2,1)} %bitcast.191), calls=%async_computation.1 | async-start | bytes 1310720 | tf_op jit(solution)/shard_map/all_to_all | solution.py:1013
  141.8 16.6 %all-to-all-done.1 = bf16[8,40,1024]{2,1,0:T(8,128)(2,1)} async-done(((bf16[8,40,1024]{2,1,0:T(8,128)(2,1)}), bf16[8,40,1024]{2,1,0:T(8,128)(2,1)}, u32[]{:S(2)}, u32[]{:S(2)}) %all-to-all-start.1) | async-done | bytes 655392 | tf_op jit(solution)/shard_map/all_to_all | solution.py:1013
  164.1 20.5 %all_to_all.50 = bf16[8,40,1024]{2,1,0:T(8,128)(2,1)} all-to-all(bf16[8,40,1024]{2,1,0:T(8,128)(2,1)S(1)} %bitcast.193), channel_id=1, replica_groups=mesh['dp'=8,'expert'=2,'shard'=2] {'dp'}, dimensions={0} | all-to-all | bytes 1310720 | tf_op jit(solution)/shard_map/all_to_all | solution.py:985
  187.0 8.9 %expert_begin.1 = (bf16[640,1408]{1,0:T(8,128)(2,1)}, bf16[640,1408]{1,0:T(8,128)(2,1)}) custom-call(s32[1]{0:T(128)} %bitcast.3.shard_ref, bf16[320,1024]{1,0:T(8,128)(2,1)} %bitcast.23.p0, bf16[320,1024]{1,0:T(8,128)(2,1)} %collective-permute-done.19.p2, bf16[2048,1408]{1,0:T(8,128)(2,1)} %refs_2_.3, bf16[2048,1408]{1,0:T(8,128)(2,1)} %refs_3_.3), custom_call_target="tpu_custom_call" | custom-call | flops 3690987520 | bytes 15597568 | tf_op jit(solution)/shard_map/expert_begin/pallas_call | solution.py:351
  195.8 6.2 %collective-permute-done.18.p1 = bf16[320,1024]{1,0:T(8,128)(2,1)} collective-permute-done((bf16[320,1024]{1,0:T(8,128)(2,1)}, bf16[320,1024]{1,0:T(8,128)(2,1)}, u32[]{:S(2)}, u32[]{:S(2)}) %collective-permute-start.18) | collective-permute-done | bytes 655392 | tf_op jit(solution)/shard_map/ppermute | solution.py:41
  204.4 15.0 %expert_in.1 = (bf16[640,2048]{1,0:T(8,128)(2,1)}, f32[640,128]{1,0:T(8,128)}, f32[640,128]{1,0:T(8,128)}, bf16[640,1408]{1,0:T(8,128)(2,1)}, bf16[640,1408]{1,0:T(8,128)(2,1)}, /*index=5*/bf16[640,1408]{1,0:T(8,128)(2,1)}) custom-call(s32[1]{0:T(128)} %bitcast.3.shard_ref, bf16[320,1024]{1,0:T(8,128)(2,1)} %bitcast.23.p0, ...), custom_call_target="tpu_custom_call" | custom-call | flops 3690987520 | bytes 27230208 | tf_op jit(solution)/shard_map/expert_in/pallas_call | solution.py:431
  219.4 9.4 %rows_theirs.5 = (bf16[320,1024]{1,0:T(8,128)(2,1)}, bf16[320,1024]{1,0:T(8,128)(2,1)}, f32[640,8]{1,0:T(8,128)}) custom-call(s32[1]{0:T(128)} %bitcast.3.shard_ref, bf16[640,1408]{1,0:T(8,128)(2,1)} %get-tuple-element.200.refs_0_, bf16[640,1408]{1,0:T(8,128)(2,1)} %get-tuple-element.201.refs_1_, bf16[2048,1408]{1,0:T(8,128)(2,1)} %refs_2_.3, ...), custom_call_target="tpu_custom_call" | custom-call | flops 3690987520 | bytes 10682368 | tf_op jit(solution)/shard_map/rows_theirs/pallas_call | solution.py:586
  235.0 9.4 %rows_mine.5 = (bf16[320,1024]{1,0:T(8,128)(2,1)}, bf16[320,1024]{1,0:T(8,128)(2,1)}, f32[640,8]{1,0:T(8,128)}) custom-call(s32[1]{0:T(128)} %bitcast.3.shard_ref, bf16[640,1408]{1,0:T(8,128)(2,1)} %get-tuple-element.200.refs_0_, bf16[640,1408]{1,0:T(8,128)(2,1)} %get-tuple-element.201.refs_1_, bf16[2048,1408]{1,0:T(8,128)(2,1)} %refs_2_.3, ...), custom_call_target="tpu_custom_call" | custom-call | flops 3690987520 | bytes 10682368 | tf_op jit(solution)/shard_map/rows_mine/pallas_call | solution.py:586
  244.4 6.0 %collective-permute-done.22 = bf16[320,1024]{1,0:T(8,128)(2,1)} collective-permute-done((bf16[320,1024]{1,0:T(8,128)(2,1)}, bf16[320,1024]{1,0:T(8,128)(2,1)}, u32[]{:S(2)}, u32[]{:S(2)}) %collective-permute-start.22) | collective-permute-done | bytes 655392 | tf_op jit(solution)/shard_map/ppermute | solution.py:41
  255.2 4.6 all-to-all-start.3
  266.7 7.8 %fusion.29 = f32[2048,1408]{1,0:T(8,128)} fusion(bf16[640,2048]{1,0:T(8,128)(2,1)S(1)} %copy-done.45, bf16[640,1408]{1,0:T(8,128)(2,1)S(1)} %copy-done.40), kind=kOutput, calls=%fused_computation.115 | convolution fusion | flops 3690987520 | bytes 15958016 | tf_op jit(solution)/shard_map/dot_general | solution.py:31
  285.6 4.2 all-to-all-start.4
  299.7 7.8 %fusion.30 = f32[2048,1408]{1,0:T(8,128)} fusion(bf16[640,2048]{1,0:T(8,128)(2,1)S(1)} %copy-done.46, bf16[640,1408]{1,0:T(8,128)(2,1)S(1)} %copy-done.39), kind=kOutput, calls=%fused_computation.116 | convolution fusion | flops 3690987520 | bytes 15958016 | tf_op jit(solution)/shard_map/dot_general | solution.py:31
  309.2 6.1 %all-to-all-start.5 = ((bf16[8,40,1024]{2,1,0:T(8,128)(2,1)}), bf16[8,40,1024]{2,1,0:T(8,128)(2,1)}, u32[]{:S(2)}, u32[]{:S(2)}) async-start(bf16[8,40,1024]{2,1,0:T(8,128)(2,1)} %bitcast.30), calls=%async_computation.5 | async-start | bytes 1310720 | tf_op jit(solution)/shard_map/all_to_all | solution.py:1107
  315.3 9.7 %fusion.32 = f32[2048,1408]{1,0:T(8,128)} fusion(bf16[640,2048]{1,0:T(8,128)(2,1)} %copy-done.35, bf16[640,1408]{1,0:T(8,128)(2,1)} %get-tuple-element.223.refs_0_), kind=kOutput, calls=%fused_computation.118 | convolution fusion | flops 3690987520 | bytes 15958016 | tf_op jit(solution)/shard_map/dot_general | solution.py:31
  334.8 14.8 %attend_back.1 = (bf16[640,512]{1,0:T(8,128)(2,1)}, bf16[8,2,1024,128]{3,2,1,0:T(8,128)(2,1)}) custom-call(bf16[640,512]{1,0:T(8,128)(2,1)} %copy-done.23, bf16[2048,1024]{1,0:T(8,128)(2,1)} %get-tuple-element.165.k_ref.v_ref, bf16[2048,1024]{1,0:T(8,128)(2,1)} %get-tuple-element.165.k_ref.v_ref, bf16[640,1024]{1,0:T(8,128)(2,1)} %get-tuple-element.166.bias_ref, ...), custom_call_target="tpu_custom_call" | custom-call | flops 3355443200 | bytes 9699328 | tf_op jit(solution)/shard_map/attend_back/pallas_call | solution.py:236
  353.0 6.4 %collective-permute-done.33 = bf16[1,1024,128]{2,1,0:T(8,128)(2,1)S(1)} collective-permute-done((bf16[1,1024,128]{2,1,0:T(8,128)(2,1)S(1)}, bf16[1,1024,128]{2,1,0:T(8,128)(2,1)S(1)}, u32[]{:S(2)}, u32[]{:S(2)}) %collective-permute-start.33) | collective-permute-done | bytes 262176 | tf_op jit(solution)/shard_map/ppermute | solution.py:146
  368.6 10.5 %collective-permute-done.35 = bf16[2,1024,128]{2,1,0:T(8,128)(2,1)S(1)} collective-permute-done((bf16[2,1024,128]{2,1,0:T(8,128)(2,1)S(1)}, bf16[2,1024,128]{2,1,0:T(8,128)(2,1)S(1)}, u32[]{:S(2)}, u32[]{:S(2)}) %collective-permute-start.35) | collective-permute-done | bytes 524320 | tf_op jit(solution)/shard_map/ppermute | solution.py:146
  430.0 4.5 all-to-all-start.7
  434.5 8.0 %shared_out.1 = (bf16[128,1024]{1,0:T(8,128)(2,1)}, bf16[128,1024]{1,0:T(8,128)(2,1)}, bf16[128,1024]{1,0:T(8,128)(2,1)}, bf16[128,1024]{1,0:T(8,128)(2,1)}) custom-call(s32[3]{0:T(128)} %pad_add_fusion.1.scalars, bf16[8,2,128,128]{3,2,1,0:T(8,128)(2,1)} %copy-done.49, bf16[2048,1024]{1,0:T(8,128)(2,1)} %key_ref.1, bf16[2048,1024]{1,0:T(8,128)(2,1)} %value_ref.1, ...), custom_call_target="tpu_custom_call" | custom-call | flops 1073741824 | bytes 10485760 | tf_op jit(solution)/shard_map/shared_out/pallas_call | solution.py:876
  449.9 4.4 collective-permute-done.45
  455.0 6.0 %all-to-all-start.8 = ((bf16[8,256,128]{2,1,0:T(8,128)(2,1)}), bf16[8,256,128]{2,1,0:T(8,128)(2,1)S(1)}, u32[]{:S(2)}, u32[]{:S(2)}) async-start(bf16[8,256,128]{2,1,0:T(8,128)(2,1)} %bitcast.48), calls=%async_computation.8 | async-start | bytes 1048576 | tf_op jit(solution)/shard_map/all_to_all | solution.py:1131
  474.9 6.0 %all-to-all-start.9 = ((f32[8,24,128]{2,1,0:T(8,128)}), f32[8,24,128]{2,1,0:T(8,128)S(1)}, u32[]{:S(2)}, u32[]{:S(2)}) async-start(f32[8,24,128]{2,1,0:T(8,128)} %fusion.25), calls=%async_computation.9 | async-start | bytes 196608 | tf_op jit(solution)/shard_map/all_to_all | solution.py:1222
  482.2 5.8 %all-to-all-done.9 = f32[8,24,128]{2,1,0:T(8,128)S(1)} async-done(((f32[8,24,128]{2,1,0:T(8,128)}), f32[8,24,128]{2,1,0:T(8,128)S(1)}, u32[]{:S(2)}, u32[]{:S(2)}) %all-to-all-start.9) | async-done | bytes 98336 | tf_op jit(solution)/shard_map/all_to_all | solution.py:1222
  (338 shorter events, 222.7 us)
Async XLA Ops:
  6.4 16.1 %collective-permute-start.1 = (bf16[128,2176]{1,0:T(8,128)(2,1)S(1)}, bf16[128,2176]{1,0:T(8,128)(2,1)}, u32[]{:S(2)}, u32[]{:S(2)}) collective-permute-start(bf16[128,2176]{1,0:T(8,128)(2,1)S(1)} %get-tuple-element.148), channel_id=1, source_target_pairs={{0,4},{8,0},{16,8},{24,16},{28,24},{20,28},{12,20},{4,12},{1,5},{9... | collective-permute-start | bytes 1671176 | tf_op jit(solution)/shard_map/ppermute | solution.py:102
  9.5 14.2 %collective-permute-start = (bf16[128,2176]{1,0:T(8,128)(2,1)S(1)}, bf16[128,2176]{1,0:T(8,128)(2,1)}, u32[]{:S(2)}, u32[]{:S(2)}) collective-permute-start(bf16[128,2176]{1,0:T(8,128)(2,1)S(1)} %get-tuple-element.148), channel_id=1, source_target_pairs={{0,8},{8,16},{16,24},{24,28},{28,20},{20,12},{12,4},{4,0},{1,9},{9... | collective-permute-start | bytes 1671176 | tf_op jit(solution)/shard_map/ppermute | solution.py:101
  14.1 46.2 %collective-permute-start.8 = (bf16[2048,512]{1,0:T(8,128)(2,1)}, bf16[2048,512]{1,0:T(8,128)(2,1)S(1)}, u32[]{:S(2)}, u32[]{:S(2)}) collective-permute-start(bf16[2048,512]{1,0:T(8,128)(2,1)} %get-tuple-element.159), channel_id=1, source_target_pairs={{0,1},{3,2},{4,5},{7,6},{8,9},{11,10},{12,13},{15,14},{16,17},{19,... | collective-permute-start | bytes 6291464 | tf_op jit(solution)/shard_map/ppermute | solution.py:963
  18.0 46.2 %collective-permute-start.9 = (bf16[2048,512]{1,0:T(8,128)(2,1)}, bf16[2048,512]{1,0:T(8,128)(2,1)}, u32[]{:S(2)}, u32[]{:S(2)}) collective-permute-start(bf16[2048,512]{1,0:T(8,128)(2,1)} %get-tuple-element.160), channel_id=1, source_target_pairs={{0,1},{3,2},{4,5},{7,6},{8,9},{11,10},{12,13},{15,14},{16,17},{19,... | collective-permute-start | bytes 6291464 | tf_op jit(solution)/shard_map/ppermute | solution.py:963
  23.6 13.4 %collective-permute-start.2 = (bf16[128,2176]{1,0:T(8,128)(2,1)}, bf16[128,2176]{1,0:T(8,128)(2,1)S(1)}, u32[]{:S(2)}, u32[]{:S(2)}) collective-permute-start(bf16[128,2176]{1,0:T(8,128)(2,1)} %collective-permute-done), channel_id=1, source_target_pairs={{0,8},{8,16},{16,24},{24,28},{28,20},{20,12},{12,4},{4,0},{1,9},{9... | collective-permute-start | bytes 1671176 | tf_op jit(solution)/shard_map/ppermute | solution.py:101
  24.2 13.3 %collective-permute-start.3 = (bf16[128,2176]{1,0:T(8,128)(2,1)}, bf16[128,2176]{1,0:T(8,128)(2,1)S(1)}, u32[]{:S(2)}, u32[]{:S(2)}) collective-permute-start(bf16[128,2176]{1,0:T(8,128)(2,1)} %collective-permute-done.1), channel_id=1, source_target_pairs={{0,4},{8,0},{16,8},{24,16},{28,24},{20,28},{12,20},{4,12},{1,5},{9... | collective-permute-start | bytes 1671176 | tf_op jit(solution)/shard_map/ppermute | solution.py:102
  37.5 12.2 %collective-permute-start.4 = (bf16[128,2176]{1,0:T(8,128)(2,1)S(1)}, bf16[128,2176]{1,0:T(8,128)(2,1)S(1)}, u32[]{:S(2)}, u32[]{:S(2)}) collective-permute-start(bf16[128,2176]{1,0:T(8,128)(2,1)S(1)} %collective-permute-done.2), channel_id=1, source_target_pairs={{0,8},{8,16},{16,24},{24,28},{28,20},{20,12},{12,4},{4,0},{1,9},{9... | collective-permute-start | bytes 1671176 | tf_op jit(solution)/shard_map/ppermute | solution.py:101
  39.0 12.7 %collective-permute-start.5 = (bf16[128,2176]{1,0:T(8,128)(2,1)S(1)}, bf16[128,2176]{1,0:T(8,128)(2,1)S(1)}, u32[]{:S(2)}, u32[]{:S(2)}) collective-permute-start(bf16[128,2176]{1,0:T(8,128)(2,1)S(1)} %collective-permute-done.3), channel_id=1, source_target_pairs={{0,4},{8,0},{16,8},{24,16},{28,24},{20,28},{12,20},{4,12},{1,5},{9... | collective-permute-start | bytes 1671176 | tf_op jit(solution)/shard_map/ppermute | solution.py:102
  64.2 28.9 %all-to-all-start = ((bf16[8,40,1024]{2,1,0:T(8,128)(2,1)}), bf16[8,40,1024]{2,1,0:T(8,128)(2,1)}, u32[]{:S(2)}, u32[]{:S(2)}) async-start(bf16[8,40,1024]{2,1,0:T(8,128)(2,1)} %bitcast.14), calls=%async_computation | async-start | bytes 1310720 | tf_op jit(solution)/shard_map/all_to_all | solution.py:1022
  93.1 17.8 %collective-permute-start.11 = (bf16[320,1024]{1,0:T(8,128)(2,1)}, bf16[320,1024]{1,0:T(8,128)(2,1)S(1)}, u32[]{:S(2)}, u32[]{:S(2)}) collective-permute-start(bf16[320,1024]{1,0:T(8,128)(2,1)} %bitcast.17.p0), channel_id=1, source_target_pairs={{0,1},{1,0},{2,3},{3,2},{4,5},{5,4},{6,7},{7,6},{8,9},{9,8},{10,11... | collective-permute-start | bytes 1966088 | tf_op jit(solution)/shard_map/ppermute | solution.py:41
  114.6 16.8 %collective-permute-start.13 = (bf16[320,1024]{1,0:T(8,128)(2,1)S(1)}, bf16[320,1024]{1,0:T(8,128)(2,1)S(1)}, u32[]{:S(2)}, u32[]{:S(2)}) collective-permute-start(bf16[320,1024]{1,0:T(8,128)(2,1)S(1)} %add_convert_fusion.7), channel_id=1, source_target_pairs={{0,1},{1,0},{2,3},{3,2},{4,5},{5,4},{6,7},{7,6},{8,9},{9,8},{10,11... | collective-permute-start | bytes 1966088 | tf_op jit(solution)/shard_map/ppermute | solution.py:41
  134.7 23.7 %all-to-all-start.1 = ((bf16[8,40,1024]{2,1,0:T(8,128)(2,1)}), bf16[8,40,1024]{2,1,0:T(8,128)(2,1)}, u32[]{:S(2)}, u32[]{:S(2)}) async-start(bf16[8,40,1024]{2,1,0:T(8,128)(2,1)} %bitcast.191), calls=%async_computation.1 | async-start | bytes 1310720 | tf_op jit(solution)/shard_map/all_to_all | solution.py:1013
  184.5 17.5 %collective-permute-start.18 = (bf16[320,1024]{1,0:T(8,128)(2,1)}, bf16[320,1024]{1,0:T(8,128)(2,1)}, u32[]{:S(2)}, u32[]{:S(2)}) collective-permute-start(bf16[320,1024]{1,0:T(8,128)(2,1)} %bitcast.23.p0), channel_id=1, source_target_pairs={{0,1},{1,0},{2,3},{3,2},{4,5},{5,4},{6,7},{7,6},{8,9},{9,8},{10,11... | collective-permute-start | bytes 1966088 | tf_op jit(solution)/shard_map/ppermute | solution.py:41
  233.4 17.1 %collective-permute-start.22 = (bf16[320,1024]{1,0:T(8,128)(2,1)}, bf16[320,1024]{1,0:T(8,128)(2,1)}, u32[]{:S(2)}, u32[]{:S(2)}) collective-permute-start(bf16[320,1024]{1,0:T(8,128)(2,1)} %add_convert_fusion.5), channel_id=1, source_target_pairs={{0,1},{1,0},{2,3},{3,2},{4,5},{5,4},{6,7},{7,6},{8,9},{9,8},{10,11... | collective-permute-start | bytes 1966088 | tf_op jit(solution)/shard_map/ppermute | solution.py:41
  255.2 22.5 %all-to-all-start.3 = ((bf16[8,40,1024]{2,1,0:T(8,128)(2,1)}), bf16[8,40,1024]{2,1,0:T(8,128)(2,1)}, u32[]{:S(2)}, u32[]{:S(2)}) async-start(bf16[8,40,1024]{2,1,0:T(8,128)(2,1)} %bitcast.190), calls=%async_computation.3 | async-start | bytes 1310720 | tf_op jit(solution)/shard_map/all_to_all | solution.py:1013
  285.6 23.0 %all-to-all-start.4 = ((bf16[8,40,1024]{2,1,0:T(8,128)(2,1)}), bf16[8,40,1024]{2,1,0:T(8,128)(2,1)}, u32[]{:S(2)}, u32[]{:S(2)}) async-start(bf16[8,40,1024]{2,1,0:T(8,128)(2,1)} %bitcast.189), calls=%async_computation.4 | async-start | bytes 1310720 | tf_op jit(solution)/shard_map/all_to_all | solution.py:985
  289.8 17.7 %collective-permute-start.30 = (bf16[320,1024]{1,0:T(8,128)(2,1)}, bf16[320,1024]{1,0:T(8,128)(2,1)S(1)}, u32[]{:S(2)}, u32[]{:S(2)}) collective-permute-start(bf16[320,1024]{1,0:T(8,128)(2,1)} %add_convert_fusion.3), channel_id=1, source_target_pairs={{0,1},{1,0},{2,3},{3,2},{4,5},{5,4},{6,7},{7,6},{8,9},{9,8},{10,11... | collective-permute-start | bytes 1966088 | tf_op jit(solution)/shard_map/ppermute | solution.py:41
  308.7 17.5 %collective-permute-start.27 = (bf16[320,1024]{1,0:T(8,128)(2,1)}, bf16[320,1024]{1,0:T(8,128)(2,1)}, u32[]{:S(2)}, u32[]{:S(2)}) collective-permute-start(bf16[320,1024]{1,0:T(8,128)(2,1)} %bitcast.29.p0), channel_id=1, source_target_pairs={{0,2},{2,0},{1,3},{3,1},{4,6},{6,4},{5,7},{7,5},{8,10},{10,8},{9,1... | collective-permute-start | bytes 1966088 | tf_op jit(solution)/shard_map/ppermute | solution.py:41
  308.9 17.2 %collective-permute-start.26 = (bf16[320,1024]{1,0:T(8,128)(2,1)}, bf16[320,1024]{1,0:T(8,128)(2,1)}, u32[]{:S(2)}, u32[]{:S(2)}) collective-permute-start(bf16[320,1024]{1,0:T(8,128)(2,1)} %bitcast.29.p0), channel_id=1, source_target_pairs={{0,1},{1,0},{2,3},{3,2},{4,5},{5,4},{6,7},{7,6},{8,9},{9,8},{10,11... | collective-permute-start | bytes 1966088 | tf_op jit(solution)/shard_map/ppermute | solution.py:41
  309.2 40.4 %all-to-all-start.5 = ((bf16[8,40,1024]{2,1,0:T(8,128)(2,1)}), bf16[8,40,1024]{2,1,0:T(8,128)(2,1)}, u32[]{:S(2)}, u32[]{:S(2)}) async-start(bf16[8,40,1024]{2,1,0:T(8,128)(2,1)} %bitcast.30), calls=%async_computation.5 | async-start | bytes 1310720 | tf_op jit(solution)/shard_map/all_to_all | solution.py:1107
  364.7 14.4 %collective-permute-start.34 = (bf16[2,1024,128]{2,1,0:T(8,128)(2,1)S(1)}, bf16[2,1024,128]{2,1,0:T(8,128)(2,1)S(1)}, u32[]{:S(2)}, u32[]{:S(2)}) collective-permute-start(bf16[2,1024,128]{2,1,0:T(8,128)(2,1)S(1)} %get-tuple-element.319), channel_id=1, source_target_pairs={{0,8},{8,16},{16,24},{24,28},{28,20},{20,12},{12,4},{4,0},{1,9},{9... | collective-permute-start | bytes 1572872 | tf_op jit(solution)/shard_map/ppermute | solution.py:145
  365.0 14.1 %collective-permute-start.35 = (bf16[2,1024,128]{2,1,0:T(8,128)(2,1)S(1)}, bf16[2,1024,128]{2,1,0:T(8,128)(2,1)S(1)}, u32[]{:S(2)}, u32[]{:S(2)}) collective-permute-start(bf16[2,1024,128]{2,1,0:T(8,128)(2,1)S(1)} %get-tuple-element.318), channel_id=1, source_target_pairs={{0,4},{8,0},{16,8},{24,16},{28,24},{20,28},{12,20},{4,12},{1,5},{9... | collective-permute-start | bytes 1572872 | tf_op jit(solution)/shard_map/ppermute | solution.py:146
  381.5 13.8 %collective-permute-start.38 = (bf16[2,1024,128]{2,1,0:T(8,128)(2,1)}, bf16[2,1024,128]{2,1,0:T(8,128)(2,1)}, u32[]{:S(2)}, u32[]{:S(2)}) collective-permute-start(bf16[2,1024,128]{2,1,0:T(8,128)(2,1)} %get-tuple-element.316), channel_id=1, source_target_pairs={{0,4},{8,0},{16,8},{24,16},{28,24},{20,28},{12,20},{4,12},{1,5},{9... | collective-permute-start | bytes 1572872 | tf_op jit(solution)/shard_map/ppermute | solution.py:146
  383.2 13.3 %collective-permute-start.37 = (bf16[2,1024,128]{2,1,0:T(8,128)(2,1)}, bf16[2,1024,128]{2,1,0:T(8,128)(2,1)}, u32[]{:S(2)}, u32[]{:S(2)}) collective-permute-start(bf16[2,1024,128]{2,1,0:T(8,128)(2,1)} %get-tuple-element.317), channel_id=1, source_target_pairs={{0,8},{8,16},{16,24},{24,28},{28,20},{20,12},{12,4},{4,0},{1,9},{9... | collective-permute-start | bytes 1572872 | tf_op jit(solution)/shard_map/ppermute | solution.py:145
  384.2 23.1 %collective-permute-start.41 = (bf16[320,1024]{1,0:T(8,128)(2,1)}, bf16[320,1024]{1,0:T(8,128)(2,1)S(1)}, u32[]{:S(2)}, u32[]{:S(2)}) collective-permute-start(bf16[320,1024]{1,0:T(8,128)(2,1)} %add_convert_fusion.1), channel_id=1, source_target_pairs={{0,1},{1,0},{2,3},{3,2},{4,5},{5,4},{6,7},{7,6},{8,9},{9,8},{10,11... | collective-permute-start | bytes 1966088 | tf_op jit(solution)/shard_map/ppermute | solution.py:41
  398.3 12.1 %collective-permute-start.40 = (bf16[2,1024,128]{2,1,0:T(8,128)(2,1)S(1)}, bf16[2,1024,128]{2,1,0:T(8,128)(2,1)S(1)}, u32[]{:S(2)}, u32[]{:S(2)}) collective-permute-start(bf16[2,1024,128]{2,1,0:T(8,128)(2,1)S(1)} %get-tuple-element.314), channel_id=1, source_target_pairs={{0,4},{8,0},{16,8},{24,16},{28,24},{20,28},{12,20},{4,12},{1,5},{9... | collective-permute-start | bytes 1572872 | tf_op jit(solution)/shard_map/ppermute | solution.py:146
  402.7 40.0 %collective-permute-start.31 = (bf16[128,1024]{1,0:T(8,128)(2,1)}, bf16[128,1024]{1,0:T(8,128)(2,1)S(1)}, u32[]{:S(2)}, u32[]{:S(2)}) collective-permute-start(bf16[128,1024]{1,0:T(8,128)(2,1)} %fusion), channel_id=1, source_target_pairs={{0,1},{1,0},{2,3},{3,2},{4,5},{5,4},{6,7},{7,6},{8,9},{9,8},{10,11... | collective-permute-start | bytes 786440 | tf_op jit(solution)/shard_map/ppermute | solution.py:41
  403.4 22.2 %collective-permute-start.42 = (bf16[320,1024]{1,0:T(8,128)(2,1)}, bf16[320,1024]{1,0:T(8,128)(2,1)}, u32[]{:S(2)}, u32[]{:S(2)}) collective-permute-start(bf16[320,1024]{1,0:T(8,128)(2,1)} %get-tuple-element.255), channel_id=1, source_target_pairs={{0,2},{2,0},{1,3},{3,1},{4,6},{6,4},{5,7},{7,5},{8,10},{10,8},{9,1... | collective-permute-start | bytes 1966088 | tf_op jit(solution)/shard_map/ppermute | solution.py:41
  413.9 16.1 %all-to-all-start.6 = ((bf16[8,2,128,128]{3,2,1,0:T(8,128)(2,1)}), bf16[8,2,128,128]{3,2,1,0:T(8,128)(2,1)S(1)}, u32[]{:S(2)}, u32[]{:S(2)}) async-start(bf16[8,2,128,128]{3,2,1,0:T(8,128)(2,1)} %bitcast.182), calls=%async_computation.6 | async-start | bytes 1048576 | tf_op jit(solution)/shard_map/all_to_all | solution.py:1131
  430.0 24.4 %all-to-all-start.7 = ((bf16[8,40,1024]{2,1,0:T(8,128)(2,1)}), bf16[8,40,1024]{2,1,0:T(8,128)(2,1)S(1)}, u32[]{:S(2)}, u32[]{:S(2)}) async-start(bf16[8,40,1024]{2,1,0:T(8,128)(2,1)} %bitcast.49), calls=%async_computation.7 | async-start | bytes 1310720 | tf_op jit(solution)/shard_map/all_to_all | solution.py:1184
  455.0 19.9 %all-to-all-start.8 = ((bf16[8,256,128]{2,1,0:T(8,128)(2,1)}), bf16[8,256,128]{2,1,0:T(8,128)(2,1)S(1)}, u32[]{:S(2)}, u32[]{:S(2)}) async-start(bf16[8,256,128]{2,1,0:T(8,128)(2,1)} %bitcast.48), calls=%async_computation.8 | async-start | bytes 1048576 | tf_op jit(solution)/shard_map/all_to_all | solution.py:1131
  474.9 13.1 %all-to-all-start.9 = ((f32[8,24,128]{2,1,0:T(8,128)}), f32[8,24,128]{2,1,0:T(8,128)S(1)}, u32[]{:S(2)}, u32[]{:S(2)}) async-start(f32[8,24,128]{2,1,0:T(8,128)} %fusion.25), calls=%async_computation.9 | async-start | bytes 196608 | tf_op jit(solution)/shard_map/all_to_all | solution.py:1222
  (98 other events, 1230.3 us)

commit v4 on v3

--- a/solution.py
+++ b/solution.py
@@ -372,12 +372,14 @@
 
 
 def expert_in_body(
-    columns, shard_ref, p0, p1, p2, p3, router_ref, info_ref, plain_ref, gp_ref, up_ref, gw_ref, uw_ref,
-    x_ref, gate_ref, total_ref, hidden_ref, dgate_ref, dup_ref, their_ref, sems,
+    columns, tiles, shard_ref, p0, p1, p2, p3, router_ref, info_ref, plain_ref, gp_ref, up_ref, gw_ref, uw_ref,
+    g_ref, u_ref, r_ref, x_ref, gate_ref, total_ref, hidden_ref, dgate_ref, dup_ref, own_ref, other_ref,
+    their_ref, dgate_all, dup_all, coef_ref, sems,
 ):
     tile = gw_ref.shape[1]
     rows = p0.shape[0]
     step = pl.program_id(0)
+    difference = info_ref[:, MLP : MLP + router_ref.shape[1]]
 
     @pl.when(step == 0)
     def _():
@@ -391,15 +393,14 @@
         for copy in copies:
             copy.wait()
         logits = product(x_ref[...], router_ref[...])
-        difference = info_ref[:, MLP : MLP + router_ref.shape[1]]
         gate = jax.nn.sigmoid(jnp.sum(logits * difference, axis=1, keepdims=True))
         gate_ref[...] = jnp.broadcast_to(gate, gate_ref.shape)
         total_ref[...] = jnp.zeros_like(total_ref)
 
     chunk = chunk_of(x_ref.shape[0])
-
-    @pl.loop(0, x_ref.shape[0] // chunk)
-    def _(i):
+    at = pl.ds(pl.multiple_of(jnp.minimum(step, tiles - 1) * tile, 128), tile)
+
+    def first_part(i):
         here = pl.ds(pl.multiple_of(i * chunk, 16), chunk)
         their = their_ref[here, :]
         gate_pre = gp_ref[here, :].astype(f32) + product(their, gw_ref[...])
@@ -417,22 +418,50 @@
         hidden_grad = gate * plain
         up_grad = hidden_grad * silu
         dup_ref[here, :] = up_grad.astype(bf16)
+        dup_all[here, at] = up_grad.astype(bf16)
         gate_grad = hidden_grad * up_pre * (sigmoid + silu * (1.0 - sigmoid))
         dgate_ref[here, :] = gate_grad.astype(bf16)
-
-
-def expert_in(shard, pieces, router, info, plain, begun, gate_weight, up_weight, tile=256):
+        dgate_all[here, at] = gate_grad.astype(bf16)
+
+    @pl.when(step < tiles)
+    def _():
+        pl.loop(0, x_ref.shape[0] // chunk)(first_part)
+
+    @pl.when(step == tiles)
+    def _():
+        coef_ref[...] = (1.0 - gate_ref[:, :1]) * total_ref[:, :1] * difference
+
+    @pl.when(step >= tiles)
+    def _():
+        for t, out_ref in enumerate((own_ref, other_ref)):
+            here = pl.ds(t * rows, rows)
+            value = product_last(dgate_all[here, :columns], g_ref[...])
+            value = value + product_last(dup_all[here, :columns], u_ref[...])
+            value = value + product_last(coef_ref[here, :].astype(bf16), r_ref[...])
+            out_ref[...] = value.astype(bf16)
+
+
+def expert_in(shard, pieces, router, info, plain, begun, gate_weight, up_weight, tile=512, row_tile=256):
     rows, half = pieces[0].shape
     columns = gate_weight.shape[1]
-    weight_spec = pl.BlockSpec((half, tile), lambda j, s: (1 - s[0], j))
-    tile_spec = pl.BlockSpec((2 * rows, tile), lambda j, s: (0, j))
+    tile = min(tile, columns)
+    tiles, steps = pl.cdiv(columns, tile), half // row_tile
+    weight_spec = pl.BlockSpec((half, tile), lambda j, s: (1 - s[0], jnp.minimum(j, tiles - 1)))
+    tile_spec = pl.BlockSpec((2 * rows, tile), lambda j, s: (0, jnp.minimum(j, tiles - 1)))
+    out_spec = pl.BlockSpec((rows, row_tile), lambda j, s: (0, jnp.maximum(j - tiles, 0)))
+
+    def row_spec(columns):
+        return pl.BlockSpec(
+            (row_tile, columns), lambda j, s: (steps * (1 - s[0]) + jnp.maximum(j - tiles, 0), 0)
+        )
+
     held_spec = pl.BlockSpec((2 * rows, 128), lambda j, s: (0, 0))
     hidden_shape = jax.ShapeDtypeStruct((2 * rows, columns), bf16)
     return pl.pallas_call(
-        functools.partial(expert_in_body, columns),
+        functools.partial(expert_in_body, columns, tiles),
         grid_spec=pltpu.PrefetchScalarGridSpec(
             num_scalar_prefetch=1,
-            grid=(pl.cdiv(columns, tile),),
+            grid=(tiles + steps,),
             in_specs=[pl.BlockSpec(memory_space=pl.ANY)] * 4
             + [
                 pl.BlockSpec(router.shape, lambda j, s: (0, 0)),
@@ -442,6 +471,9 @@
                 tile_spec,
                 weight_spec,
                 weight_spec,
+                row_spec(columns),
+                row_spec(columns),
+                row_spec(router.shape[1]),
             ],
             out_specs=[
                 pl.BlockSpec((2 * rows, 2 * half), lambda j, s: (0, 0)),
@@ -450,9 +482,14 @@
                 tile_spec,
                 tile_spec,
                 tile_spec,
+                out_spec,
+                out_spec,
             ],
             scratch_shapes=[
                 pltpu.VMEM((2 * rows, half), bf16),
+                pltpu.VMEM((2 * rows, tiles * tile), bf16),
+                pltpu.VMEM((2 * rows, tiles * tile), bf16),
+                pltpu.VMEM((2 * rows, router.shape[1]), f32),
                 pltpu.SemaphoreType.DMA((6,)),
             ],
         ),
@@ -463,15 +500,17 @@
             hidden_shape,
             hidden_shape,
             hidden_shape,
+            jax.ShapeDtypeStruct((rows, half), bf16),
+            jax.ShapeDtypeStruct((rows, half), bf16),
         ],
         compiler_params=pltpu.CompilerParams(vmem_limit_bytes=60 * 2**20),
         cost_estimate=pl.CostEstimate(
-            flops=8 * rows * half * columns,
+            flops=16 * rows * half * columns,
             bytes_accessed=16 * rows * half + 4 * half * columns + 36 * rows * columns,
             transcendentals=2 * rows * columns,
         ),
         name="expert_in",
-    )(shard, *pieces, router, info, plain, *begun, gate_weight, up_weight)
+    )(shard, *pieces, router, info, plain, *begun, gate_weight, up_weight, gate_weight, up_weight, router)
 
 
 def attended_in_body(
@@ -625,8 +664,8 @@
     places = lax.broadcasted_iota(jnp.int32, attn_pack_ref.shape, 0).astype(f32)
     tile_ref[...] = jnp.zeros_like(tile_ref)
     for at, (route_ref, pack_ref) in enumerate(((attn_ref, attn_pack_ref), (mlp_ref, mlp_pack_ref))):
-        routes = route_ref[0].astype(f32)
-        rows = product_first(routes, same)
+        rows = route_ref[...].astype(f32)
+        routes = product_last(same, rows)
         hit = None
         for k in range(2):
             route = rows[k : k + 1]
@@ -939,8 +978,8 @@
         tokens,
         attn_gain[None],
         slot_order,
-        attn_routes,
-        mlp_routes,
+        attn_routes[0].T,
+        mlp_routes[0].T,
         segment_ids,
         parent_ids,
         experts,
@@ -960,7 +999,7 @@
 
     def partner_columns(weight):
         columns = lax.dynamic_slice_in_dim(weight, (partner_at - offset) * piece, piece, 1)
-        return lax.ppermute(after(columns, block), names, sends)
+        return lax.ppermute(columns, names, sends)
 
     grad_half = lax.dynamic_slice_in_dim(cotangent[0], shard * half, half, 1)
 
@@ -1055,11 +1094,13 @@
         return expert_begin(shard_index, own, other, gate_weight, up_weight)
 
     mlp_pieces, _, begun = dispatch(pack_rows(mlp_normed, mlp_pack), None, begin)
-    mlp_rows, mlp_gate, mlp_total, gated_hidden, gate_pre_grad, up_pre_grad = expert_in(
+    mlp_rows, mlp_gate, mlp_total, gated_hidden, gate_pre_grad, up_pre_grad, *theirs_rows = expert_in(
         shard_index, mlp_pieces, mlp_router, info, plain_grad, begun, gate_weight, up_weight
     )
 
     def mlp_sides(mine, event):
+        if not mine:
+            return theirs_rows
         return rows_half(
             shard_index,
             mine,
@@ -1156,10 +1197,10 @@
     def output_work(event):
         return [kept[1], product_first(after(term_rows, event), mixed)]
 
-    works = [None, theirs_work, mine_work, output_work]
+    works = [theirs_work, mine_work, None, output_work]
     key_sums, made = ring_scatter(held, experts, members, works)
     key_sums = key_sums.astype(bf16)
-    _, _, (own, other, attn_coefs, query_grad), (back, output_grad) = made
+    _, (own, other, attn_coefs, query_grad), _, (back, output_grad) = made
     total = own.astype(f32) + swap(other, "expert").astype(f32) + back.astype(f32)
     input_joined = for_tokens(total)
     scalars = jnp.stack([shard, local, local_at]).astype(jnp.int32)
@@ -1195,31 +1236,39 @@
     def spread(values):
         return lax.dynamic_update_slice(jnp.zeros((1, width), f32), values[None], (0, shard * half))
 
+    normed_grad = sum_tokens(back, attn_pack) + shared
+    gain_part = jnp.sum(normed_grad * attn_n, axis=0)
+
     def last_work(event):
-        normed_grad = sum_tokens(after(back, event), attn_pack) + shared
-        weighted = normed_grad * my_half(attn_gain)
-        gain_part = jnp.sum(normed_grad * attn_n, axis=0)
+        grad = after(normed_grad, event)
+        weighted = grad * my_half(attn_gain)
         grad = middle_grad + attn_scale * (weighted - attn_n * feature_mean(weighted * attn_n))
-        small = [attn_router_part, mlp_router_part, spread(gain_part), spread(mlp_gain_part)]
-        small = jnp.pad(jnp.concatenate(small), ((0, 6), (0, 0)))
-        small = small + swap(small, "shard")
-        small = small.reshape(-1, blocks, 2, features).transpose(2, 1, 0, 3)
-        mine = lax.dynamic_index_in_dim(small, core, 0, keepdims=False)
-        theirs = lax.dynamic_index_in_dim(small, 1 - core, 0, keepdims=False)
-        return [grad, swap(grad.astype(bf16), "shard"), mine + swap(theirs, "expert")]
+        return [grad, swap(grad.astype(bf16), "shard")]
 
     attn_router_part = product_first(attn_coefs, after(rows, key_sums).astype(f32))
-    weight_sums = after(weight_sums, back)
-    (weight_sums,), (tokens_grad, got, small) = pinned(
-        (to_experts(weight_sums),), last_work, weight_sums
-    )
+    small = [attn_router_part, mlp_router_part, spread(gain_part), spread(mlp_gain_part)]
+    small = jnp.pad(jnp.concatenate(small), ((0, 6), (0, 0)))
+    small = small.reshape(-1, blocks, 2, features).transpose(1, 2, 0, 3)
+    small = small.reshape(blocks, -1, features).astype(bf16)
+    if members > 1:
+        (weight_sums,), (tokens_grad, got) = pinned((to_experts(weight_sums),), last_work, small)
+        small = lax.all_to_all(small, "dp", 0, 0, tiled=True)
+    else:
+        height = weight_sums.shape[1]
+        both = jnp.concatenate([weight_sums, small], axis=1)
+        (both,), (tokens_grad, got) = pinned((to_experts(both),), last_work, both)
+        weight_sums, small = both[:, :height], both[:, height:]
     weight_sums = join_parts(weight_sums)
+    small = jnp.sum(small.astype(f32), axis=0).reshape(2, -1, features)
+    mine = lax.dynamic_index_in_dim(small, core, 0, keepdims=False)
+    theirs = lax.dynamic_index_in_dim(small, 1 - core, 0, keepdims=False)
+    small = mine + swap(theirs, "expert")
+    small = small + swap(small, "shard")
     layer_out = whole((middle + sum_tokens(term_back, mlp_pack)).astype(bf16))[None]
     got = got.astype(f32)
     tokens_grad = jnp.concatenate(
         [jnp.where(shard == 0, tokens_grad, got), jnp.where(shard == 0, got, tokens_grad)], axis=1
     )[None]
-    small = jnp.sum(lax.all_to_all(small, "dp", 0, 0, tiled=True), axis=0)
 
     heads = piece // HEAD
     pieces = weight_sums.reshape(2 * heads, members, 2, features, HEAD).transpose(1, 2, 0, 3, 4)

time: 503 us -> 490 us (0.974)
  waiting for transfers between devices: 130 us -> 138 us
  other arithmetic: 32.8 us -> 26.3 us
  starting transfers between devices: 92.9 us -> 86.6 us
    ppermute x34, waiting for transfers between devices: 52.7 us -> 63 us  [swap(): return lax.ppermute(values, axis, [(0, 1), (1, 0)])]
    pallas_call x8 -> x7, Pallas kernels: 30.9 us -> 20.9 us  [rows_half(): pl.pallas_call(functools.partial(rows_half_body, len(lefts), extra is not...]
    pallas_call x1, Pallas kernels: 15 us -> 22.3 us  [expert_in(): pl.pallas_call(functools.partial(expert_in_body, columns, tiles), grid_sp...]
    all_to_all x1 -> x0, starting transfers between devices: 5.99 us -> none  [per_device(): small = jnp.sum(lax.all_to_all(small, 'dp', 0, 0, tiled=True), axis=0)]
    all_to_all x1 -> x0, waiting for transfers between devices: 5.85 us -> none  [per_device(): small = jnp.sum(lax.all_to_all(small, 'dp', 0, 0, tiled=True), axis=0)]
    unnamed x145 -> x136, local copies, waits for them, and re-layouts: 25 us -> 24.2 us
  transfers between devices with their start and end apart: 61 -> 60, of which waited for: 39 -> 41; matrix products, arithmetic and copies ran while one was open for 19% -> 17% of each run, Pallas kernels for 18% -> 18%
where the time goes in v4:
time: 490 us; the launch traced here: 485 us
  waiting for transfers between devices  138 us (28%)
  Pallas kernels  115 us (23%)
  starting transfers between devices  86.6 us (18%)
  matrix products  53 us (11%)
  local copies, waits for them, and re-layouts  43.3 us (9%)
  other arithmetic  26.3 us (5%)
  blocking collectives  20.5 us (4%)
    ppermute x34, waiting for transfers between devices, swap(): return lax.ppermute(values, axis, [(0, 1), (1, 0)])  63 us
    dot_general x13, matrix products, product_first(): lax.dot_general(former, latter, (((0,), (0,)), ((), ())), preferred_eleme...  45.8 us
    ppermute x4, waiting for transfers between devices, ring_scatter(): backward = lax.ppermute(backward, 'dp', left)  26.1 us
    unnamed x136, local copies, waits for them, and re-layouts  24.2 us
    pallas_call x1, Pallas kernels, expert_in(): pl.pallas_call(functools.partial(expert_in_body, columns, tiles), grid_sp...  22.3 us
    ppermute x34, starting transfers between devices, swap(): return lax.ppermute(values, axis, [(0, 1), (1, 0)])  21.6 us
    pallas_call x1, Pallas kernels, front(): pl.pallas_call(functools.partial(front_body, capacity, steps), grid_spec=...  21 us
    pallas_call x7, Pallas kernels, rows_half(): pl.pallas_call(functools.partial(rows_half_body, len(lefts), extra is not...  20.9 us
  transfers between devices with their start and end apart: 60, of which 41 were waited for; matrix products, arithmetic and copies ran while one was open for 17% of the time, Pallas kernels for 18%

profile of v4, /device:TPU:0, one launch (start us, length us, event | category | flops | bytes accessed | tf_op | source)
XLA Modules:
  0.0 484.6 jit_solution(1343618789321233374)
XLA Ops:
  29.3 7.5 %collective-permute-done.2 = bf16[128,2176]{1,0:T(8,128)(2,1)S(1)} collective-permute-done((bf16[128,2176]{1,0:T(8,128)(2,1)}, bf16[128,2176]{1,0:T(8,128)(2,1)S(1)}, u32[]{:S(2)}, u32[]{:S(2)}) %collective-permute-start.2) | collective-permute-done | bytes 557088 | tf_op jit(solution)/shard_map/ppermute | solution.py:101
  41.1 8.1 %collective-permute-done.4 = bf16[128,2176]{1,0:T(8,128)(2,1)S(1)} collective-permute-done((bf16[128,2176]{1,0:T(8,128)(2,1)S(1)}, bf16[128,2176]{1,0:T(8,128)(2,1)S(1)}, u32[]{:S(2)}, u32[]{:S(2)}) %collective-permute-start.4) | collective-permute-done | bytes 557088 | tf_op jit(solution)/shard_map/ppermute | solution.py:101
  62.7 6.1 %all-to-all-start = ((bf16[8,40,1024]{2,1,0:T(8,128)(2,1)}), bf16[8,40,1024]{2,1,0:T(8,128)(2,1)}, u32[]{:S(2)}, u32[]{:S(2)}) async-start(bf16[8,40,1024]{2,1,0:T(8,128)(2,1)} %bitcast.18), calls=%async_computation | async-start | bytes 1310720 | tf_op jit(solution)/shard_map/all_to_all | solution.py:1061
  70.6 21.0 %front.1 = (bf16[2048,1024]{1,0:T(8,128)(2,1)}, bf16[640,2048]{1,0:T(8,128)(2,1)}, bf16[640,1024]{1,0:T(8,128)(2,1)}, f32[640,128]{1,0:T(8,128)}) custom-call(s32[3]{0:T(128)} %pad_add_fusion.scalars, bf16[8,128,2176]{2,1,0:T(8,128)(2,1)} %bitcast_dynamic-update-slice_fusion.7.own_ref.own_marks_ref, ...), custom_call_target="tpu_custom_call" | custom-call | flops 8589934592 | bytes 12582912 | tf_op jit(solution)/shard_map/front/pallas_call | solution.py:837
  97.6 8.4 %attend.1 = (bf16[640,512]{1,0:T(8,128)(2,1)S(1)}, f32[640,128]{1,0:T(8,128)S(1)}) custom-call(bf16[640,512]{1,0:T(8,128)(2,1)S(1)} %convolution_convert_fusion.4.q_ref, bf16[2048,1024]{1,0:T(8,128)(2,1)S(1)} %copy-done.5, bf16[2048,1024]{1,0:T(8,128)(2,1)S(1)} %copy-done.5, bf16[640,1024]{1,0:T(8,128)(2,1)S(1)} %copy-done.16, f32[640,128]{1,0:T(8,128)S(1)} %copy-done.2), custom_call_target="tpu_custom_call" | custom-call | flops 1342177280 | bytes 5505024 | tf_op jit(solution)/shard_map/attend/pallas_call | solution.py:178
  116.1 6.6 %plain_in.1 = (bf16[640,2048]{1,0:T(8,128)(2,1)S(1)}, bf16[640,1408]{1,0:T(8,128)(2,1)S(1)}) custom-call(s32[1]{0:T(128)} %bitcast.7.shard_ref, bf16[320,1024]{1,0:T(8,128)(2,1)} %bitcast.21.p0, bf16[320,1024]{1,0:T(8,128)(2,1)S(1)} %collective-permute-done.11.p1, bf16[320,1024]{1,0:T(8,128)(2,1)S(1)} %collective-permute-done.14.p2, ...), custom_call_target="tpu_custom_call" | custom-call | flops 3690987520 | bytes 14614528 | tf_op jit(solution)/shard_map/plain_in/pallas_call | solution.py:296
  123.9 6.0 %collective-permute-done.13 = bf16[320,1024]{1,0:T(8,128)(2,1)S(1)} collective-permute-done((bf16[320,1024]{1,0:T(8,128)(2,1)S(1)}, bf16[320,1024]{1,0:T(8,128)(2,1)S(1)}, u32[]{:S(2)}, u32[]{:S(2)}) %collective-permute-start.13) | collective-permute-done | bytes 655392 | tf_op jit(solution)/shard_map/ppermute | solution.py:41
  133.2 6.0 %all-to-all-start.1 = ((bf16[8,40,1024]{2,1,0:T(8,128)(2,1)}), bf16[8,40,1024]{2,1,0:T(8,128)(2,1)}, u32[]{:S(2)}, u32[]{:S(2)}) async-start(bf16[8,40,1024]{2,1,0:T(8,128)(2,1)} %bitcast.198), calls=%async_computation.1 | async-start | bytes 1310720 | tf_op jit(solution)/shard_map/all_to_all | solution.py:1052
  140.3 16.6 %all-to-all-done.1 = bf16[8,40,1024]{2,1,0:T(8,128)(2,1)} async-done(((bf16[8,40,1024]{2,1,0:T(8,128)(2,1)}), bf16[8,40,1024]{2,1,0:T(8,128)(2,1)}, u32[]{:S(2)}, u32[]{:S(2)}) %all-to-all-start.1) | async-done | bytes 655392 | tf_op jit(solution)/shard_map/all_to_all | solution.py:1052
  162.6 20.5 %all_to_all.45 = bf16[8,40,1024]{2,1,0:T(8,128)(2,1)} all-to-all(bf16[8,40,1024]{2,1,0:T(8,128)(2,1)S(1)} %bitcast.199), channel_id=1, replica_groups=mesh['dp'=8,'expert'=2,'shard'=2] {'dp'}, dimensions={0} | all-to-all | bytes 1310720 | tf_op jit(solution)/shard_map/all_to_all | solution.py:1024
  185.5 8.9 %expert_begin.1 = (bf16[640,1408]{1,0:T(8,128)(2,1)}, bf16[640,1408]{1,0:T(8,128)(2,1)}) custom-call(s32[1]{0:T(128)} %bitcast.7.shard_ref, bf16[320,1024]{1,0:T(8,128)(2,1)} %bitcast.27.p0, bf16[320,1024]{1,0:T(8,128)(2,1)} %collective-permute-done.19.p2, bf16[2048,1408]{1,0:T(8,128)(2,1)} %refs_2_.1, bf16[2048,1408]{1,0:T(8,128)(2,1)} %refs_3_.1), custom_call_target="tpu_custom_call" | custom-call | flops 3690987520 | bytes 15597568 | tf_op jit(solution)/shard_map/expert_begin/pallas_call | solution.py:351
  194.4 6.2 %collective-permute-done.18.p1 = bf16[320,1024]{1,0:T(8,128)(2,1)} collective-permute-done((bf16[320,1024]{1,0:T(8,128)(2,1)}, bf16[320,1024]{1,0:T(8,128)(2,1)}, u32[]{:S(2)}, u32[]{:S(2)}) %collective-permute-start.18) | collective-permute-done | bytes 655392 | tf_op jit(solution)/shard_map/ppermute | solution.py:41
  203.0 22.3 %expert_in.1 = (bf16[640,2048]{1,0:T(8,128)(2,1)}, f32[640,128]{1,0:T(8,128)}, f32[640,128]{1,0:T(8,128)}, bf16[640,1408]{1,0:T(8,128)(2,1)}, bf16[640,1408]{1,0...) custom-call(s32[1]{0:T(128)} %bitcast.7.shard_ref, ...), custom_call_target="tpu_custom_call" | custom-call | flops 7381975040 | bytes 27230208 | tf_op jit(solution)/shard_map/expert_in/pallas_call | solution.py:460
  232.4 9.4 %rows_mine.5 = (bf16[320,1024]{1,0:T(8,128)(2,1)}, bf16[320,1024]{1,0:T(8,128)(2,1)}, f32[640,8]{1,0:T(8,128)}) custom-call(s32[1]{0:T(128)} %bitcast.7.shard_ref, bf16[640,1408]{1,0:T(8,128)(2,1)} %get-tuple-element.192.refs_0_, bf16[640,1408]{1,0:T(8,128)(2,1)} %get-tuple-element.193.refs_1_, bf16[2048,1408]{1,0:T(8,128)(2,1)} %refs_2_.1, ...), custom_call_target="tpu_custom_call" | custom-call | flops 3690987520 | bytes 10682368 | tf_op jit(solution)/shard_map/rows_mine/pallas_call | solution.py:625
  241.9 5.9 %collective-permute-done.22 = bf16[320,1024]{1,0:T(8,128)(2,1)} collective-permute-done((bf16[320,1024]{1,0:T(8,128)(2,1)}, bf16[320,1024]{1,0:T(8,128)(2,1)}, u32[]{:S(2)}, u32[]{:S(2)}) %collective-permute-start.22) | collective-permute-done | bytes 655392 | tf_op jit(solution)/shard_map/ppermute | solution.py:41
  252.5 4.6 all-to-all-start.3
  264.0 7.8 %fusion.34 = f32[2048,1408]{1,0:T(8,128)} fusion(bf16[640,2048]{1,0:T(8,128)(2,1)S(1)} %copy-done.46, bf16[640,1408]{1,0:T(8,128)(2,1)S(1)} %copy-done.52), kind=kOutput, calls=%fused_computation.118 | convolution fusion | flops 3690987520 | bytes 15958016 | tf_op jit(solution)/shard_map/dot_general | solution.py:31
  282.4 4.2 all-to-all-start.4
  296.6 7.8 %fusion.35 = f32[2048,1408]{1,0:T(8,128)} fusion(bf16[640,2048]{1,0:T(8,128)(2,1)S(1)} %copy-done.47, bf16[640,1408]{1,0:T(8,128)(2,1)S(1)} %copy-done.51), kind=kOutput, calls=%fused_computation.119 | convolution fusion | flops 3690987520 | bytes 15958016 | tf_op jit(solution)/shard_map/dot_general | solution.py:31
  305.8 6.1 %all-to-all-start.5 = ((bf16[8,40,1024]{2,1,0:T(8,128)(2,1)}), bf16[8,40,1024]{2,1,0:T(8,128)(2,1)}, u32[]{:S(2)}, u32[]{:S(2)}) async-start(bf16[8,40,1024]{2,1,0:T(8,128)(2,1)} %bitcast.34), calls=%async_computation.5 | async-start | bytes 1310720 | tf_op jit(solution)/shard_map/all_to_all | solution.py:1148
  311.9 9.7 %fusion.37 = f32[2048,1408]{1,0:T(8,128)} fusion(bf16[640,2048]{1,0:T(8,128)(2,1)} %copy-done.37, bf16[640,1408]{1,0:T(8,128)(2,1)} %get-tuple-element.217.refs_0_), kind=kOutput, calls=%fused_computation.121 | convolution fusion | flops 3690987520 | bytes 15958016 | tf_op jit(solution)/shard_map/dot_general | solution.py:31
  331.7 15.0 %attend_back.1 = (bf16[640,512]{1,0:T(8,128)(2,1)}, bf16[8,2,1024,128]{3,2,1,0:T(8,128)(2,1)}) custom-call(bf16[640,512]{1,0:T(8,128)(2,1)} %copy-done.21, bf16[2048,1024]{1,0:T(8,128)(2,1)} %get-tuple-element.159.k_ref.v_ref, bf16[2048,1024]{1,0:T(8,128)(2,1)} %get-tuple-element.159.k_ref.v_ref, bf16[640,1024]{1,0:T(8,128)(2,1)} %get-tuple-element.160.bias_ref, ...), custom_call_target="tpu_custom_call" | custom-call | flops 3355443200 | bytes 9699328 | tf_op jit(solution)/shard_map/attend_back/pallas_call | solution.py:236
  355.6 7.0 %collective-permute-done.33 = bf16[1,1024,128]{2,1,0:T(8,128)(2,1)S(1)} collective-permute-done((bf16[1,1024,128]{2,1,0:T(8,128)(2,1)S(1)}, bf16[1,1024,128]{2,1,0:T(8,128)(2,1)S(1)}, u32[]{:S(2)}, u32[]{:S(2)}) %collective-permute-start.33) | collective-permute-done | bytes 262176 | tf_op jit(solution)/shard_map/ppermute | solution.py:146
  370.5 5.4 %collective-permute-done.36 = bf16[2,1024,128]{2,1,0:T(8,128)(2,1)S(1)} collective-permute-done((bf16[2,1024,128]{2,1,0:T(8,128)(2,1)S(1)}, bf16[2,1024,128]{2,1,0:T(8,128)(2,1)S(1)}, u32[]{:S(2)}, u32[]{:S(2)}) %collective-permute-start.36) | collective-permute-done | bytes 524320 | tf_op jit(solution)/shard_map/ppermute | solution.py:146
  380.3 9.6 %collective-permute-done.38 = bf16[2,1024,128]{2,1,0:T(8,128)(2,1)} collective-permute-done((bf16[2,1024,128]{2,1,0:T(8,128)(2,1)}, bf16[2,1024,128]{2,1,0:T(8,128)(2,1)}, u32[]{:S(2)}, u32[]{:S(2)}) %collective-permute-start.38) | collective-permute-done | bytes 524320 | tf_op jit(solution)/shard_map/ppermute | solution.py:146
  399.4 4.0 collective-permute-done.40
  406.9 4.1 all-to-all-start.6
  425.4 8.0 %shared_out.1 = (bf16[128,1024]{1,0:T(8,128)(2,1)}, bf16[128,1024]{1,0:T(8,128)(2,1)}, bf16[128,1024]{1,0:T(8,128)(2,1)}, bf16[128,1024]{1,0:T(8,128)(2,1)}) custom-call(s32[3]{0:T(128)} %pad_add_fusion.1.scalars, bf16[8,2,128,128]{3,2,1,0:T(8,128)(2,1)} %all-to-all-done.6.sums_ref, bf16[2048,1024]{1,0:T(8,128)(2,1)} %key_ref.1, ...), custom_call_target="tpu_custom_call" | custom-call | flops 1073741824 | bytes 10485760 | tf_op jit(solution)/shard_map/shared_out/pallas_call | solution.py:915
  439.0 5.6 %collective-permute-done.45 = bf16[128,1024]{1,0:T(8,128)(2,1)S(1)} collective-permute-done((bf16[128,1024]{1,0:T(8,128)(2,1)S(1)}, bf16[128,1024]{1,0:T(8,128)(2,1)S(1)}, u32[]{:S(2)}, u32[]{:S(2)}) %collective-permute-start.45) | collective-permute-done | bytes 262176 | tf_op jit(solution)/shard_map/ppermute | solution.py:41
  447.2 6.0 %all-to-all-start.8 = ((bf16[8,304,128]{2,1,0:T(8,128)(2,1)}), bf16[8,304,128]{2,1,0:T(8,128)(2,1)S(1)}, u32[]{:S(2)}, u32[]{:S(2)}) async-start(bf16[8,304,128]{2,1,0:T(8,128)(2,1)} %pad_maximum_fusion), calls=%async_computation.8 | async-start | bytes 1245184 | tf_op jit(solution)/shard_map/all_to_all | solution.py:1172
  458.5 6.1 %collective-permute-done.31 = bf16[128,1024]{1,0:T(8,128)(2,1)S(1)} collective-permute-done((bf16[128,1024]{1,0:T(8,128)(2,1)S(1)}, bf16[128,1024]{1,0:T(8,128)(2,1)S(1)}, u32[]{:S(2)}, u32[]{:S(2)}) %collective-permute-start.31) | collective-permute-done | bytes 262176 | tf_op jit(solution)/shard_map/ppermute | solution.py:41
  476.1 5.7 %collective-permute-done.51 = bf16[1,8,128,128]{3,2,1,0:T(8,128)(2,1)S(1)} collective-permute-done((bf16[1,8,128,128]{3,2,1,0:T(8,128)(2,1)S(1)}, bf16[1,8,128,128]{3,2,1,0:T(8,128)(2,1)S(1)}, u32[]{:S(2)}, u32[]{:S(2)}) %collective-permute-start.51) | collective-permute-done | bytes 262176 | tf_op jit(solution)/shard_map/ppermute | solution.py:41
  (331 shorter events, 206.7 us)
Async XLA Ops:
  6.2 16.3 %collective-permute-start.1 = (bf16[128,2176]{1,0:T(8,128)(2,1)S(1)}, bf16[128,2176]{1,0:T(8,128)(2,1)}, u32[]{:S(2)}, u32[]{:S(2)}) collective-permute-start(bf16[128,2176]{1,0:T(8,128)(2,1)S(1)} %get-tuple-element.144), channel_id=1, source_target_pairs={{0,4},{8,0},{16,8},{24,16},{28,24},{20,28},{12,20},{4,12},{1,5},{9... | collective-permute-start | bytes 1671176 | tf_op jit(solution)/shard_map/ppermute | solution.py:102
  9.3 14.2 %collective-permute-start = (bf16[128,2176]{1,0:T(8,128)(2,1)S(1)}, bf16[128,2176]{1,0:T(8,128)(2,1)}, u32[]{:S(2)}, u32[]{:S(2)}) collective-permute-start(bf16[128,2176]{1,0:T(8,128)(2,1)S(1)} %get-tuple-element.144), channel_id=1, source_target_pairs={{0,8},{8,16},{16,24},{24,28},{28,20},{20,12},{12,4},{4,0},{1,9},{9... | collective-permute-start | bytes 1671176 | tf_op jit(solution)/shard_map/ppermute | solution.py:101
  12.6 47.4 %collective-permute-start.9 = (bf16[2048,512]{1,0:T(8,128)(2,1)}, bf16[2048,512]{1,0:T(8,128)(2,1)S(1)}, u32[]{:S(2)}, u32[]{:S(2)}) collective-permute-start(bf16[2048,512]{1,0:T(8,128)(2,1)} %constant_dynamic-slice_fusion), channel_id=1, source_target_pairs={{0,1},{3,2},{4,5},{7,6},{8,9},{11,10},{12,13},{15,14},{16,17},{19,... | collective-permute-start | bytes 6291464 | tf_op jit(solution)/shard_map/ppermute | solution.py:1002
  18.1 44.6 %collective-permute-start.8 = (bf16[2048,512]{1,0:T(8,128)(2,1)}, bf16[2048,512]{1,0:T(8,128)(2,1)}, u32[]{:S(2)}, u32[]{:S(2)}) collective-permute-start(bf16[2048,512]{1,0:T(8,128)(2,1)} %constant_dynamic-slice_fusion.1), channel_id=1, source_target_pairs={{0,1},{3,2},{4,5},{7,6},{8,9},{11,10},{12,13},{15,14},{16,17},{19,... | collective-permute-start | bytes 6291464 | tf_op jit(solution)/shard_map/ppermute | solution.py:1002
  23.5 13.4 %collective-permute-start.2 = (bf16[128,2176]{1,0:T(8,128)(2,1)}, bf16[128,2176]{1,0:T(8,128)(2,1)S(1)}, u32[]{:S(2)}, u32[]{:S(2)}) collective-permute-start(bf16[128,2176]{1,0:T(8,128)(2,1)} %collective-permute-done), channel_id=1, source_target_pairs={{0,8},{8,16},{16,24},{24,28},{28,20},{20,12},{12,4},{4,0},{1,9},{9... | collective-permute-start | bytes 1671176 | tf_op jit(solution)/shard_map/ppermute | solution.py:101
  24.2 13.1 %collective-permute-start.3 = (bf16[128,2176]{1,0:T(8,128)(2,1)}, bf16[128,2176]{1,0:T(8,128)(2,1)S(1)}, u32[]{:S(2)}, u32[]{:S(2)}) collective-permute-start(bf16[128,2176]{1,0:T(8,128)(2,1)} %collective-permute-done.1), channel_id=1, source_target_pairs={{0,4},{8,0},{16,8},{24,16},{28,24},{20,28},{12,20},{4,12},{1,5},{9... | collective-permute-start | bytes 1671176 | tf_op jit(solution)/shard_map/ppermute | solution.py:102
  37.3 11.9 %collective-permute-start.4 = (bf16[128,2176]{1,0:T(8,128)(2,1)S(1)}, bf16[128,2176]{1,0:T(8,128)(2,1)S(1)}, u32[]{:S(2)}, u32[]{:S(2)}) collective-permute-start(bf16[128,2176]{1,0:T(8,128)(2,1)S(1)} %collective-permute-done.2), channel_id=1, source_target_pairs={{0,8},{8,16},{16,24},{24,28},{28,20},{20,12},{12,4},{4,0},{1,9},{9... | collective-permute-start | bytes 1671176 | tf_op jit(solution)/shard_map/ppermute | solution.py:101
  38.8 12.7 %collective-permute-start.5 = (bf16[128,2176]{1,0:T(8,128)(2,1)S(1)}, bf16[128,2176]{1,0:T(8,128)(2,1)S(1)}, u32[]{:S(2)}, u32[]{:S(2)}) collective-permute-start(bf16[128,2176]{1,0:T(8,128)(2,1)S(1)} %collective-permute-done.3), channel_id=1, source_target_pairs={{0,4},{8,0},{16,8},{24,16},{28,24},{20,28},{12,20},{4,12},{1,5},{9... | collective-permute-start | bytes 1671176 | tf_op jit(solution)/shard_map/ppermute | solution.py:102
  62.7 28.9 %all-to-all-start = ((bf16[8,40,1024]{2,1,0:T(8,128)(2,1)}), bf16[8,40,1024]{2,1,0:T(8,128)(2,1)}, u32[]{:S(2)}, u32[]{:S(2)}) async-start(bf16[8,40,1024]{2,1,0:T(8,128)(2,1)} %bitcast.18), calls=%async_computation | async-start | bytes 1310720 | tf_op jit(solution)/shard_map/all_to_all | solution.py:1061
  91.6 17.8 %collective-permute-start.11 = (bf16[320,1024]{1,0:T(8,128)(2,1)}, bf16[320,1024]{1,0:T(8,128)(2,1)S(1)}, u32[]{:S(2)}, u32[]{:S(2)}) collective-permute-start(bf16[320,1024]{1,0:T(8,128)(2,1)} %bitcast.21.p0), channel_id=1, source_target_pairs={{0,1},{1,0},{2,3},{3,2},{4,5},{5,4},{6,7},{7,6},{8,9},{9,8},{10,11... | collective-permute-start | bytes 1966088 | tf_op jit(solution)/shard_map/ppermute | solution.py:41
  113.1 16.8 %collective-permute-start.13 = (bf16[320,1024]{1,0:T(8,128)(2,1)S(1)}, bf16[320,1024]{1,0:T(8,128)(2,1)S(1)}, u32[]{:S(2)}, u32[]{:S(2)}) collective-permute-start(bf16[320,1024]{1,0:T(8,128)(2,1)S(1)} %add_convert_fusion.7), channel_id=1, source_target_pairs={{0,1},{1,0},{2,3},{3,2},{4,5},{5,4},{6,7},{7,6},{8,9},{9,8},{10,11... | collective-permute-start | bytes 1966088 | tf_op jit(solution)/shard_map/ppermute | solution.py:41
  133.2 23.7 %all-to-all-start.1 = ((bf16[8,40,1024]{2,1,0:T(8,128)(2,1)}), bf16[8,40,1024]{2,1,0:T(8,128)(2,1)}, u32[]{:S(2)}, u32[]{:S(2)}) async-start(bf16[8,40,1024]{2,1,0:T(8,128)(2,1)} %bitcast.198), calls=%async_computation.1 | async-start | bytes 1310720 | tf_op jit(solution)/shard_map/all_to_all | solution.py:1052
  183.1 17.5 %collective-permute-start.18 = (bf16[320,1024]{1,0:T(8,128)(2,1)}, bf16[320,1024]{1,0:T(8,128)(2,1)}, u32[]{:S(2)}, u32[]{:S(2)}) collective-permute-start(bf16[320,1024]{1,0:T(8,128)(2,1)} %bitcast.27.p0), channel_id=1, source_target_pairs={{0,1},{1,0},{2,3},{3,2},{4,5},{5,4},{6,7},{7,6},{8,9},{9,8},{10,11... | collective-permute-start | bytes 1966088 | tf_op jit(solution)/shard_map/ppermute | solution.py:41
  229.8 17.9 %collective-permute-start.22 = (bf16[320,1024]{1,0:T(8,128)(2,1)}, bf16[320,1024]{1,0:T(8,128)(2,1)}, u32[]{:S(2)}, u32[]{:S(2)}) collective-permute-start(bf16[320,1024]{1,0:T(8,128)(2,1)} %add_convert_fusion.5), channel_id=1, source_target_pairs={{0,1},{1,0},{2,3},{3,2},{4,5},{5,4},{6,7},{7,6},{8,9},{9,8},{10,11... | collective-permute-start | bytes 1966088 | tf_op jit(solution)/shard_map/ppermute | solution.py:41
  252.5 22.5 %all-to-all-start.3 = ((bf16[8,40,1024]{2,1,0:T(8,128)(2,1)}), bf16[8,40,1024]{2,1,0:T(8,128)(2,1)}, u32[]{:S(2)}, u32[]{:S(2)}) async-start(bf16[8,40,1024]{2,1,0:T(8,128)(2,1)} %bitcast.197), calls=%async_computation.3 | async-start | bytes 1310720 | tf_op jit(solution)/shard_map/all_to_all | solution.py:1052
  282.4 23.1 %all-to-all-start.4 = ((bf16[8,40,1024]{2,1,0:T(8,128)(2,1)}), bf16[8,40,1024]{2,1,0:T(8,128)(2,1)}, u32[]{:S(2)}, u32[]{:S(2)}) async-start(bf16[8,40,1024]{2,1,0:T(8,128)(2,1)} %bitcast.196), calls=%async_computation.4 | async-start | bytes 1310720 | tf_op jit(solution)/shard_map/all_to_all | solution.py:1024
  286.6 17.7 %collective-permute-start.30 = (bf16[320,1024]{1,0:T(8,128)(2,1)}, bf16[320,1024]{1,0:T(8,128)(2,1)S(1)}, u32[]{:S(2)}, u32[]{:S(2)}) collective-permute-start(bf16[320,1024]{1,0:T(8,128)(2,1)} %add_convert_fusion.3), channel_id=1, source_target_pairs={{0,1},{1,0},{2,3},{3,2},{4,5},{5,4},{6,7},{7,6},{8,9},{9,8},{10,11... | collective-permute-start | bytes 1966088 | tf_op jit(solution)/shard_map/ppermute | solution.py:41
  305.6 17.5 %collective-permute-start.27 = (bf16[320,1024]{1,0:T(8,128)(2,1)}, bf16[320,1024]{1,0:T(8,128)(2,1)}, u32[]{:S(2)}, u32[]{:S(2)}) collective-permute-start(bf16[320,1024]{1,0:T(8,128)(2,1)} %bitcast.33.p0), channel_id=1, source_target_pairs={{0,2},{2,0},{1,3},{3,1},{4,6},{6,4},{5,7},{7,5},{8,10},{10,8},{9,1... | collective-permute-start | bytes 1966088 | tf_op jit(solution)/shard_map/ppermute | solution.py:41
  305.6 17.5 %collective-permute-start.26 = (bf16[320,1024]{1,0:T(8,128)(2,1)}, bf16[320,1024]{1,0:T(8,128)(2,1)}, u32[]{:S(2)}, u32[]{:S(2)}) collective-permute-start(bf16[320,1024]{1,0:T(8,128)(2,1)} %bitcast.33.p0), channel_id=1, source_target_pairs={{0,1},{1,0},{2,3},{3,2},{4,5},{5,4},{6,7},{7,6},{8,9},{9,8},{10,11... | collective-permute-start | bytes 1966088 | tf_op jit(solution)/shard_map/ppermute | solution.py:41
  305.8 40.9 %all-to-all-start.5 = ((bf16[8,40,1024]{2,1,0:T(8,128)(2,1)}), bf16[8,40,1024]{2,1,0:T(8,128)(2,1)}, u32[]{:S(2)}, u32[]{:S(2)}) async-start(bf16[8,40,1024]{2,1,0:T(8,128)(2,1)} %bitcast.34), calls=%async_computation.5 | async-start | bytes 1310720 | tf_op jit(solution)/shard_map/all_to_all | solution.py:1148
  352.5 10.1 %collective-permute-start.32 = (bf16[1,1024,128]{2,1,0:T(8,128)(2,1)S(1)}, bf16[1,1024,128]{2,1,0:T(8,128)(2,1)S(1)}, u32[]{:S(2)}, u32[]{:S(2)}) collective-permute-start(bf16[1,1024,128]{2,1,0:T(8,128)(2,1)S(1)} %get-tuple-element.297), channel_id=1, source_target_pairs={{0,8},{8,16},{16,24},{24,28},{28,20},{20,12},{12,4},{4,0},{1,9},{9... | collective-permute-start | bytes 786440 | tf_op jit(solution)/shard_map/ppermute | solution.py:145
  362.8 13.1 %collective-permute-start.36 = (bf16[2,1024,128]{2,1,0:T(8,128)(2,1)S(1)}, bf16[2,1024,128]{2,1,0:T(8,128)(2,1)S(1)}, u32[]{:S(2)}, u32[]{:S(2)}) collective-permute-start(bf16[2,1024,128]{2,1,0:T(8,128)(2,1)S(1)} %get-tuple-element.294), channel_id=1, source_target_pairs={{0,4},{8,0},{16,8},{24,16},{28,24},{20,28},{12,20},{4,12},{1,5},{9... | collective-permute-start | bytes 1572872 | tf_op jit(solution)/shard_map/ppermute | solution.py:146
  363.1 13.1 %collective-permute-start.35 = (bf16[2,1024,128]{2,1,0:T(8,128)(2,1)S(1)}, bf16[2,1024,128]{2,1,0:T(8,128)(2,1)S(1)}, u32[]{:S(2)}, u32[]{:S(2)}) collective-permute-start(bf16[2,1024,128]{2,1,0:T(8,128)(2,1)S(1)} %get-tuple-element.295), channel_id=1, source_target_pairs={{0,8},{8,16},{16,24},{24,28},{28,20},{20,12},{12,4},{4,0},{1,9},{9... | collective-permute-start | bytes 1572872 | tf_op jit(solution)/shard_map/ppermute | solution.py:145
  377.4 12.5 %collective-permute-start.38 = (bf16[2,1024,128]{2,1,0:T(8,128)(2,1)}, bf16[2,1024,128]{2,1,0:T(8,128)(2,1)}, u32[]{:S(2)}, u32[]{:S(2)}) collective-permute-start(bf16[2,1024,128]{2,1,0:T(8,128)(2,1)} %get-tuple-element.292), channel_id=1, source_target_pairs={{0,4},{8,0},{16,8},{24,16},{28,24},{20,28},{12,20},{4,12},{1,5},{9... | collective-permute-start | bytes 1572872 | tf_op jit(solution)/shard_map/ppermute | solution.py:146
  378.9 11.9 %collective-permute-start.37 = (bf16[2,1024,128]{2,1,0:T(8,128)(2,1)}, bf16[2,1024,128]{2,1,0:T(8,128)(2,1)}, u32[]{:S(2)}, u32[]{:S(2)}) collective-permute-start(bf16[2,1024,128]{2,1,0:T(8,128)(2,1)} %get-tuple-element.293), channel_id=1, source_target_pairs={{0,8},{8,16},{16,24},{24,28},{28,20},{20,12},{12,4},{4,0},{1,9},{9... | collective-permute-start | bytes 1572872 | tf_op jit(solution)/shard_map/ppermute | solution.py:145
  379.7 19.7 %collective-permute-start.41 = (bf16[320,1024]{1,0:T(8,128)(2,1)S(1)}, bf16[320,1024]{1,0:T(8,128)(2,1)S(1)}, u32[]{:S(2)}, u32[]{:S(2)}) collective-permute-start(bf16[320,1024]{1,0:T(8,128)(2,1)S(1)} %copy-done.55), channel_id=1, source_target_pairs={{0,1},{1,0},{2,3},{3,2},{4,5},{5,4},{6,7},{7,6},{8,9},{9,8},{10,11... | collective-permute-start | bytes 1966088 | tf_op jit(solution)/shard_map/ppermute | solution.py:41
  392.7 10.8 %collective-permute-start.40 = (bf16[2,1024,128]{2,1,0:T(8,128)(2,1)S(1)}, bf16[2,1024,128]{2,1,0:T(8,128)(2,1)S(1)}, u32[]{:S(2)}, u32[]{:S(2)}) collective-permute-start(bf16[2,1024,128]{2,1,0:T(8,128)(2,1)S(1)} %get-tuple-element.290), channel_id=1, source_target_pairs={{0,4},{8,0},{16,8},{24,16},{28,24},{20,28},{12,20},{4,12},{1,5},{9... | collective-permute-start | bytes 1572872 | tf_op jit(solution)/shard_map/ppermute | solution.py:146
  394.2 10.6 %collective-permute-start.39 = (bf16[2,1024,128]{2,1,0:T(8,128)(2,1)S(1)}, bf16[2,1024,128]{2,1,0:T(8,128)(2,1)S(1)}, u32[]{:S(2)}, u32[]{:S(2)}) collective-permute-start(bf16[2,1024,128]{2,1,0:T(8,128)(2,1)S(1)} %get-tuple-element.291), channel_id=1, source_target_pairs={{0,8},{8,16},{16,24},{24,28},{28,20},{20,12},{12,4},{4,0},{1,9},{9... | collective-permute-start | bytes 1572872 | tf_op jit(solution)/shard_map/ppermute | solution.py:145
  395.5 19.4 %collective-permute-start.42 = (bf16[320,1024]{1,0:T(8,128)(2,1)S(1)}, bf16[320,1024]{1,0:T(8,128)(2,1)}, u32[]{:S(2)}, u32[]{:S(2)}) collective-permute-start(bf16[320,1024]{1,0:T(8,128)(2,1)S(1)} %copy-done.34), channel_id=1, source_target_pairs={{0,2},{2,0},{1,3},{3,1},{4,6},{6,4},{5,7},{7,5},{8,10},{10,8},{9,1... | collective-permute-start | bytes 1966088 | tf_op jit(solution)/shard_map/ppermute | solution.py:41
  406.9 14.8 %all-to-all-start.6 = ((bf16[8,2,128,128]{3,2,1,0:T(8,128)(2,1)}), bf16[8,2,128,128]{3,2,1,0:T(8,128)(2,1)}, u32[]{:S(2)}, u32[]{:S(2)}) async-start(bf16[8,2,128,128]{3,2,1,0:T(8,128)(2,1)} %bitcast.186), calls=%async_computation.6 | async-start | bytes 1048576 | tf_op jit(solution)/shard_map/all_to_all | solution.py:1172
  421.7 23.0 %all-to-all-start.7 = ((bf16[8,40,1024]{2,1,0:T(8,128)(2,1)}), bf16[8,40,1024]{2,1,0:T(8,128)(2,1)S(1)}, u32[]{:S(2)}, u32[]{:S(2)}) async-start(bf16[8,40,1024]{2,1,0:T(8,128)(2,1)} %bitcast.53), calls=%async_computation.7 | async-start | bytes 1310720 | tf_op jit(solution)/shard_map/all_to_all | solution.py:1225
  447.2 22.1 %all-to-all-start.8 = ((bf16[8,304,128]{2,1,0:T(8,128)(2,1)}), bf16[8,304,128]{2,1,0:T(8,128)(2,1)S(1)}, u32[]{:S(2)}, u32[]{:S(2)}) async-start(bf16[8,304,128]{2,1,0:T(8,128)(2,1)} %pad_maximum_fusion), calls=%async_computation.8 | async-start | bytes 1245184 | tf_op jit(solution)/shard_map/all_to_all | solution.py:1172
  (94 other events, 1045.3 us)

commit v5 on v4

--- a/solution.py
+++ b/solution.py
@@ -35,6 +35,10 @@
 
 def limit_of(rows):
     return min(56, max(40, rows * 24 // 640)) * 2**20
+
+
+def grant(size, rows):
+    return min(60, size * max(1, rows // 640)) * 2**20
 
 
 def swap(values, axis):
@@ -503,7 +507,7 @@
             jax.ShapeDtypeStruct((rows, half), bf16),
             jax.ShapeDtypeStruct((rows, half), bf16),
         ],
-        compiler_params=pltpu.CompilerParams(vmem_limit_bytes=60 * 2**20),
+        compiler_params=pltpu.CompilerParams(vmem_limit_bytes=grant(50, 2 * rows)),
         cost_estimate=pl.CostEstimate(
             flops=16 * rows * half * columns,
             bytes_accessed=16 * rows * half + 4 * half * columns + 36 * rows * columns,
@@ -628,7 +632,7 @@
             num_scalar_prefetch=1, grid=(steps,), in_specs=in_specs, out_specs=out_specs
         ),
         out_shape=out_shape,
-        compiler_params=pltpu.CompilerParams(vmem_limit_bytes=limit_of(2 * rows) if len(lefts) == 1 else 60 * 2**20),
+        compiler_params=pltpu.CompilerParams(vmem_limit_bytes=grant(40, 2 * rows)),
         cost_estimate=pl.CostEstimate(
             flops=4 * rows * half * depth,
             bytes_accessed=4 * rows * depth + 2 * half * depth + 4 * rows * half,
@@ -864,7 +868,7 @@
             jax.ShapeDtypeStruct((2 * rows, length), bf16),
             jax.ShapeDtypeStruct((2 * rows, 128), f32),
         ],
-        compiler_params=pltpu.CompilerParams(vmem_limit_bytes=60 * 2**20),
+        compiler_params=pltpu.CompilerParams(vmem_limit_bytes=grant(52, 2 * rows)),
         cost_estimate=pl.CostEstimate(
             flops=8 * length * width * piece,
             bytes_accessed=4 * length * width + 4 * width * piece,

time: 490 us -> 486 us (level)
  local copies, waits for them, and re-layouts: 43.3 us -> 50.3 us
  Pallas kernels: 115 us -> 110 us
    unnamed x136 -> x150, local copies, waits for them, and re-layouts: 24.2 us -> 30.2 us
where the time goes in v5:
time: 486 us; the launch traced here: 481 us
  waiting for transfers between devices  139 us (29%)
  Pallas kernels  110 us (23%)
  starting transfers between devices  85.7 us (18%)
  matrix products  51.4 us (11%)
  local copies, waits for them, and re-layouts  50.3 us (10%)
  other arithmetic  22.7 us (5%)
  blocking collectives  20.4 us (4%)
    ppermute x34, waiting for transfers between devices, swap(): return lax.ppermute(values, axis, [(0, 1), (1, 0)])  62.5 us
    dot_general x13, matrix products, product_first(): lax.dot_general(former, latter, (((0,), (0,)), ((), ())), preferred_eleme...  44.5 us
    unnamed x150, local copies, waits for them, and re-layouts  30.2 us
    ppermute x4, waiting for transfers between devices, ring_scatter(): backward = lax.ppermute(backward, 'dp', left)  26.1 us
    ppermute x34, starting transfers between devices, swap(): return lax.ppermute(values, axis, [(0, 1), (1, 0)])  21.6 us
    pallas_call x1, Pallas kernels, expert_in(): pl.pallas_call(functools.partial(expert_in_body, columns, tiles), grid_sp...  21.4 us
    pallas_call x1, Pallas kernels, front(): pl.pallas_call(functools.partial(front_body, capacity, steps), grid_spec=...  20.5 us
    all_to_all x1, blocking collectives, dispatch(): arrived = lax.all_to_all(packed, 'dp', 0, 0, tiled=True)  20.4 us
  transfers between devices with their start and end apart: 60, of which 41 were waited for; matrix products, arithmetic and copies ran while one was open for 17% of the time, Pallas kernels for 18%

profile of v5, /device:TPU:0, one launch (start us, length us, event | category | flops | bytes accessed | tf_op | source)
XLA Modules:
  0.0 480.7 jit_solution(13699246491303555923)
XLA Ops:
  29.3 7.5 %collective-permute-done.2 = bf16[128,2176]{1,0:T(8,128)(2,1)S(1)} collective-permute-done((bf16[128,2176]{1,0:T(8,128)(2,1)}, bf16[128,2176]{1,0:T(8,128)(2,1)S(1)}, u32[]{:S(2)}, u32[]{:S(2)}) %collective-permute-start.2) | collective-permute-done | bytes 557088 | tf_op jit(solution)/shard_map/ppermute | solution.py:105
  41.1 8.2 %collective-permute-done.4 = bf16[128,2176]{1,0:T(8,128)(2,1)S(1)} collective-permute-done((bf16[128,2176]{1,0:T(8,128)(2,1)S(1)}, bf16[128,2176]{1,0:T(8,128)(2,1)S(1)}, u32[]{:S(2)}, u32[]{:S(2)}) %collective-permute-start.4) | collective-permute-done | bytes 557088 | tf_op jit(solution)/shard_map/ppermute | solution.py:105
  62.7 6.0 %all-to-all-start = ((bf16[8,40,1024]{2,1,0:T(8,128)(2,1)}), bf16[8,40,1024]{2,1,0:T(8,128)(2,1)S(1)}, u32[]{:S(2)}, u32[]{:S(2)}) async-start(bf16[8,40,1024]{2,1,0:T(8,128)(2,1)} %bitcast.18), calls=%async_computation | async-start | bytes 1310720 | tf_op jit(solution)/shard_map/all_to_all | solution.py:1065
  70.6 20.5 %front.1 = (bf16[2048,1024]{1,0:T(8,128)(2,1)}, bf16[640,2048]{1,0:T(8,128)(2,1)}, bf16[640,1024]{1,0:T(8,128)(2,1)}, f32[640,128]{1,0:T(8,128)S(1)}) custom-call(s32[3]{0:T(128)S(1)} %pad_add_fusion.scalars, bf16[8,128,2176]{2,1,0:T(8,128)(2,1)} %bitcast_dynamic-update-slice_fusion.7.own_ref.own_marks_ref, ...), custom_call_target="tpu_custom_call" | custom-call | flops 8589934592 | bytes 12582912 | tf_op jit(solution)/shard_map/front/pallas_call | solution.py:841
  93.7 4.0 convolution_convert_fusion.4.q_ref
  97.8 8.4 %attend.1 = (bf16[640,512]{1,0:T(8,128)(2,1)S(1)}, f32[640,128]{1,0:T(8,128)S(1)}) custom-call(bf16[640,512]{1,0:T(8,128)(2,1)S(1)} %convolution_convert_fusion.4.q_ref, bf16[2048,1024]{1,0:T(8,128)(2,1)S(1)} %copy-done.4, bf16[2048,1024]{1,0:T(8,128)(2,1)S(1)} %copy-done.4, bf16[640,1024]{1,0:T(8,128)(2,1)S(1)} %copy-done.21, ...), custom_call_target="tpu_custom_call" | custom-call | flops 1342177280 | bytes 5505024 | tf_op jit(solution)/shard_map/attend/pallas_call | solution.py:182
  115.3 5.7 %plain_in.1 = (bf16[640,2048]{1,0:T(8,128)(2,1)S(1)}, bf16[640,1408]{1,0:T(8,128)(2,1)S(1)}) custom-call(s32[1]{0:T(128)} %bitcast.7.shard_ref, bf16[320,1024]{1,0:T(8,128)(2,1)S(1)} %bitcast.200, bf16[320,1024]{1,0:T(8,128)(2,1)S(1)} %collective-permute-done.11.p1, bf16[320,1024]{1,0:T(8,128)(2,1)S(1)} %collective-permute-done.14.p2, ...), custom_call_target="tpu_custom_call" | custom-call | flops 3690987520 | bytes 14614528 | tf_op jit(solution)/shard_map/plain_in/pallas_call | solution.py:300
  122.3 6.8 %collective-permute-done.13 = bf16[320,1024]{1,0:T(8,128)(2,1)S(1)} collective-permute-done((bf16[320,1024]{1,0:T(8,128)(2,1)S(1)}, bf16[320,1024]{1,0:T(8,128)(2,1)S(1)}, u32[]{:S(2)}, u32[]{:S(2)}) %collective-permute-start.13) | collective-permute-done | bytes 655392 | tf_op jit(solution)/shard_map/ppermute | solution.py:45
  132.4 6.0 %all-to-all-start.1 = ((bf16[8,40,1024]{2,1,0:T(8,128)(2,1)}), bf16[8,40,1024]{2,1,0:T(8,128)(2,1)}, u32[]{:S(2)}, u32[]{:S(2)}) async-start(bf16[8,40,1024]{2,1,0:T(8,128)(2,1)} %bitcast.22), calls=%async_computation.1 | async-start | bytes 1310720 | tf_op jit(solution)/shard_map/all_to_all | solution.py:1056
  138.5 17.6 %all-to-all-done.1 = bf16[8,40,1024]{2,1,0:T(8,128)(2,1)} async-done(((bf16[8,40,1024]{2,1,0:T(8,128)(2,1)}), bf16[8,40,1024]{2,1,0:T(8,128)(2,1)}, u32[]{:S(2)}, u32[]{:S(2)}) %all-to-all-start.1) | async-done | bytes 655392 | tf_op jit(solution)/shard_map/all_to_all | solution.py:1056
  161.6 20.4 %all_to_all.45 = bf16[8,40,1024]{2,1,0:T(8,128)(2,1)S(1)} all-to-all(bf16[8,40,1024]{2,1,0:T(8,128)(2,1)S(1)} %bitcast.210), channel_id=1, replica_groups=mesh['dp'=8,'expert'=2,'shard'=2] {'dp'}, dimensions={0} | all-to-all | bytes 1310720 | tf_op jit(solution)/shard_map/all_to_all | solution.py:1028
  184.9 8.9 %expert_begin.1 = (bf16[640,1408]{1,0:T(8,128)(2,1)}, bf16[640,1408]{1,0:T(8,128)(2,1)}) custom-call(s32[1]{0:T(128)} %bitcast.7.shard_ref, bf16[320,1024]{1,0:T(8,128)(2,1)} %bitcast.196, bf16[320,1024]{1,0:T(8,128)(2,1)} %copy-done.58, bf16[2048,1408]{1,0:T(8,128)(2,1)} %refs_2_.1, bf16[2048,1408]{1,0:T(8,128)(2,1)} %refs_3_.1), custom_call_target="tpu_custom_call" | custom-call | flops 3690987520 | bytes 15597568 | tf_op jit(solution)/shard_map/expert_begin/pallas_call | solution.py:355
  193.8 5.4 %collective-permute-done.18.p1 = bf16[320,1024]{1,0:T(8,128)(2,1)} collective-permute-done((bf16[320,1024]{1,0:T(8,128)(2,1)S(1)}, bf16[320,1024]{1,0:T(8,128)(2,1)}, u32[]{:S(2)}, u32[]{:S(2)}) %collective-permute-start.18) | collective-permute-done | bytes 655392 | tf_op jit(solution)/shard_map/ppermute | solution.py:45
  202.8 21.4 %expert_in.1 = (bf16[640,2048]{1,0:T(8,128)(2,1)}, f32[640,128]{1,0:T(8,128)S(1)}, f32[640,128]{1,0:T(8,128)S(1)}, bf16[640,1408]{1,0:T(8,128)(2,1)}, bf16[640,1...) custom-call(s32[1]{0:T(128)} %bitcast.7.shard_ref, ...), custom_call_target="tpu_custom_call" | custom-call | flops 7381975040 | bytes 27230208 | tf_op jit(solution)/shard_map/expert_in/pallas_call | solution.py:464
  229.9 6.5 %rows_mine.5 = (bf16[320,1024]{1,0:T(8,128)(2,1)S(1)}, bf16[320,1024]{1,0:T(8,128)(2,1)S(1)}, f32[640,8]{1,0:T(8,128)S(1)}) custom-call(s32[1]{0:T(128)} %bitcast.7.shard_ref, bf16[640,1408]{1,0:T(8,128)(2,1)S(1)} %copy-done.19, bf16[640,1408]{1,0:T(8,128)(2,1)S(1)} %copy-done.17, bf16[2048,1408]{1,0:T(8,128)(2,1)S(1)} %bitcast.188, ...), custom_call_target="tpu_custom_call" | custom-call | flops 3690987520 | bytes 10682368 | tf_op jit(solution)/shard_map/rows_mine/pallas_call | solution.py:629
  236.4 7.0 %collective-permute-done.22 = bf16[320,1024]{1,0:T(8,128)(2,1)S(1)} collective-permute-done((bf16[320,1024]{1,0:T(8,128)(2,1)S(1)}, bf16[320,1024]{1,0:T(8,128)(2,1)S(1)}, u32[]{:S(2)}, u32[]{:S(2)}) %collective-permute-start.22) | collective-permute-done | bytes 655392 | tf_op jit(solution)/shard_map/ppermute | solution.py:45
  246.7 3.9 all-to-all-start.3
  257.6 7.8 %fusion.34 = f32[2048,1408]{1,0:T(8,128)} fusion(bf16[640,2048]{1,0:T(8,128)(2,1)S(1)} %copy-done.53, bf16[640,1408]{1,0:T(8,128)(2,1)S(1)} %copy-done.20), kind=kOutput, calls=%fused_computation.118 | convolution fusion | flops 3690987520 | bytes 15958016 | tf_op jit(solution)/shard_map/dot_general | solution.py:31
  287.5 7.8 %fusion.35 = f32[2048,1408]{1,0:T(8,128)} fusion(bf16[640,2048]{1,0:T(8,128)(2,1)S(1)} %copy-done.54, bf16[640,1408]{1,0:T(8,128)(2,1)S(1)} %copy-done.18), kind=kOutput, calls=%fused_computation.119 | convolution fusion | flops 3690987520 | bytes 15958016 | tf_op jit(solution)/shard_map/dot_general | solution.py:31
  296.8 6.2 %all-to-all-start.5 = ((bf16[8,40,1024]{2,1,0:T(8,128)(2,1)}), bf16[8,40,1024]{2,1,0:T(8,128)(2,1)}, u32[]{:S(2)}, u32[]{:S(2)}) async-start(bf16[8,40,1024]{2,1,0:T(8,128)(2,1)} %bitcast.208), calls=%async_computation.5 | async-start | bytes 1310720 | tf_op jit(solution)/shard_map/all_to_all | solution.py:1152
  303.0 9.7 %fusion.37 = f32[2048,1408]{1,0:T(8,128)} fusion(bf16[640,2048]{1,0:T(8,128)(2,1)} %copy-done.42, bf16[640,1408]{1,0:T(8,128)(2,1)} %get-tuple-element.217.refs_0_), kind=kOutput, calls=%fused_computation.121 | convolution fusion | flops 3690987520 | bytes 15958016 | tf_op jit(solution)/shard_map/dot_general | solution.py:31
  324.8 14.9 %attend_back.1 = (bf16[640,512]{1,0:T(8,128)(2,1)}, bf16[8,2,1024,128]{3,2,1,0:T(8,128)(2,1)}) custom-call(bf16[640,512]{1,0:T(8,128)(2,1)} %copy-done.26, bf16[2048,1024]{1,0:T(8,128)(2,1)} %get-tuple-element.159.k_ref.v_ref, bf16[2048,1024]{1,0:T(8,128)(2,1)} %get-tuple-element.159.k_ref.v_ref, bf16[640,1024]{1,0:T(8,128)(2,1)} %get-tuple-element.160.bias_ref, ...), custom_call_target="tpu_custom_call" | custom-call | flops 3355443200 | bytes 9699328 | tf_op jit(solution)/shard_map/attend_back/pallas_call | solution.py:240
  349.1 7.2 %collective-permute-done.33 = bf16[1,1024,128]{2,1,0:T(8,128)(2,1)S(1)} collective-permute-done((bf16[1,1024,128]{2,1,0:T(8,128)(2,1)S(1)}, bf16[1,1024,128]{2,1,0:T(8,128)(2,1)S(1)}, u32[]{:S(2)}, u32[]{:S(2)}) %collective-permute-start.33) | collective-permute-done | bytes 262176 | tf_op jit(solution)/shard_map/ppermute | solution.py:150
  364.1 5.4 %collective-permute-done.36 = bf16[2,1024,128]{2,1,0:T(8,128)(2,1)S(1)} collective-permute-done((bf16[2,1024,128]{2,1,0:T(8,128)(2,1)S(1)}, bf16[2,1024,128]{2,1,0:T(8,128)(2,1)S(1)}, u32[]{:S(2)}, u32[]{:S(2)}) %collective-permute-start.36) | collective-permute-done | bytes 524320 | tf_op jit(solution)/shard_map/ppermute | solution.py:150
  374.1 9.6 %collective-permute-done.38 = bf16[2,1024,128]{2,1,0:T(8,128)(2,1)} collective-permute-done((bf16[2,1024,128]{2,1,0:T(8,128)(2,1)}, bf16[2,1024,128]{2,1,0:T(8,128)(2,1)}, u32[]{:S(2)}, u32[]{:S(2)}) %collective-permute-start.38) | collective-permute-done | bytes 524320 | tf_op jit(solution)/shard_map/ppermute | solution.py:150
  393.1 4.0 collective-permute-done.40
  400.6 4.1 all-to-all-start.6
  419.5 7.8 %shared_out.1 = (bf16[128,1024]{1,0:T(8,128)(2,1)}, bf16[128,1024]{1,0:T(8,128)(2,1)}, bf16[128,1024]{1,0:T(8,128)(2,1)}, bf16[128,1024]{1,0:T(8,128)(2,1)}) custom-call(s32[3]{0:T(128)} %pad_add_fusion.1.scalars, bf16[8,2,128,128]{3,2,1,0:T(8,128)(2,1)} %all-to-all-done.6.sums_ref, bf16[2048,1024]{1,0:T(8,128)(2,1)} %key_ref.1, ...), custom_call_target="tpu_custom_call" | custom-call | flops 1073741824 | bytes 10485760 | tf_op jit(solution)/shard_map/shared_out/pallas_call | solution.py:919
  433.2 5.4 %collective-permute-done.45 = bf16[128,1024]{1,0:T(8,128)(2,1)S(1)} collective-permute-done((bf16[128,1024]{1,0:T(8,128)(2,1)S(1)}, bf16[128,1024]{1,0:T(8,128)(2,1)S(1)}, u32[]{:S(2)}, u32[]{:S(2)}) %collective-permute-start.45) | collective-permute-done | bytes 262176 | tf_op jit(solution)/shard_map/ppermute | solution.py:45
  441.1 6.0 %all-to-all-start.8 = ((bf16[8,304,128]{2,1,0:T(8,128)(2,1)}), bf16[8,304,128]{2,1,0:T(8,128)(2,1)}, u32[]{:S(2)}, u32[]{:S(2)}) async-start(bf16[8,304,128]{2,1,0:T(8,128)(2,1)} %pad_maximum_fusion), calls=%async_computation.8 | async-start | bytes 1245184 | tf_op jit(solution)/shard_map/all_to_all | solution.py:1176
  452.9 5.8 %collective-permute-done.31 = bf16[128,1024]{1,0:T(8,128)(2,1)S(1)} collective-permute-done((bf16[128,1024]{1,0:T(8,128)(2,1)S(1)}, bf16[128,1024]{1,0:T(8,128)(2,1)S(1)}, u32[]{:S(2)}, u32[]{:S(2)}) %collective-permute-start.31) | collective-permute-done | bytes 262176 | tf_op jit(solution)/shard_map/ppermute | solution.py:45
  472.3 5.5 %collective-permute-done.51 = bf16[1,8,128,128]{3,2,1,0:T(8,128)(2,1)S(1)} collective-permute-done((bf16[1,8,128,128]{3,2,1,0:T(8,128)(2,1)S(1)}, bf16[1,8,128,128]{3,2,1,0:T(8,128)(2,1)S(1)}, u32[]{:S(2)}, u32[]{:S(2)}) %collective-permute-start.51) | collective-permute-done | bytes 262176 | tf_op jit(solution)/shard_map/ppermute | solution.py:45
  (346 shorter events, 207.1 us)
Async XLA Ops:
  6.2 16.3 %collective-permute-start.1 = (bf16[128,2176]{1,0:T(8,128)(2,1)S(1)}, bf16[128,2176]{1,0:T(8,128)(2,1)}, u32[]{:S(2)}, u32[]{:S(2)}) collective-permute-start(bf16[128,2176]{1,0:T(8,128)(2,1)S(1)} %get-tuple-element.144), channel_id=1, source_target_pairs={{0,4},{8,0},{16,8},{24,16},{28,24},{20,28},{12,20},{4,12},{1,5},{9... | collective-permute-start | bytes 1671176 | tf_op jit(solution)/shard_map/ppermute | solution.py:106
  9.3 14.2 %collective-permute-start = (bf16[128,2176]{1,0:T(8,128)(2,1)S(1)}, bf16[128,2176]{1,0:T(8,128)(2,1)}, u32[]{:S(2)}, u32[]{:S(2)}) collective-permute-start(bf16[128,2176]{1,0:T(8,128)(2,1)S(1)} %get-tuple-element.144), channel_id=1, source_target_pairs={{0,8},{8,16},{16,24},{24,28},{28,20},{20,12},{12,4},{4,0},{1,9},{9... | collective-permute-start | bytes 1671176 | tf_op jit(solution)/shard_map/ppermute | solution.py:105
  12.6 47.5 %collective-permute-start.9 = (bf16[2048,512]{1,0:T(8,128)(2,1)}, bf16[2048,512]{1,0:T(8,128)(2,1)S(1)}, u32[]{:S(2)}, u32[]{:S(2)}) collective-permute-start(bf16[2048,512]{1,0:T(8,128)(2,1)} %constant_dynamic-slice_fusion), channel_id=1, source_target_pairs={{0,1},{3,2},{4,5},{7,6},{8,9},{11,10},{12,13},{15,14},{16,17},{19,... | collective-permute-start | bytes 6291464 | tf_op jit(solution)/shard_map/ppermute | solution.py:1006
  18.1 44.6 %collective-permute-start.8 = (bf16[2048,512]{1,0:T(8,128)(2,1)}, bf16[2048,512]{1,0:T(8,128)(2,1)}, u32[]{:S(2)}, u32[]{:S(2)}) collective-permute-start(bf16[2048,512]{1,0:T(8,128)(2,1)} %constant_dynamic-slice_fusion.1), channel_id=1, source_target_pairs={{0,1},{3,2},{4,5},{7,6},{8,9},{11,10},{12,13},{15,14},{16,17},{19,... | collective-permute-start | bytes 6291464 | tf_op jit(solution)/shard_map/ppermute | solution.py:1006
  23.5 13.4 %collective-permute-start.2 = (bf16[128,2176]{1,0:T(8,128)(2,1)}, bf16[128,2176]{1,0:T(8,128)(2,1)S(1)}, u32[]{:S(2)}, u32[]{:S(2)}) collective-permute-start(bf16[128,2176]{1,0:T(8,128)(2,1)} %collective-permute-done), channel_id=1, source_target_pairs={{0,8},{8,16},{16,24},{24,28},{28,20},{20,12},{12,4},{4,0},{1,9},{9... | collective-permute-start | bytes 1671176 | tf_op jit(solution)/shard_map/ppermute | solution.py:105
  24.1 13.1 %collective-permute-start.3 = (bf16[128,2176]{1,0:T(8,128)(2,1)}, bf16[128,2176]{1,0:T(8,128)(2,1)S(1)}, u32[]{:S(2)}, u32[]{:S(2)}) collective-permute-start(bf16[128,2176]{1,0:T(8,128)(2,1)} %collective-permute-done.1), channel_id=1, source_target_pairs={{0,4},{8,0},{16,8},{24,16},{28,24},{20,28},{12,20},{4,12},{1,5},{9... | collective-permute-start | bytes 1671176 | tf_op jit(solution)/shard_map/ppermute | solution.py:106
  37.3 12.0 %collective-permute-start.4 = (bf16[128,2176]{1,0:T(8,128)(2,1)S(1)}, bf16[128,2176]{1,0:T(8,128)(2,1)S(1)}, u32[]{:S(2)}, u32[]{:S(2)}) collective-permute-start(bf16[128,2176]{1,0:T(8,128)(2,1)S(1)} %collective-permute-done.2), channel_id=1, source_target_pairs={{0,8},{8,16},{16,24},{24,28},{28,20},{20,12},{12,4},{4,0},{1,9},{9... | collective-permute-start | bytes 1671176 | tf_op jit(solution)/shard_map/ppermute | solution.py:105
  38.8 12.7 %collective-permute-start.5 = (bf16[128,2176]{1,0:T(8,128)(2,1)S(1)}, bf16[128,2176]{1,0:T(8,128)(2,1)S(1)}, u32[]{:S(2)}, u32[]{:S(2)}) collective-permute-start(bf16[128,2176]{1,0:T(8,128)(2,1)S(1)} %collective-permute-done.3), channel_id=1, source_target_pairs={{0,4},{8,0},{16,8},{24,16},{28,24},{20,28},{12,20},{4,12},{1,5},{9... | collective-permute-start | bytes 1671176 | tf_op jit(solution)/shard_map/ppermute | solution.py:106
  62.7 28.4 %all-to-all-start = ((bf16[8,40,1024]{2,1,0:T(8,128)(2,1)}), bf16[8,40,1024]{2,1,0:T(8,128)(2,1)S(1)}, u32[]{:S(2)}, u32[]{:S(2)}) async-start(bf16[8,40,1024]{2,1,0:T(8,128)(2,1)} %bitcast.18), calls=%async_computation | async-start | bytes 1310720 | tf_op jit(solution)/shard_map/all_to_all | solution.py:1065
  91.1 17.6 %collective-permute-start.11 = (bf16[320,1024]{1,0:T(8,128)(2,1)S(1)}, bf16[320,1024]{1,0:T(8,128)(2,1)S(1)}, u32[]{:S(2)}, u32[]{:S(2)}) collective-permute-start(bf16[320,1024]{1,0:T(8,128)(2,1)S(1)} %bitcast.198), channel_id=1, source_target_pairs={{0,1},{1,0},{2,3},{3,2},{4,5},{5,4},{6,7},{7,6},{8,9},{9,8},{10,11... | collective-permute-start | bytes 1966088 | tf_op jit(solution)/shard_map/ppermute | solution.py:45
  112.3 16.8 %collective-permute-start.13 = (bf16[320,1024]{1,0:T(8,128)(2,1)S(1)}, bf16[320,1024]{1,0:T(8,128)(2,1)S(1)}, u32[]{:S(2)}, u32[]{:S(2)}) collective-permute-start(bf16[320,1024]{1,0:T(8,128)(2,1)S(1)} %add_convert_fusion.7), channel_id=1, source_target_pairs={{0,1},{1,0},{2,3},{3,2},{4,5},{5,4},{6,7},{7,6},{8,9},{9,8},{10,11... | collective-permute-start | bytes 1966088 | tf_op jit(solution)/shard_map/ppermute | solution.py:45
  132.4 23.7 %all-to-all-start.1 = ((bf16[8,40,1024]{2,1,0:T(8,128)(2,1)}), bf16[8,40,1024]{2,1,0:T(8,128)(2,1)}, u32[]{:S(2)}, u32[]{:S(2)}) async-start(bf16[8,40,1024]{2,1,0:T(8,128)(2,1)} %bitcast.22), calls=%async_computation.1 | async-start | bytes 1310720 | tf_op jit(solution)/shard_map/all_to_all | solution.py:1056
  182.0 17.3 %collective-permute-start.18 = (bf16[320,1024]{1,0:T(8,128)(2,1)S(1)}, bf16[320,1024]{1,0:T(8,128)(2,1)}, u32[]{:S(2)}, u32[]{:S(2)}) collective-permute-start(bf16[320,1024]{1,0:T(8,128)(2,1)S(1)} %bitcast.195), channel_id=1, source_target_pairs={{0,1},{1,0},{2,3},{3,2},{4,5},{5,4},{6,7},{7,6},{8,9},{9,8},{10,11... | collective-permute-start | bytes 1966088 | tf_op jit(solution)/shard_map/ppermute | solution.py:45
  226.6 16.8 %collective-permute-start.22 = (bf16[320,1024]{1,0:T(8,128)(2,1)S(1)}, bf16[320,1024]{1,0:T(8,128)(2,1)S(1)}, u32[]{:S(2)}, u32[]{:S(2)}) collective-permute-start(bf16[320,1024]{1,0:T(8,128)(2,1)S(1)} %add_convert_fusion.5), channel_id=1, source_target_pairs={{0,1},{1,0},{2,3},{3,2},{4,5},{5,4},{6,7},{7,6},{8,9},{9,8},{10,11... | collective-permute-start | bytes 1966088 | tf_op jit(solution)/shard_map/ppermute | solution.py:45
  246.7 21.8 %all-to-all-start.3 = ((bf16[8,40,1024]{2,1,0:T(8,128)(2,1)}), bf16[8,40,1024]{2,1,0:T(8,128)(2,1)S(1)}, u32[]{:S(2)}, u32[]{:S(2)}) async-start(bf16[8,40,1024]{2,1,0:T(8,128)(2,1)} %bitcast.28), calls=%async_computation.3 | async-start | bytes 1310720 | tf_op jit(solution)/shard_map/all_to_all | solution.py:1056
  273.9 22.6 %all-to-all-start.4 = ((bf16[8,40,1024]{2,1,0:T(8,128)(2,1)}), bf16[8,40,1024]{2,1,0:T(8,128)(2,1)S(1)}, u32[]{:S(2)}, u32[]{:S(2)}) async-start(bf16[8,40,1024]{2,1,0:T(8,128)(2,1)} %bitcast.32), calls=%async_computation.4 | async-start | bytes 1310720 | tf_op jit(solution)/shard_map/all_to_all | solution.py:1028
  277.7 17.6 %collective-permute-start.30 = (bf16[320,1024]{1,0:T(8,128)(2,1)}, bf16[320,1024]{1,0:T(8,128)(2,1)S(1)}, u32[]{:S(2)}, u32[]{:S(2)}) collective-permute-start(bf16[320,1024]{1,0:T(8,128)(2,1)} %add_convert_fusion.3), channel_id=1, source_target_pairs={{0,1},{1,0},{2,3},{3,2},{4,5},{5,4},{6,7},{7,6},{8,9},{9,8},{10,11... | collective-permute-start | bytes 1966088 | tf_op jit(solution)/shard_map/ppermute | solution.py:45
  296.5 17.3 %collective-permute-start.27 = (bf16[320,1024]{1,0:T(8,128)(2,1)S(1)}, bf16[320,1024]{1,0:T(8,128)(2,1)S(1)}, u32[]{:S(2)}, u32[]{:S(2)}) collective-permute-start(bf16[320,1024]{1,0:T(8,128)(2,1)S(1)} %bitcast.191), channel_id=1, source_target_pairs={{0,2},{2,0},{1,3},{3,1},{4,6},{6,4},{5,7},{7,5},{8,10},{10,8},{9,1... | collective-permute-start | bytes 1966088 | tf_op jit(solution)/shard_map/ppermute | solution.py:45
  296.5 17.3 %collective-permute-start.26 = (bf16[320,1024]{1,0:T(8,128)(2,1)S(1)}, bf16[320,1024]{1,0:T(8,128)(2,1)}, u32[]{:S(2)}, u32[]{:S(2)}) collective-permute-start(bf16[320,1024]{1,0:T(8,128)(2,1)S(1)} %bitcast.192), channel_id=1, source_target_pairs={{0,1},{1,0},{2,3},{3,2},{4,5},{5,4},{6,7},{7,6},{8,9},{9,8},{10,11... | collective-permute-start | bytes 1966088 | tf_op jit(solution)/shard_map/ppermute | solution.py:45
  296.8 42.8 %all-to-all-start.5 = ((bf16[8,40,1024]{2,1,0:T(8,128)(2,1)}), bf16[8,40,1024]{2,1,0:T(8,128)(2,1)}, u32[]{:S(2)}, u32[]{:S(2)}) async-start(bf16[8,40,1024]{2,1,0:T(8,128)(2,1)} %bitcast.208), calls=%async_computation.5 | async-start | bytes 1310720 | tf_op jit(solution)/shard_map/all_to_all | solution.py:1152
  345.9 10.3 %collective-permute-start.32 = (bf16[1,1024,128]{2,1,0:T(8,128)(2,1)S(1)}, bf16[1,1024,128]{2,1,0:T(8,128)(2,1)S(1)}, u32[]{:S(2)}, u32[]{:S(2)}) collective-permute-start(bf16[1,1024,128]{2,1,0:T(8,128)(2,1)S(1)} %get-tuple-element.297), channel_id=1, source_target_pairs={{0,8},{8,16},{16,24},{24,28},{28,20},{20,12},{12,4},{4,0},{1,9},{9... | collective-permute-start | bytes 786440 | tf_op jit(solution)/shard_map/ppermute | solution.py:149
  356.4 13.1 %collective-permute-start.36 = (bf16[2,1024,128]{2,1,0:T(8,128)(2,1)S(1)}, bf16[2,1024,128]{2,1,0:T(8,128)(2,1)S(1)}, u32[]{:S(2)}, u32[]{:S(2)}) collective-permute-start(bf16[2,1024,128]{2,1,0:T(8,128)(2,1)S(1)} %get-tuple-element.294), channel_id=1, source_target_pairs={{0,4},{8,0},{16,8},{24,16},{28,24},{20,28},{12,20},{4,12},{1,5},{9... | collective-permute-start | bytes 1572872 | tf_op jit(solution)/shard_map/ppermute | solution.py:150
  356.8 13.1 %collective-permute-start.35 = (bf16[2,1024,128]{2,1,0:T(8,128)(2,1)S(1)}, bf16[2,1024,128]{2,1,0:T(8,128)(2,1)S(1)}, u32[]{:S(2)}, u32[]{:S(2)}) collective-permute-start(bf16[2,1024,128]{2,1,0:T(8,128)(2,1)S(1)} %get-tuple-element.295), channel_id=1, source_target_pairs={{0,8},{8,16},{16,24},{24,28},{28,20},{20,12},{12,4},{4,0},{1,9},{9... | collective-permute-start | bytes 1572872 | tf_op jit(solution)/shard_map/ppermute | solution.py:149
  371.1 12.5 %collective-permute-start.38 = (bf16[2,1024,128]{2,1,0:T(8,128)(2,1)}, bf16[2,1024,128]{2,1,0:T(8,128)(2,1)}, u32[]{:S(2)}, u32[]{:S(2)}) collective-permute-start(bf16[2,1024,128]{2,1,0:T(8,128)(2,1)} %get-tuple-element.292), channel_id=1, source_target_pairs={{0,4},{8,0},{16,8},{24,16},{28,24},{20,28},{12,20},{4,12},{1,5},{9... | collective-permute-start | bytes 1572872 | tf_op jit(solution)/shard_map/ppermute | solution.py:150
  372.6 11.9 %collective-permute-start.37 = (bf16[2,1024,128]{2,1,0:T(8,128)(2,1)}, bf16[2,1024,128]{2,1,0:T(8,128)(2,1)}, u32[]{:S(2)}, u32[]{:S(2)}) collective-permute-start(bf16[2,1024,128]{2,1,0:T(8,128)(2,1)} %get-tuple-element.293), channel_id=1, source_target_pairs={{0,8},{8,16},{16,24},{24,28},{28,20},{20,12},{12,4},{4,0},{1,9},{9... | collective-permute-start | bytes 1572872 | tf_op jit(solution)/shard_map/ppermute | solution.py:149
  373.4 19.7 %collective-permute-start.41 = (bf16[320,1024]{1,0:T(8,128)(2,1)}, bf16[320,1024]{1,0:T(8,128)(2,1)S(1)}, u32[]{:S(2)}, u32[]{:S(2)}) collective-permute-start(bf16[320,1024]{1,0:T(8,128)(2,1)} %add_convert_fusion.1), channel_id=1, source_target_pairs={{0,1},{1,0},{2,3},{3,2},{4,5},{5,4},{6,7},{7,6},{8,9},{9,8},{10,11... | collective-permute-start | bytes 1966088 | tf_op jit(solution)/shard_map/ppermute | solution.py:45
  386.3 10.7 %collective-permute-start.40 = (bf16[2,1024,128]{2,1,0:T(8,128)(2,1)S(1)}, bf16[2,1024,128]{2,1,0:T(8,128)(2,1)S(1)}, u32[]{:S(2)}, u32[]{:S(2)}) collective-permute-start(bf16[2,1024,128]{2,1,0:T(8,128)(2,1)S(1)} %get-tuple-element.290), channel_id=1, source_target_pairs={{0,4},{8,0},{16,8},{24,16},{28,24},{20,28},{12,20},{4,12},{1,5},{9... | collective-permute-start | bytes 1572872 | tf_op jit(solution)/shard_map/ppermute | solution.py:150
  387.8 10.6 %collective-permute-start.39 = (bf16[2,1024,128]{2,1,0:T(8,128)(2,1)S(1)}, bf16[2,1024,128]{2,1,0:T(8,128)(2,1)S(1)}, u32[]{:S(2)}, u32[]{:S(2)}) collective-permute-start(bf16[2,1024,128]{2,1,0:T(8,128)(2,1)S(1)} %get-tuple-element.291), channel_id=1, source_target_pairs={{0,8},{8,16},{16,24},{24,28},{28,20},{20,12},{12,4},{4,0},{1,9},{9... | collective-permute-start | bytes 1572872 | tf_op jit(solution)/shard_map/ppermute | solution.py:149
  389.2 19.4 %collective-permute-start.42 = (bf16[320,1024]{1,0:T(8,128)(2,1)S(1)}, bf16[320,1024]{1,0:T(8,128)(2,1)}, u32[]{:S(2)}, u32[]{:S(2)}) collective-permute-start(bf16[320,1024]{1,0:T(8,128)(2,1)S(1)} %copy-done.39), channel_id=1, source_target_pairs={{0,2},{2,0},{1,3},{3,1},{4,6},{6,4},{5,7},{7,5},{8,10},{10,8},{9,1... | collective-permute-start | bytes 1966088 | tf_op jit(solution)/shard_map/ppermute | solution.py:45
  400.6 15.2 %all-to-all-start.6 = ((bf16[8,2,128,128]{3,2,1,0:T(8,128)(2,1)}), bf16[8,2,128,128]{3,2,1,0:T(8,128)(2,1)}, u32[]{:S(2)}, u32[]{:S(2)}) async-start(bf16[8,2,128,128]{3,2,1,0:T(8,128)(2,1)} %bitcast.186), calls=%async_computation.6 | async-start | bytes 1048576 | tf_op jit(solution)/shard_map/all_to_all | solution.py:1176
  415.8 22.8 %all-to-all-start.7 = ((bf16[8,40,1024]{2,1,0:T(8,128)(2,1)}), bf16[8,40,1024]{2,1,0:T(8,128)(2,1)S(1)}, u32[]{:S(2)}, u32[]{:S(2)}) async-start(bf16[8,40,1024]{2,1,0:T(8,128)(2,1)} %bitcast.53), calls=%async_computation.7 | async-start | bytes 1310720 | tf_op jit(solution)/shard_map/all_to_all | solution.py:1229
  441.1 22.2 %all-to-all-start.8 = ((bf16[8,304,128]{2,1,0:T(8,128)(2,1)}), bf16[8,304,128]{2,1,0:T(8,128)(2,1)}, u32[]{:S(2)}, u32[]{:S(2)}) async-start(bf16[8,304,128]{2,1,0:T(8,128)(2,1)} %pad_maximum_fusion), calls=%async_computation.8 | async-start | bytes 1245184 | tf_op jit(solution)/shard_map/all_to_all | solution.py:1176
  (101 other events, 723.1 us)
